TPU v7x, 32 devices: a whole 2x2x4 slice. The times are simulated.
32 devices in a mesh: dp: 8 (over z, x), seq: 4 (over y, core).
Axes of the slice: x: 2, y: 2, z: 4, core: 2. Of those that a mesh axis runs over, the one named last changes fastest.
Arguments:
- tokens: bfloat16 [16, 1024, 1024], P('dp', 'seq'), may hold values from -6 to 6
- segments: int32 [16, 1024], P('dp', 'seq'), may hold values from 0 to 4, as said below
- norm_in_gain: bfloat16 [1024], P(('dp', 'seq')), may hold values from 0.5 to 1.5
- gate_in_weight: bfloat16 [1024, 1536], P(('dp', 'seq')), may hold values from -0.1875 to 0.1875
- signal_in_weight: bfloat16 [1024, 1536], P(('dp', 'seq')), may hold values from -0.1875 to 0.1875
- conv_weight: bfloat16 [4, 1536], P(None, ('dp', 'seq')), may hold values from -3 to 3
- rec_gate_weight: bfloat16 [1536, 128], P(('dp', 'seq')), may hold values from -0.5 to 0.5
- input_gate_weight: bfloat16 [1536, 128], P(('dp', 'seq')), may hold values from -0.5 to 0.5
- decay_param: bfloat16 [1536], P(('dp', 'seq')), may hold values from 4 to 16
- branch_out_weight: bfloat16 [1536, 1024], P(('dp', 'seq')), may hold values from -0.4375 to 0.4375
- norm_mid_gain: bfloat16 [1024], P(('dp', 'seq')), may hold values from 0.5 to 1.5
- mlp_gate_weight: bfloat16 [1024, 3072], P(('dp', 'seq')), may hold values from -0.1875 to 0.1875
- mlp_up_weight: bfloat16 [1024, 3072], P(('dp', 'seq')), may hold values from -0.1875 to 0.1875
- mlp_down_weight: bfloat16 [3072, 1024], P(('dp', 'seq')), may hold values from -0.21875 to 0.21875
- cotangent: bfloat16 [16, 1024, 1024], P('dp', 'seq'), may hold values from -6 to 6
Outputs:
- block_out: float32 [16, 1024, 1024], P('dp', 'seq')
- tokens_grad: float32 [16, 1024, 1024], P('dp', 'seq')
- norm_in_grad: float32 [1024], P(('dp', 'seq'))
- gate_in_grad: float32 [1024, 1536], P(('dp', 'seq'))
- signal_in_grad: float32 [1024, 1536], P(('dp', 'seq'))
- conv_weight_grad: float32 [4, 1536], P(None, ('dp', 'seq'))
- rec_gate_grad: float32 [1536, 128], P(('dp', 'seq'))
- input_gate_grad: float32 [1536, 128], P(('dp', 'seq'))
- decay_param_grad: float32 [1536], P(('dp', 'seq'))
- branch_out_grad: float32 [1536, 1024], P(('dp', 'seq'))
- norm_mid_grad: float32 [1024], P(('dp', 'seq'))
- mlp_gate_grad: float32 [1024, 3072], P(('dp', 'seq'))
- mlp_up_grad: float32 [1024, 3072], P(('dp', 'seq'))
- mlp_down_grad: float32 [3072, 1024], P(('dp', 'seq'))
Inputs may be any that keep to these rules, and one draw needn't show every extreme that they name: `segments`: within each row the ids start at 0, never fall and rise by one at each new document; every row holds five documents, the third of which begins within the row's first 256 tokens and ends within its last 256 tokens.
All inputs are finite; a program needn't handle non-finite values.
Results may differ from a plain program's by a relative error of at most 0.01.
Values may be sent and summed in bfloat16 or wider, within the bound.
No kernel may reach another device: no remote copies, remote signals or barrier semaphores. Data moves between devices by JAX's collectives and lax.ppermute only.
A program may use at most 320 MiB of HBM per device.

v0:
```python
import jax
import jax.numpy as jnp
from jax import lax
from jax.sharding import PartitionSpec as P

epsilon = 1e-06
rate_scale = 8.0


def passed_along(block, axis, distance):
    devices = range(lax.axis_size(axis))
    route = [(i - distance, i) for i in devices if i - distance in devices]
    return lax.ppermute(block, axis, route)


def carried_in(part, axis, combine, identity, reverse):
    count = lax.axis_size(axis)
    place = lax.axis_index(axis)
    ahead = count - 1 - place if reverse else place
    gathered = jax.tree.map(lambda a: lax.all_gather(a, axis), part)
    state = jax.tree.map(lambda a, e: jnp.zeros_like(a) + jnp.asarray(e, a.dtype), part, identity)

    def one(turn, state):
        source = count - 1 - turn if reverse else turn
        return combine(
            state, jax.tree.map(lambda a: lax.dynamic_index_in_dim(a, source, 0, False), gathered)
        )

    return lax.fori_loop(0, ahead, one, state)


def rms_scale(values, norm_gain):
    return (
        values * lax.rsqrt(jnp.mean(values * values, axis=-1, keepdims=True) + epsilon) * norm_gain
    )


def combine_pairs(earlier, later):
    return (earlier[0] * later[0], later[0] * earlier[1] + later[1])


def block_apply(values, weight_blocks):
    return jnp.einsum("nhi,hij->nhj", values, weight_blocks, preferred_element_type=jnp.float32)


def block_back(grads, weight_blocks):
    return jnp.einsum("nhj,hij->nhi", grads, weight_blocks, preferred_element_type=jnp.float32)


def body(
    tokens,
    segments,
    norm_in_gain,
    gate_in_weight,
    signal_in_weight,
    conv_weight,
    rec_gate_weight,
    input_gate_weight,
    decay_param,
    branch_out_weight,
    norm_mid_gain,
    mlp_gate_weight,
    mlp_up_weight,
    mlp_down_weight,
    cotangent,
):
    gathered = (
        lax.all_gather(norm_in_gain, ("dp", "seq"), axis=0, tiled=True),
        lax.all_gather(gate_in_weight, ("dp", "seq"), axis=0, tiled=True),
        lax.all_gather(signal_in_weight, ("dp", "seq"), axis=0, tiled=True),
        lax.all_gather(conv_weight, ("dp", "seq"), axis=1, tiled=True),
        lax.all_gather(rec_gate_weight, ("dp", "seq"), axis=0, tiled=True),
        lax.all_gather(input_gate_weight, ("dp", "seq"), axis=0, tiled=True),
        lax.all_gather(decay_param, ("dp", "seq"), axis=0, tiled=True),
        lax.all_gather(branch_out_weight, ("dp", "seq"), axis=0, tiled=True),
        lax.all_gather(norm_mid_gain, ("dp", "seq"), axis=0, tiled=True),
        lax.all_gather(mlp_gate_weight, ("dp", "seq"), axis=0, tiled=True),
        lax.all_gather(mlp_up_weight, ("dp", "seq"), axis=0, tiled=True),
        lax.all_gather(mlp_down_weight, ("dp", "seq"), axis=0, tiled=True),
    )
    (
        gain_in_low,
        full_gate_in,
        full_signal,
        conv_low_weights,
        full_rec,
        full_input,
        decay_low,
        full_branch,
        gain_mid_low,
        full_mlp_gate,
        full_mlp_up,
        full_mlp_down,
    ) = gathered
    gain_in = gain_in_low.astype(jnp.float32)
    conv_taps = conv_low_weights.astype(jnp.float32)
    decay_full = decay_low.astype(jnp.float32)
    gain_mid = gain_mid_low.astype(jnp.float32)
    row_count, row_tokens, model_width = tokens.shape
    lru_width = full_signal.shape[1]
    block_width = full_rec.shape[1]
    block_count = lru_width // block_width
    halo_rows = conv_taps.shape[0] - 1
    token_count = row_count * row_tokens
    rec_blocks = full_rec.reshape(block_count, block_width, block_width)
    input_blocks = full_input.reshape(block_count, block_width, block_width)
    inputs_flat = tokens.astype(jnp.float32).reshape(token_count, model_width)
    normed_value, norm_in_pull = jax.vjp(rms_scale, inputs_flat, gain_in)
    normed_in = normed_value.astype(jnp.bfloat16)
    gate_pre = jnp.dot(normed_in, full_gate_in, preferred_element_type=jnp.float32)
    signal = (
        jnp.dot(normed_in, full_signal, preferred_element_type=jnp.float32)
        .astype(jnp.bfloat16)
        .reshape(row_count, row_tokens, lru_width)
    )
    tail_signal, tail_ids = passed_along(
        (signal[:, row_tokens - halo_rows :], segments[:, row_tokens - halo_rows :]), "seq", 1
    )
    first_device = lax.axis_index("seq") == 0
    tail_ids = jnp.where(first_device, jnp.int32(-1), tail_ids)
    signal_ext = jnp.concatenate([tail_signal, signal], axis=1)
    ids_ext = jnp.concatenate([tail_ids, segments], axis=1)
    same_masks = []
    earlier_signals = []
    conv_out = jnp.zeros((row_count, row_tokens, lru_width), jnp.float32)
    for offset in range(halo_rows + 1):
        earlier_ids = lax.slice_in_dim(
            ids_ext, halo_rows - offset, halo_rows - offset + row_tokens, axis=1
        )
        same_masks.append((earlier_ids == segments).astype(jnp.float32)[:, :, None])
        earlier_signals.append(
            lax.slice_in_dim(
                signal_ext, halo_rows - offset, halo_rows - offset + row_tokens, axis=1
            )
        )
        conv_out = conv_out + conv_taps[offset] * earlier_signals[offset] * same_masks[offset]
    reset_mask = same_masks[1] == 0.0
    conv_low = conv_out.astype(jnp.bfloat16)
    conv_blocks = conv_low.reshape(token_count, block_count, block_width)
    rec_logit = block_apply(conv_blocks, rec_blocks).reshape(row_count, row_tokens, lru_width)
    input_logit = block_apply(conv_blocks, input_blocks).reshape(row_count, row_tokens, lru_width)

    def gate_terms(rec_value, input_value, conv_value, decay_value):
        rec_share = jax.nn.sigmoid(rec_value)
        input_share = jax.nn.sigmoid(input_value)
        log_keep = -rate_scale * jax.nn.softplus(-decay_value) * (0.1 + 0.9 * rec_share)
        keep_value = jnp.where(reset_mask, 0.0, jnp.exp(log_keep))
        inject_scale = jnp.where(reset_mask, 1.0, jnp.sqrt(-jnp.expm1(2.0 * log_keep)))
        return (keep_value, inject_scale * conv_value * input_share)

    (keep_factor, inject), gate_pull = jax.vjp(
        gate_terms, rec_logit, input_logit, conv_low.astype(jnp.float32), decay_full
    )
    cum_keep, local_state = lax.associative_scan(combine_pairs, (keep_factor, inject), axis=1)
    end_keep = cum_keep[:, -1]
    end_state = local_state[:, -1]
    state_in = carried_in(
        (end_keep, end_state),
        "seq",
        combine_pairs,
        (jnp.ones_like(end_keep), jnp.zeros_like(end_state)),
        False,
    )[1]
    states = local_state + cum_keep * state_in[:, None, :]
    gate_act, gelu_pull = jax.vjp(jax.nn.gelu, gate_pre)
    states_flat = states.reshape(token_count, lru_width)
    mixed = (gate_act * states_flat).astype(jnp.bfloat16)
    middle = inputs_flat + jnp.dot(mixed, full_branch, preferred_element_type=jnp.float32)
    normed_mid_value, norm_mid_pull = jax.vjp(rms_scale, middle, gain_mid)
    normed_mid = normed_mid_value.astype(jnp.bfloat16)
    mlp_gate_pre = jnp.dot(normed_mid, full_mlp_gate, preferred_element_type=jnp.float32)
    mlp_up_pre = jnp.dot(normed_mid, full_mlp_up, preferred_element_type=jnp.float32)
    mlp_act, mlp_gelu_pull = jax.vjp(jax.nn.gelu, mlp_gate_pre)
    hidden = (mlp_act * mlp_up_pre).astype(jnp.bfloat16)
    block_out = middle + jnp.dot(hidden, full_mlp_down, preferred_element_type=jnp.float32)
    out_grad = cotangent.reshape(token_count, model_width)
    down_full = jnp.einsum("nf,nd->fd", hidden, out_grad, preferred_element_type=jnp.float32)
    hidden_grad = jnp.einsum(
        "nd,fd->nf", out_grad, full_mlp_down, preferred_element_type=jnp.float32
    )
    gate_grad_low = mlp_gelu_pull(hidden_grad * mlp_up_pre)[0].astype(jnp.bfloat16)
    up_grad_low = (hidden_grad * mlp_act).astype(jnp.bfloat16)
    mlp_gate_full = jnp.einsum(
        "nd,nf->df", normed_mid, gate_grad_low, preferred_element_type=jnp.float32
    )
    mlp_up_full = jnp.einsum(
        "nd,nf->df", normed_mid, up_grad_low, preferred_element_type=jnp.float32
    )
    normed_mid_grad = jnp.einsum(
        "nf,df->nd", gate_grad_low, full_mlp_gate, preferred_element_type=jnp.float32
    ) + jnp.einsum("nf,df->nd", up_grad_low, full_mlp_up, preferred_element_type=jnp.float32)
    middle_norm_grad, gain_mid_grad = norm_mid_pull(normed_mid_grad)
    middle_grad = out_grad.astype(jnp.float32) + middle_norm_grad
    middle_low = middle_grad.astype(jnp.bfloat16)
    branch_full = jnp.einsum("nl,nd->ld", mixed, middle_low, preferred_element_type=jnp.float32)
    mixed_grad = jnp.einsum(
        "nd,ld->nl", middle_low, full_branch, preferred_element_type=jnp.float32
    )
    gate_pre_low = gelu_pull(mixed_grad * states_flat)[0].astype(jnp.bfloat16)
    state_seed = (mixed_grad * gate_act).reshape(row_count, row_tokens, lru_width)
    next_keep = jnp.concatenate([keep_factor[:, 1:], jnp.ones_like(keep_factor[:, :1])], axis=1)
    rev_keep, rev_grad = lax.associative_scan(
        combine_pairs, (next_keep[:, ::-1], state_seed[:, ::-1]), axis=1
    )
    tail_keep = rev_keep[:, ::-1]
    local_grad = rev_grad[:, ::-1]
    head_factor = keep_factor[:, 0] * tail_keep[:, 0]
    head_grad = keep_factor[:, 0] * local_grad[:, 0]
    grad_in = carried_in(
        (head_factor, head_grad),
        "seq",
        combine_pairs,
        (jnp.ones_like(head_factor), jnp.zeros_like(head_grad)),
        True,
    )[1]
    state_grad = local_grad + tail_keep * grad_in[:, None, :]
    prev_states = jnp.concatenate([state_in[:, None, :], states[:, :-1]], axis=1)
    rec_logit_grad, input_logit_grad, conv_direct, decay_grad = gate_pull(
        (state_grad * prev_states, state_grad)
    )
    rec_low = rec_logit_grad.astype(jnp.bfloat16).reshape(token_count, block_count, block_width)
    input_low = input_logit_grad.astype(jnp.bfloat16).reshape(token_count, block_count, block_width)
    rec_full = jnp.einsum(
        "nhi,nhj->hij", conv_blocks, rec_low, preferred_element_type=jnp.float32
    ).reshape(lru_width, block_width)
    input_full = jnp.einsum(
        "nhi,nhj->hij", conv_blocks, input_low, preferred_element_type=jnp.float32
    ).reshape(lru_width, block_width)
    conv_grad = conv_direct + (
        block_back(rec_low, rec_blocks) + block_back(input_low, input_blocks)
    ).reshape(row_count, row_tokens, lru_width)
    ext_grad = jnp.zeros((row_count, row_tokens + halo_rows, lru_width), jnp.float32)
    tap_grads = []
    for offset in range(halo_rows + 1):
        masked_grad = conv_grad * same_masks[offset]
        tap_grads.append(jnp.sum(masked_grad * earlier_signals[offset], axis=(0, 1)))
        ext_grad = ext_grad + jnp.pad(
            masked_grad * conv_taps[offset], ((0, 0), (halo_rows - offset, offset), (0, 0))
        )
    conv_full = jnp.stack(tap_grads, axis=0)
    from_right = passed_along(ext_grad[:, :halo_rows].astype(jnp.bfloat16), "seq", -1).astype(
        jnp.float32
    )
    signal_grad = ext_grad[:, halo_rows:] + jnp.pad(
        from_right, ((0, 0), (row_tokens - halo_rows, 0), (0, 0))
    )
    signal_low = signal_grad.astype(jnp.bfloat16).reshape(token_count, lru_width)
    gate_in_full = jnp.einsum(
        "nd,nl->dl", normed_in, gate_pre_low, preferred_element_type=jnp.float32
    )
    signal_full = jnp.einsum("nd,nl->dl", normed_in, signal_low, preferred_element_type=jnp.float32)
    normed_in_grad = jnp.einsum(
        "nl,dl->nd", gate_pre_low, full_gate_in, preferred_element_type=jnp.float32
    ) + jnp.einsum("nl,dl->nd", signal_low, full_signal, preferred_element_type=jnp.float32)
    input_norm_grad, gain_in_grad = norm_in_pull(normed_in_grad)
    tokens_grad = (middle_grad + input_norm_grad).reshape(row_count, row_tokens, model_width)
    shards = (
        lax.psum_scatter(gain_in_grad, ("dp", "seq"), scatter_dimension=0, tiled=True),
        lax.psum_scatter(gate_in_full, ("dp", "seq"), scatter_dimension=0, tiled=True),
        lax.psum_scatter(signal_full, ("dp", "seq"), scatter_dimension=0, tiled=True),
        lax.psum_scatter(conv_full, ("dp", "seq"), scatter_dimension=1, tiled=True),
        lax.psum_scatter(rec_full, ("dp", "seq"), scatter_dimension=0, tiled=True),
        lax.psum_scatter(input_full, ("dp", "seq"), scatter_dimension=0, tiled=True),
        lax.psum_scatter(decay_grad, ("dp", "seq"), scatter_dimension=0, tiled=True),
        lax.psum_scatter(branch_full, ("dp", "seq"), scatter_dimension=0, tiled=True),
        lax.psum_scatter(gain_mid_grad, ("dp", "seq"), scatter_dimension=0, tiled=True),
        lax.psum_scatter(mlp_gate_full, ("dp", "seq"), scatter_dimension=0, tiled=True),
        lax.psum_scatter(mlp_up_full, ("dp", "seq"), scatter_dimension=0, tiled=True),
        lax.psum_scatter(down_full, ("dp", "seq"), scatter_dimension=0, tiled=True),
    )
    return (
        block_out.reshape(row_count, row_tokens, model_width),
        tokens_grad,
        shards[0],
        shards[1],
        shards[2],
        shards[3],
        shards[4],
        shards[5],
        shards[6],
        shards[7],
        shards[8],
        shards[9],
        shards[10],
        shards[11],
    )


def solution(mesh):
    placed = (
        P("dp", "seq", None),
        P("dp", "seq"),
        P(("dp", "seq")),
        P(("dp", "seq"), None),
        P(("dp", "seq"), None),
        P(None, ("dp", "seq")),
        P(("dp", "seq"), None),
        P(("dp", "seq"), None),
        P(("dp", "seq")),
        P(("dp", "seq"), None),
        P(("dp", "seq")),
        P(("dp", "seq"), None),
        P(("dp", "seq"), None),
        P(("dp", "seq"), None),
        P("dp", "seq", None),
    )
    return jax.shard_map(
        body,
        mesh=mesh,
        in_specs=placed,
        out_specs=(
            P("dp", "seq", None),
            P("dp", "seq", None),
            P(("dp", "seq")),
            P(("dp", "seq"), None),
            P(("dp", "seq"), None),
            P(None, ("dp", "seq")),
            P(("dp", "seq"), None),
            P(("dp", "seq"), None),
            P(("dp", "seq")),
            P(("dp", "seq"), None),
            P(("dp", "seq")),
            P(("dp", "seq"), None),
            P(("dp", "seq"), None),
            P(("dp", "seq"), None),
        ),
        check_vma=False,
    )
```

profile of v0, /device:TPU:0, one launch (start us, length us, event | category | flops | bytes accessed | tf_op | source)
XLA Modules:
  0.0 2183.0 jit_solution(17430137556312776790)
XLA Ops:
  16.3 42.2 %all-reduce.78 = (bf16[1024]{0:T(1024)(128)(2,1)S(1)}, bf16[1536]{0:T(1024)(128)(2,1)S(1)}, bf16[1024]{0:T(1024)(128)(2,1)S(1)}) all-reduce(bf16[1024]{0:T(1024)(128)(2,1)S(1)} %dynamic-update-slice, bf16[1536]{0:T(1024)(128)(2,1)S(1)} %dynamic-update-slice.1, ...), channel_id=1, replica_groups=mesh['dp'=8,'seq'=4] {'dp','seq'}, use_global_device_ids=true, to_apply=%add.71 | all-reduce | flops 3584 | bytes 14336
  61.2 40.3 %all-gather.4 = bf16[32,48,4]{1,2,0:T(4,128)(2,1)S(1)} all-gather(bf16[1,48,4]{1,2,0:T(4,128)(2,1)} %bitcast.184), channel_id=1, replica_groups=mesh['dp'=8,'seq'=4] {'dp','seq'}, dimensions={0}, use_global_device_ids=true | all-gather | bytes 12672 | tf_op jit(solution)/shard_map/all_gather | solution.py:71
  102.3 41.0 %all_gather.55 = bf16[1536,128]{1,0:T(8,128)(2,1)} all-gather(bf16[48,128]{1,0:T(8,128)(2,1)} %param.25), channel_id=1, replica_groups=mesh['dp'=8,'seq'=4] {'dp','seq'}, dimensions={0}, use_global_device_ids=true | all-gather | bytes 405504 | tf_op jit(solution)/shard_map/all_gather | solution.py:72
  143.3 39.6 %all_gather.56 = bf16[1536,128]{1,0:T(8,128)(2,1)S(1)} all-gather(bf16[48,128]{1,0:T(8,128)(2,1)} %param.26), channel_id=1, replica_groups=mesh['dp'=8,'seq'=4] {'dp','seq'}, dimensions={0}, use_global_device_ids=true | all-gather | bytes 405504 | tf_op jit(solution)/shard_map/all_gather | solution.py:73
  224.0 8.0 fusion.61
  232.0 7.7 slice.561
  244.0 7.6 slice.562
  251.6 7.8 slice.563
  371.9 7.7 slice.617
  383.9 7.7 slice.639
  391.6 7.6 slice.646
  399.2 7.6 slice.637
  512.9 6.3 pad.251
  525.8 12.8 slice.640
  538.6 12.8 slice.647
  551.4 12.8 slice.638
  565.3 7.8 multiply_add_fusion.2
  573.1 7.6 fusion.38
  587.8 9.1 fusion.104
  596.9 9.2 fusion.105
  606.1 14.1 multiply_convert_fusion
  620.2 8.2 fusion.106
  642.2 7.6 slice.641
  649.8 7.6 slice.643
  657.3 12.8 slice.642
  670.1 12.8 slice.644
  785.6 7.7 slice.699
  794.1 13.0 slice.700
  890.9 6.2 pad.284
  906.0 6.2 pad.267
  912.2 6.3 pad.283
  938.0 16.1 rev.9
  954.2 25.0 %rev.8 = f32[2,256,1536]{2,1,0:T(8,128)} reverse(f32[2,256,1536]{2,1,0:T(8,128)} %add.580), dimensions={1} | reverse | bytes 6291456 | tf_op jit(solution)/shard_map/rev | solution.py:206
  979.2 8.4 multiply_reduce_fusion
  1025.2 11.2 fusion.13
  1072.7 10.3 fusion.112
  1083.0 10.3 fusion.113
  1093.6 10.2 fusion.114
  1108.9 7.7 convolution_add_fusion.2
  1120.0 37.3 %all-reduce.77 = (f32[1024]{0:T(1024)S(1)}, f32[1536]{0:T(1024)S(1)}, f32[1024]{0:T(1024)S(1)}) all-reduce(f32[1024]{0:T(1024)S(1)} %get-tuple-element.160, f32[1536]{0:T(1024)S(1)} %fusion.85, f32[1024]{0:T(1024)S(1)} %copy-done.104), channel_id=6, replica_groups=mesh['dp'=8,'seq'=4] {'dp','seq'}, use_global_device_ids=true, to_apply=%region_9.10.clone | all-reduce | flops 3584 | bytes 28672
  1164.0 67.2 %reduce-scatter.16.cloned.1.call-done = f32[48,128]{1,0:T(8,128)} async-done(((f32[1536,128]{1,0:T(8,128)}), f32[48,128]{1,0:T(8,128)}) %reduce-scatter.16.cloned.1.call-update) | async-done | bytes 24592 | tf_op jit(solution)/shard_map/reduce_scatter | solution.py:262
  1231.1 100.3 %reduce-scatter.18.cloned.1.call-done = f32[48,128]{1,0:T(8,128)} async-done(((f32[1536,128]{1,0:T(8,128)}), f32[48,128]{1,0:T(8,128)}) %reduce-scatter.18.cloned.1.call-update) | async-done | bytes 24592 | tf_op jit(solution)/shard_map/reduce_scatter | solution.py:263
  1331.4 119.5 %reduce-scatter.20.cloned.1.call-done = f32[48,1024]{1,0:T(8,128)} async-done(((f32[1536,1024]{1,0:T(8,128)}), f32[48,1024]{1,0:T(8,128)}) %reduce-scatter.20.cloned.1.call-update) | async-done | bytes 196624 | tf_op jit(solution)/shard_map/reduce_scatter | solution.py:265
  1450.9 120.7 %reduce-scatter.12.cloned.1.call-done = f32[32,1536]{1,0:T(8,128)} async-done(((f32[1024,1536]{1,0:T(8,128)}), f32[32,1536]{1,0:T(8,128)}) %reduce-scatter.12.cloned.1.call-update) | async-done | bytes 196624 | tf_op jit(solution)/shard_map/reduce_scatter | solution.py:259
  1571.6 119.6 %reduce-scatter.14.cloned.1.call-done = f32[32,1536]{1,0:T(8,128)} async-done(((f32[1024,1536]{1,0:T(8,128)}), f32[32,1536]{1,0:T(8,128)}) %reduce-scatter.14.cloned.1.call-update) | async-done | bytes 196624 | tf_op jit(solution)/shard_map/reduce_scatter | solution.py:260
  1691.2 162.2 %reduce-scatter.22.cloned.1.call-done = f32[32,3072]{1,0:T(8,128)} async-done(((f32[1024,3072]{1,0:T(8,128)}), f32[32,3072]{1,0:T(8,128)}) %reduce-scatter.22.cloned.1.call-update) | async-done | bytes 393232 | tf_op jit(solution)/shard_map/reduce_scatter | solution.py:267
  1853.4 160.9 %reduce-scatter.24.cloned.1.call-done = f32[32,3072]{1,0:T(8,128)} async-done(((f32[1024,3072]{1,0:T(8,128)}), f32[32,3072]{1,0:T(8,128)}) %reduce-scatter.24.cloned.1.call-update) | async-done | bytes 393232 | tf_op jit(solution)/shard_map/reduce_scatter | solution.py:268
  2014.3 162.0 %reduce-scatter.26.cloned.1.call-done = f32[96,1024]{1,0:T(8,128)} async-done(((f32[3072,1024]{1,0:T(8,128)}), f32[96,1024]{1,0:T(8,128)}) %reduce-scatter.26.cloned.1.call-update) | async-done | bytes 393232 | tf_op jit(solution)/shard_map/reduce_scatter | solution.py:269
  (600 shorter events, 612.9 us)
Async XLA Ops:
  7.2 176.5 %copy-start.20 = (bf16[2,256,1024]{2,1,0:T(8,128)(2,1)S(1)}, bf16[2,256,1024]{2,1,0:T(8,128)(2,1)}, u32[]{:S(2)}) copy-start(bf16[2,256,1024]{2,1,0:T(8,128)(2,1)} %param.19) | copy-start | bytes 3145732
  7.2 177.8 %all-gather.14.cloned.1.call-start = ((), (), s32[]{:S(2)}) async-start(), calls=%async_computation.10 | async-start | bytes 3244032 | tf_op jit(solution)/shard_map/all_gather | solution.py:70
  7.9 565.2 %all-gather.12.cloned.1.call-start = ((), (), s32[]{:S(2)}) async-start(), calls=%async_computation.9 | async-start | bytes 3244032 | tf_op jit(solution)/shard_map/all_gather | solution.py:69
  8.7 572.0 %all-gather.16.cloned.1.call-start = ((), (), s32[]{:S(2)}) async-start(), calls=%async_computation.11 | async-start | bytes 3244032 | tf_op jit(solution)/shard_map/all_gather | solution.py:75
  9.4 578.4 %all-gather.18.cloned.1.call-start = ((), (), s32[]{:S(2)}) async-start(), calls=%async_computation.12 | async-start | bytes 6488064 | tf_op jit(solution)/shard_map/all_gather | solution.py:77
  10.0 586.9 %all-gather.20.cloned.1.call-start = ((), (), s32[]{:S(2)}) async-start(), calls=%async_computation.13 | async-start | bytes 6488064 | tf_op jit(solution)/shard_map/all_gather | solution.py:78
  10.6 595.5 %all-gather.22.cloned.1.call-start = ((), (), s32[]{:S(2)}) async-start(), calls=%async_computation.14 | async-start | bytes 6488064 | tf_op jit(solution)/shard_map/all_gather | solution.py:79
  11.4 173.6 %collective-permute-start = (s32[2,3]{1,0:T(2,128)S(1)}, s32[2,3]{1,0:T(2,128)S(1)}, u32[]{:S(2)}, u32[]{:S(2)}) collective-permute-start(s32[2,3]{1,0:T(2,128)S(1)} %slice.547), channel_id=1, source_target_pairs={{0,1},{1,2},{2,3},{4,5},{5,6},{6,7},{8,9},{9,10},{10,11},{12,13},{... | collective-permute-start | bytes 80 | tf_op jit(solution)/shard_map/ppermute | solution.py:13
  13.7 1148.8 %reduce-scatter.28.cloned.1.call-start = ((), (), s32[]{:S(2)}) async-start(), calls=%async_computation.23 | async-start | bytes 811008
  58.5 130.6 %copy-start.101 = (bf16[1536]{0:T(1024)(128)(2,1)}, bf16[1536]{0:T(1024)(128)(2,1)S(1)}, u32[]{:S(2)}) copy-start(bf16[1536]{0:T(1024)(128)(2,1)S(1)} %get-tuple-element.190) | copy-start | bytes 9220
  58.5 130.6 %copy-start.85 = (f32[1024]{0:T(1024)}, f32[1024]{0:T(1024)S(1)}, u32[]{:S(2)}) copy-start(f32[1024]{0:T(1024)S(1)} %convert_element_type.101) | copy-start | bytes 12292
  60.6 128.5 %copy-start.97 = (f32[512]{0:T(512)}, f32[512]{0:T(512)S(1)}, u32[]{:S(2)}) copy-start(f32[512]{0:T(512)S(1)} %rsqrt.23) | copy-start | bytes 6148
  102.3 90.0 %copy-start.60 = (f32[1536]{0:T(1024)}, f32[1536]{0:T(1024)S(1)}, u32[]{:S(2)}) copy-start(f32[1536]{0:T(1024)S(1)} %get-tuple-element.162) | copy-start | bytes 18436
  183.0 28.8 %copy-start.38 = (bf16[1536,128]{1,0:T(8,128)(2,1)}, bf16[1536,128]{1,0:T(8,128)(2,1)S(1)}, u32[]{:S(2)}) copy-start(bf16[1536,128]{1,0:T(8,128)(2,1)S(1)} %all_gather.56) | copy-start | bytes 1179652
  183.0 41.0 %copy-start.50 = (f32[1536]{0:T(1024)}, f32[1536]{0:T(1024)S(1)}, u32[]{:S(2)}) copy-start(f32[1536]{0:T(1024)S(1)} %fusion.86) | copy-start | bytes 18436
  189.2 3.1 collective-permute-start.1
  349.7 15.8 copy-start.59
  349.7 15.8 copy-start.58
  349.7 15.9 copy-start.74
  349.7 15.9 copy-start.75
  349.7 15.9 copy-start.76
  349.7 15.9 copy-start.77
  349.7 16.7 copy-start.54
  349.7 16.7 copy-start.55
  391.5 15.2 copy-start.47
  391.5 15.2 copy-start.78
  785.5 21.6 copy-start.81
  785.5 21.6 copy-start.82
  785.5 21.7 copy-start.56
  785.5 21.8 copy-start.57
  785.5 21.8 copy-start.79
  785.5 21.8 copy-start.80
  785.5 22.6 %copy-start.52 = (f32[2,3,1536]{2,1,0:T(4,128)S(1)}, f32[2,3,1536]{2,1,0:T(4,128)}, u32[]{:S(2)}) copy-start(f32[2,3,1536]{2,1,0:T(4,128)} %slice.672) | copy-start | bytes 110596
  785.6 22.6 %copy-start.53 = (f32[2,3,1536]{2,1,0:T(4,128)S(1)}, f32[2,3,1536]{2,1,0:T(4,128)}, u32[]{:S(2)}) copy-start(f32[2,3,1536]{2,1,0:T(4,128)} %slice.689) | copy-start | bytes 110596
  954.2 25.0 %copy-start.1 = (f32[2,256,1536]{2,1,0:T(8,128)S(1)}, f32[2,256,1536]{2,1,0:T(8,128)}, u32[]{:S(2)}) copy-start(f32[2,256,1536]{2,1,0:T(8,128)} %copy-done) | copy-start | bytes 9437188
  954.2 25.0 %copy-start.51 = (f32[1536]{0:T(1024)S(1)}, f32[1536]{0:T(1024)}, u32[]{:S(2)}) copy-start(f32[1536]{0:T(1024)} %copy-done.50) | copy-start | bytes 18436
  954.2 25.0 %copy-start.68 = (f32[2,1,1536]{2,1,0:T(1,128)S(1)}, f32[2,1,1536]{2,1,0:T(1,128)}, u32[]{:S(2)}) copy-start(f32[2,1,1536]{2,1,0:T(1,128)} %copy.333) | copy-start | bytes 36868
  954.2 25.0 %copy-start.95 = (pred[2,256]{1,0:T(4,128)(4,1)S(1)}, pred[2,256]{1,0:T(4,128)(4,1)}, u32[]{:S(2)}) copy-start(pred[2,256]{1,0:T(4,128)(4,1)} %get-tuple-element.196) | copy-start | bytes 1540
  1037.8 193.3 %reduce-scatter.16.cloned.1.call-start = ((), (), s32[]{:S(2)}) async-start(), calls=%async_computation.17 | async-start | bytes 811008 | tf_op jit(solution)/shard_map/reduce_scatter | solution.py:262
  1041.2 290.2 %reduce-scatter.18.cloned.1.call-start = ((), (), s32[]{:S(2)}) async-start(), calls=%async_computation.18 | async-start | bytes 811008 | tf_op jit(solution)/shard_map/reduce_scatter | solution.py:263
  1044.8 406.1 %reduce-scatter.20.cloned.1.call-start = ((), (), s32[]{:S(2)}) async-start(), calls=%async_computation.19 | async-start | bytes 6488064 | tf_op jit(solution)/shard_map/reduce_scatter | solution.py:265
  1050.7 520.8 %reduce-scatter.12.cloned.1.call-start = ((), (), s32[]{:S(2)}) async-start(), calls=%async_computation.15 | async-start | bytes 6488064 | tf_op jit(solution)/shard_map/reduce_scatter | solution.py:259
  1057.8 633.3 %reduce-scatter.14.cloned.1.call-start = ((), (), s32[]{:S(2)}) async-start(), calls=%async_computation.16 | async-start | bytes 6488064 | tf_op jit(solution)/shard_map/reduce_scatter | solution.py:260
  1063.1 3.2 collective-permute-start.2
  1072.6 780.7 %reduce-scatter.22.cloned.1.call-start = ((), (), s32[]{:S(2)}) async-start(), calls=%async_computation.20 | async-start | bytes 12976128 | tf_op jit(solution)/shard_map/reduce_scatter | solution.py:267
  1083.0 931.3 %reduce-scatter.24.cloned.1.call-start = ((), (), s32[]{:S(2)}) async-start(), calls=%async_computation.21 | async-start | bytes 12976128 | tf_op jit(solution)/shard_map/reduce_scatter | solution.py:268
  1093.3 1083.0 %reduce-scatter.26.cloned.1.call-start = ((), (), s32[]{:S(2)}) async-start(), calls=%async_computation.22 | async-start | bytes 12976128 | tf_op jit(solution)/shard_map/reduce_scatter | solution.py:269
  1116.6 42.5 %copy-start.100 = (f32[1,2,2,128]{3,1,2,0:T(2,128)S(1)}, f32[1,2,2,128]{3,1,2,0:T(2,128)}, u32[]{:S(2)}) copy-start(f32[1,2,2,128]{3,1,2,0:T(2,128)} %copy-done.99) | copy-start | bytes 6148
  (83 other events, 425.4 us)
Sparse Core Ops, SparseCore 0:
  10.9 61.7 all-gather.13
  75.6 58.4 all-gather.11
  137.0 58.1 all-gather.15
  198.0 68.4 all-gather.17
  269.2 68.0 all-gather.19
  340.1 68.0 all-gather.21
  1037.9 92.9 reduce-scatter.27
  1136.5 94.5 reduce-scatter.15
  1236.8 94.5 reduce-scatter.17
  1337.5 113.3 reduce-scatter.19
  1458.0 113.4 reduce-scatter.11
  1577.6 113.4 reduce-scatter.13
  1698.8 154.5 reduce-scatter.21
  1859.8 154.4 reduce-scatter.23
  2021.8 154.4 reduce-scatter.25
where the time goes:
time: 2200 us; the launch traced here: 2180 us
  waiting for transfers between devices  1020 us (46%)
  local copies, waits for them, and re-layouts  572 us (26%)
  blocking collectives  222 us (10%)
  other arithmetic  200 us (9%)
  matrix products  149 us (7%)
    slice x57, local copies, waits for them, and re-layouts, body(): lax.associative_scan(combine_pairs, (next_keep[:, ::-1], state_seed[:, ::...  207 us
    reduce_scatter x1, waiting for transfers between devices, body(): lax.psum_scatter(mlp_gate_full, ('dp', 'seq'), scatter_dimension=0, tiled...  162 us
    reduce_scatter x1, waiting for transfers between devices, body(): lax.psum_scatter(down_full, ('dp', 'seq'), scatter_dimension=0, tiled=True)  162 us
    reduce_scatter x1, waiting for transfers between devices, body(): lax.psum_scatter(mlp_up_full, ('dp', 'seq'), scatter_dimension=0, tiled=T...  161 us
    slice x52, local copies, waits for them, and re-layouts, body(): lax.associative_scan(combine_pairs, (keep_factor, inject), axis=1)  124 us
    reduce_scatter x1, waiting for transfers between devices, body(): lax.psum_scatter(gate_in_full, ('dp', 'seq'), scatter_dimension=0, tiled=...  121 us
    reduce_scatter x1, waiting for transfers between devices, body(): lax.psum_scatter(signal_full, ('dp', 'seq'), scatter_dimension=0, tiled=T...  120 us
    reduce_scatter x1, waiting for transfers between devices, body(): lax.psum_scatter(branch_full, ('dp', 'seq'), scatter_dimension=0, tiled=T...  119 us
  transfers between devices with their start and end apart: 18, of which 10 were waited for; matrix products, arithmetic and copies ran while one was open for 23% of the time, Pallas kernels for 0%

commit v1 on v0

v1 whole, which is shorter than its diff:
```python
import functools

import jax
import jax.numpy as jnp
from jax import lax
from jax.experimental import pallas as pl
from jax.experimental.pallas import tpu as pltpu
from jax.sharding import PartitionSpec as P

epsilon = 1e-06
rate_scale = 8.0
f32 = jnp.float32
bf16 = jnp.bfloat16
gelu_rate = 0.7978845608028654
gelu_cube = 0.044715
halo = 8
vmem_bytes = 48 * 1024 * 1024


def grid_axes():
    dp, seq = lax.axis_size("dp"), lax.axis_size("seq")
    return {
        "z": ("dp", dp, 2, dp // 2),
        "x": ("dp", dp, 1, 2),
        "y": ("seq", seq, 2, seq // 2),
        "c": ("seq", seq, 1, 2),
    }


def place_on(which):
    name, _, stride, count = grid_axes()[which]
    return lax.rem(lax.div(lax.axis_index(name), stride), count)


def ring_step(block, which):
    name, total, stride, count = grid_axes()[which]
    route = []
    for i in range(total):
        k = (i // stride) % count
        route.append((i, i + ((k + 1) % count - k) * stride))
    return lax.ppermute(block, name, route)


def swap_cores(block):
    return ring_step(block, "c")


def passed_along(block, axis, distance):
    devices = range(lax.axis_size(axis))
    route = [(i - distance, i) for i in devices if i - distance in devices]
    return lax.ppermute(block, axis, route)


def gather_rings(piece, order):
    have = []
    for which in order:
        count = grid_axes()[which][3]
        me = place_on(which)
        spot = sum(1 for other in have if "zxyc".index(other) < "zxyc".index(which))
        parts = [piece]
        for _ in range(count - 1):
            parts.append(ring_step(parts[-1], which))
        if count == 2:
            first = me == 0
            a, b = parts
            piece = jnp.stack([jnp.where(first, a, b), jnp.where(first, b, a)], axis=spot)
        else:
            stacked = jnp.zeros(piece.shape[:spot] + (count,) + piece.shape[spot:], piece.dtype)
            for t, part in enumerate(parts):
                stacked = lax.dynamic_update_index_in_dim(
                    stacked, part, lax.rem(me - t + count, count), spot
                )
            piece = stacked
        have.append(which)
    return piece


def scatter_rings(whole, order, left):
    left = list(left)
    wide = whole.dtype
    for which in order:
        count = grid_axes()[which][3]
        me = place_on(which)
        spot = left.index(which)

        def own(back):
            return lax.dynamic_index_in_dim(whole, lax.rem(me - back + count, count), spot, False)

        total = own(1)
        for step in range(count - 1):
            moved = ring_step(total.astype(wide), which)
            total = moved.astype(f32) + own(step + 2).astype(f32)
        left.remove(which)
        whole = total if which == order[-1] else total.astype(wide)
    return whole


def rms_scale(values, norm_gain):
    return (
        values * lax.rsqrt(jnp.mean(values * values, axis=-1, keepdims=True) + epsilon) * norm_gain
    )


def gelu_parts(v):
    th = jnp.tanh(gelu_rate * (v + gelu_cube * v * v * v))
    value = 0.5 * v * (1.0 + th)
    slope = 0.5 * (1.0 + th) + 0.5 * v * (1.0 - th * th) * gelu_rate * (
        1.0 + 3.0 * gelu_cube * v * v
    )
    return value, slope


def scan_rows(a, b, reverse):
    count = a.shape[0]
    row = lax.broadcasted_iota(jnp.int32, a.shape, 0)
    s = 1
    while s < count:
        if s < 8:
            shift = count - s if reverse else s
            valid = row < count - s if reverse else row >= s
            a_far = pltpu.roll(a, shift, 0)
            b_far = pltpu.roll(b, shift, 0)
            b = jnp.where(valid, a * b_far + b, b)
            a = jnp.where(valid, a * a_far, a)
        elif reverse:
            b = jnp.concatenate([a[:-s] * b[s:] + b[:-s], b[-s:]], axis=0)
            a = jnp.concatenate([a[:-s] * a[s:], a[-s:]], axis=0)
        else:
            b = jnp.concatenate([b[:s], a[s:] * b[:-s] + b[s:]], axis=0)
            a = jnp.concatenate([a[:s], a[s:] * a[:-s]], axis=0)
        s *= 2
    return a, b


def minus_expm1(x):
    t = 1.0 + x * (1.0 / 8.0)
    for k in (7.0, 6.0, 5.0, 4.0, 3.0, 2.0):
        t = 1.0 + x * (1.0 / k) * t
    return jnp.where(x > -0.4, -x * t, 1.0 - jnp.exp(x))


def gate_values(conv_low, rec_w, inp_w, rate, reset):
    r = jax.nn.sigmoid(jnp.dot(conv_low, rec_w, preferred_element_type=f32))
    g = jax.nn.sigmoid(jnp.dot(conv_low, inp_w, preferred_element_type=f32))
    log_keep = rate * (0.1 + 0.9 * r)
    keep = jnp.where(reset, 0.0, jnp.exp(log_keep))
    lost = minus_expm1(2.0 * log_keep)
    inverse = lax.rsqrt(lost)
    scale = jnp.where(reset, 1.0, lost * inverse)
    return r, g, keep, lost, inverse, scale


def forward_kernel(
    row_count,
    sig_ref,
    tail_ref,
    mask_ref,
    taps_ref,
    rate_ref,
    rec_ref,
    inp_ref,
    conv_ref,
    keep_ref,
    cum_ref,
    local_ref,
):
    row_tokens = sig_ref.shape[0] // row_count
    for b in range(row_count):
        rows = pl.ds(b * row_tokens, row_tokens)
        sig = sig_ref[rows, :].astype(f32)
        ext = jnp.concatenate([tail_ref[pl.ds(b * halo, halo), :], sig], axis=0)
        conv = taps_ref[0:1, :] * sig
        for k in range(1, taps_ref.shape[0]):
            conv += taps_ref[k : k + 1, :] * pltpu.roll(ext, k, 0)[halo:] * mask_ref[k - 1, rows, :]
        conv_low = conv.astype(bf16)
        conv_ref[rows, :] = conv_low
        reset = mask_ref[0, rows, :] == 0.0
        _, g, keep, _, _, scale = gate_values(
            conv_low, rec_ref[...], inp_ref[...], rate_ref[...], reset
        )
        keep_ref[rows, :] = keep
        cum, local = scan_rows(keep, scale * conv_low.astype(f32) * g, False)
        cum_ref[rows, :] = cum
        local_ref[rows, :] = local


def reverse_kernel(
    row_count, mixed_grad_ref, states_ref, gate_ref, keep_ref, gate_low_ref, tail_ref, local_ref
):
    row_tokens = keep_ref.shape[0] // row_count
    for b in range(row_count):
        rows = pl.ds(b * row_tokens, row_tokens)
        value, slope = gelu_parts(gate_ref[rows, :])
        grad = mixed_grad_ref[rows, :]
        gate_low_ref[rows, :] = (grad * states_ref[rows, :] * slope).astype(bf16)
        keep = keep_ref[rows, :]
        row = lax.broadcasted_iota(jnp.int32, keep.shape, 0)
        next_keep = jnp.where(row == row_tokens - 1, 1.0, pltpu.roll(keep, row_tokens - 1, 0))
        tail, local = scan_rows(next_keep, grad * value, True)
        tail_ref[rows, :] = tail
        local_ref[rows, :] = local


def backward_kernel(
    row_count,
    sig_ref,
    before_ref,
    mask_ref,
    taps_ref,
    rate_ref,
    rec_ref,
    inp_ref,
    conv_ref,
    states_ref,
    state_in_ref,
    tail_ref,
    local_ref,
    grad_in_ref,
    signal_ref,
    head_ref,
    rec_grad_ref,
    inp_grad_ref,
    sums_ref,
):
    row_tokens = sig_ref.shape[0] // row_count
    tap_count = taps_ref.shape[0]
    rate = rate_ref[...]
    sums = [0.0] * (tap_count + 1)
    rec_total = 0.0
    inp_total = 0.0
    for b in range(row_count):
        rows = pl.ds(b * row_tokens, row_tokens)
        conv_low = conv_ref[rows, :]
        conv = conv_low.astype(f32)
        reset = mask_ref[0, rows, :] == 0.0
        r, g, keep, lost, inverse, scale = gate_values(
            conv_low, rec_ref[...], inp_ref[...], rate, reset
        )
        state_grad = local_ref[rows, :] + tail_ref[rows, :] * grad_in_ref[b : b + 1, :]
        states = states_ref[rows, :]
        row = lax.broadcasted_iota(jnp.int32, states.shape, 0)
        before = jnp.where(row == 0, state_in_ref[b : b + 1, :], pltpu.roll(states, 1, 0))
        direct = state_grad * g
        dlog = state_grad * before * keep - jnp.where(
            reset, 0.0, direct * conv * (1.0 - lost) * inverse
        )
        rec_low = (dlog * rate * 0.9 * r * (1.0 - r)).astype(bf16)
        input_low = (direct * scale * conv * (1.0 - g)).astype(bf16)
        sums[0] += jnp.sum(dlog * (0.1 + 0.9 * r), axis=0, keepdims=True)
        first = (((0,), (0,)), ((), ()))
        second = (((1,), (1,)), ((), ()))
        rec_total += lax.dot_general(conv_low, rec_low, first, preferred_element_type=f32)
        inp_total += lax.dot_general(conv_low, input_low, first, preferred_element_type=f32)
        conv_grad = (
            direct * scale
            + lax.dot_general(rec_low, rec_ref[...], second, preferred_element_type=f32)
            + lax.dot_general(input_low, inp_ref[...], second, preferred_element_type=f32)
        )
        sig = sig_ref[rows, :].astype(f32)
        ext = jnp.concatenate([before_ref[pl.ds(b * halo, halo), :], sig], axis=0)
        blank = jnp.zeros((halo, sig.shape[1]), f32)
        back = jnp.concatenate([blank, conv_grad * taps_ref[0:1, :]], axis=0)
        sums[1] += jnp.sum(conv_grad * sig, axis=0, keepdims=True)
        for k in range(1, tap_count):
            part = conv_grad * mask_ref[k - 1, rows, :]
            sums[1 + k] += jnp.sum(part * pltpu.roll(ext, k, 0)[halo:], axis=0, keepdims=True)
            moved = jnp.concatenate([blank, part * taps_ref[k : k + 1, :]], axis=0)
            back += pltpu.roll(moved, row_tokens + halo - k, 0)
        head_ref[pl.ds(b * halo, halo), :] = back[:halo]
        signal_ref[rows, :] = back[halo:]
    rec_grad_ref[...] = rec_total
    inp_grad_ref[...] = inp_total
    for k in range(tap_count + 1):
        sums_ref[k : k + 1, :] = sums[k]


def channel_call(kernel, row_count, ins, outs, width, block, flops):
    def spec(shape):
        if len(shape) == 3:
            return pl.BlockSpec((shape[0], shape[1], block), lambda h: (0, 0, 0))
        if shape == (width, block):
            return pl.BlockSpec((block, block), lambda h: (h, 0))
        return pl.BlockSpec((shape[0], block), lambda h: (0, h))

    moved = sum(a.size * a.dtype.itemsize for a in ins) + sum(
        o.size * o.dtype.itemsize for o in outs
    )
    return pl.pallas_call(
        functools.partial(kernel, row_count),
        grid=(width // block,),
        in_specs=[spec(a.shape) for a in ins],
        out_specs=[spec(o.shape) for o in outs],
        out_shape=outs,
        compiler_params=pltpu.CompilerParams(vmem_limit_bytes=vmem_bytes),
        cost_estimate=pl.CostEstimate(flops=flops, bytes_accessed=moved, transcendentals=0),
    )(*ins)


def carry_before(factor, value, reverse):
    count = lax.axis_size("seq")
    place = lax.axis_index("seq")
    both = lax.all_gather(jnp.stack([factor, value]), "seq")
    state = jnp.zeros_like(value)
    turns = range(count - 1, 0, -1) if reverse else range(count - 1)
    for source in turns:
        passed = place < source if reverse else source < place
        state = jnp.where(passed, both[source, 0] * state + both[source, 1], state)
    return state


def body(
    tokens,
    segments,
    norm_in_gain,
    gate_in_weight,
    signal_in_weight,
    conv_weight,
    rec_gate_weight,
    input_gate_weight,
    decay_param,
    branch_out_weight,
    norm_mid_gain,
    mlp_gate_weight,
    mlp_up_weight,
    mlp_down_weight,
    cotangent,
):
    row_count, row_tokens, model_width = tokens.shape
    lru_width = signal_in_weight.shape[1]
    block_width = rec_gate_weight.shape[1]
    ff_width = mlp_gate_weight.shape[1]
    tap_count = conv_weight.shape[0]
    halo_rows = tap_count - 1
    token_count = row_count * row_tokens
    device_count = lax.axis_size("dp") * lax.axis_size("seq")
    core = place_on("c")
    model_piece = norm_in_gain.shape[0]
    lru_piece = decay_param.shape[0]

    small = jnp.concatenate(
        [norm_in_gain, norm_mid_gain, decay_param, conv_weight.reshape(-1)], axis=0
    )
    small_size = small.shape[0]
    pair_width = 2 * block_width
    small_rows = -(-small_size // pair_width)
    small = jnp.pad(small, (0, small_rows * pair_width - small_size)).reshape(
        small_rows, pair_width
    )
    gate_pair = jnp.concatenate([rec_gate_weight, input_gate_weight], axis=1)
    pack = jnp.concatenate([gate_pair, small], axis=0)
    pack_rows = pack.shape[0]
    pack = jnp.pad(pack, ((0, -pack_rows % 16), (0, 0)))

    full_signal = gather_rings(signal_in_weight, "zyxc").reshape(model_width, lru_width)
    full_gate_in = gather_rings(gate_in_weight, "zxyc").reshape(model_width, lru_width)
    full_pack = gather_rings(pack, "zyxc").reshape(device_count, pack.shape[0], pair_width)
    full_branch = gather_rings(branch_out_weight, "zyxc").reshape(lru_width, model_width)
    full_mlp_gate = gather_rings(mlp_gate_weight, "zyxc").reshape(model_width, ff_width)
    full_mlp_up = gather_rings(mlp_up_weight, "zxyc").reshape(model_width, ff_width)
    full_mlp_down = gather_rings(mlp_down_weight, "xyzc").reshape(ff_width, model_width)

    gate_pairs = full_pack[:, :lru_piece].reshape(lru_width, pair_width)
    full_rec, full_input = gate_pairs[:, :block_width], gate_pairs[:, block_width:]
    smalls = full_pack[:, lru_piece : lru_piece + small_rows].reshape(device_count, -1).astype(f32)
    gain_in = smalls[:, :model_piece].reshape(model_width)
    gain_mid = smalls[:, model_piece : 2 * model_piece].reshape(model_width)
    start = 2 * model_piece
    decay_full = smalls[:, start : start + lru_piece].reshape(lru_width)
    start += lru_piece
    taps = (
        smalls[:, start : start + tap_count * lru_piece]
        .reshape(device_count, tap_count, lru_piece)
        .transpose(1, 0, 2)
        .reshape(tap_count, lru_width)
    )
    rate = (-rate_scale * jax.nn.softplus(-decay_full))[None, :]

    inputs = tokens.astype(f32).reshape(token_count, model_width)
    scale_in = lax.rsqrt(jnp.mean(inputs * inputs, axis=-1, keepdims=True) + epsilon)
    normed_in = (inputs * scale_in * gain_in).astype(bf16)
    signal = jnp.dot(normed_in, full_signal, preferred_element_type=f32).astype(bf16)
    gate_pre = jnp.dot(normed_in, full_gate_in, preferred_element_type=f32)
    tail_ids = passed_along(segments[:, row_tokens - halo_rows :], "seq", 1)
    tail_ids = jnp.where(lax.axis_index("seq") == 0, jnp.int32(-1), tail_ids)
    ids_ext = jnp.concatenate([tail_ids, segments], axis=1)
    masks = jnp.stack(
        [
            (ids_ext[:, halo_rows - k : halo_rows - k + row_tokens] == segments).astype(f32)
            for k in range(1, tap_count)
        ]
    )
    masks = jnp.broadcast_to(
        masks.reshape(halo_rows, token_count, 1), (halo_rows, token_count, block_width)
    )
    tail_signal = passed_along(
        signal.reshape(row_count, row_tokens, lru_width)[:, row_tokens - halo_rows :], "seq", 1
    )
    before = jnp.pad(
        tail_signal.astype(f32), ((0, 0), (halo - halo_rows, 0), (0, 0))
    ).reshape(row_count * halo, lru_width)

    wide_f32 = jax.ShapeDtypeStruct((token_count, lru_width), f32)
    wide_bf16 = jax.ShapeDtypeStruct((token_count, lru_width), bf16)
    block_flops = 4 * token_count * lru_width * block_width
    conv_low, keep, cum_keep, local_state = channel_call(
        forward_kernel,
        row_count,
        [signal, before, masks, taps, rate, full_rec, full_input],
        [wide_bf16, wide_f32, wide_f32, wide_f32],
        lru_width,
        block_width,
        block_flops,
    )
    cum3 = cum_keep.reshape(row_count, row_tokens, lru_width)
    local3 = local_state.reshape(row_count, row_tokens, lru_width)
    state_in = carry_before(cum3[:, -1], local3[:, -1], False)
    states = (local3 + cum3 * state_in[:, None, :]).reshape(token_count, lru_width)
    mixed = (gelu_parts(gate_pre)[0] * states).astype(bf16)
    middle = inputs + jnp.dot(mixed, full_branch, preferred_element_type=f32)
    scale_mid = lax.rsqrt(jnp.mean(middle * middle, axis=-1, keepdims=True) + epsilon)
    normed_mid = (middle * scale_mid * gain_mid).astype(bf16)
    mlp_gate_pre = jnp.dot(normed_mid, full_mlp_gate, preferred_element_type=f32)
    mlp_up_pre = jnp.dot(normed_mid, full_mlp_up, preferred_element_type=f32)
    mlp_act, mlp_slope = gelu_parts(mlp_gate_pre)
    hidden = (mlp_act * mlp_up_pre).astype(bf16)
    block_out = middle + jnp.dot(hidden, full_mlp_down, preferred_element_type=f32)

    out_grad = cotangent.reshape(token_count, model_width)

    def other_half(a):
        width = a.shape[1] // 2
        return lax.dynamic_slice_in_dim(a, (1 - core) * width, width, 1)

    def my_half(a):
        width = a.shape[1] // 2
        return lax.dynamic_slice_in_dim(a, core * width, width, 1)

    def both_rows(a):
        return jnp.concatenate([a, swap_cores(a)], axis=0)

    def both_halves(a):
        return jnp.concatenate([my_half(a), swap_cores(other_half(a))], axis=0)

    def chip_grad(left_rows, right_half, order):
        whole = lax.dot_general(
            left_rows, right_half, (((0,), (0,)), ((), ())), preferred_element_type=f32
        ).astype(bf16)
        return chip_scatter(whole, order)

    def chip_scatter(whole, order):
        sizes = [grid_axes()[a][3] for a in "zxy"]
        rows = whole.shape[0] // (sizes[0] * sizes[1] * sizes[2])
        mine = scatter_rings(whole.reshape(*sizes, rows, whole.shape[1]), order, "zxy")
        mine = mine.reshape(2, rows // 2, whole.shape[1])
        sent = swap_cores(lax.dynamic_index_in_dim(mine, 1 - core, 0, False))
        kept = lax.dynamic_index_in_dim(mine, core, 0, False)
        first = core == 0
        return jnp.concatenate(
            [jnp.where(first, kept, sent), jnp.where(first, sent, kept)], axis=1
        )

    down_shard = chip_grad(both_rows(hidden), both_halves(out_grad), "zyx")
    hidden_grad = lax.dot_general(
        out_grad, full_mlp_down, (((1,), (1,)), ((), ())), preferred_element_type=f32
    )
    gate_grad_low = (hidden_grad * mlp_up_pre * mlp_slope).astype(bf16)
    up_grad_low = (hidden_grad * mlp_act).astype(bf16)
    normed_mid_pair = both_rows(normed_mid)
    mlp_gate_shard = chip_grad(normed_mid_pair, both_halves(gate_grad_low), "xyz")
    mlp_up_shard = chip_grad(normed_mid_pair, both_halves(up_grad_low), "yxz")
    transposed = (((1,), (1,)), ((), ()))
    normed_mid_grad = lax.dot_general(
        gate_grad_low, full_mlp_gate, transposed, preferred_element_type=f32
    ) + lax.dot_general(up_grad_low, full_mlp_up, transposed, preferred_element_type=f32)

    def norm_back(grad, values, scale, gain):
        weighted = grad * gain
        inner = jnp.mean(weighted * values, axis=-1, keepdims=True)
        back = scale * weighted - values * (scale * scale * scale * inner)
        return back, jnp.sum(grad * values * scale, axis=0)

    mid_back, gain_mid_grad = norm_back(normed_mid_grad, middle, scale_mid, gain_mid)
    middle_grad = out_grad.astype(f32) + mid_back
    middle_low = middle_grad.astype(bf16)
    branch_shard = chip_grad(both_rows(mixed), both_halves(middle_low), "xyz")
    mixed_grad = lax.dot_general(middle_low, full_branch, transposed, preferred_element_type=f32)
    gate_pre_low, tail_keep, local_grad = channel_call(
        reverse_kernel,
        row_count,
        [mixed_grad, states, gate_pre, keep],
        [wide_bf16, wide_f32, wide_f32],
        lru_width,
        block_width,
        0,
    )
    normed_in_pair = both_rows(normed_in)
    gate_in_shard = chip_grad(normed_in_pair, both_halves(gate_pre_low), "yxz")
    first_keep = keep.reshape(row_count, row_tokens, lru_width)[:, 0]
    head_factor = first_keep * tail_keep.reshape(row_count, row_tokens, lru_width)[:, 0]
    head_grad = first_keep * local_grad.reshape(row_count, row_tokens, lru_width)[:, 0]
    grad_in = carry_before(head_factor, head_grad, True)
    square = jax.ShapeDtypeStruct((lru_width, block_width), f32)
    signal_part, head_part, rec_full, input_full, sums = channel_call(
        backward_kernel,
        row_count,
        [
            signal,
            before,
            masks,
            taps,
            rate,
            full_rec,
            full_input,
            conv_low,
            states,
            state_in,
            tail_keep,
            local_grad,
            grad_in,
        ],
        [
            wide_f32,
            jax.ShapeDtypeStruct((row_count * halo, lru_width), f32),
            square,
            square,
            jax.ShapeDtypeStruct((tap_count + 1, lru_width), f32),
        ],
        lru_width,
        block_width,
        3 * block_flops,
    )
    from_right = passed_along(
        head_part.reshape(row_count, halo, lru_width)[:, halo - halo_rows :].astype(bf16),
        "seq",
        -1,
    ).astype(f32)
    signal_low = (
        (
            signal_part.reshape(row_count, row_tokens, lru_width)
            + jnp.pad(from_right, ((0, 0), (row_tokens - halo_rows, 0), (0, 0)))
        )
        .astype(bf16)
        .reshape(token_count, lru_width)
    )
    signal_shard = chip_grad(normed_in_pair, both_halves(signal_low), "xyz")
    pair_grads = jnp.where(core == 0, rec_full, input_full) + swap_cores(
        jnp.where(core == 0, input_full, rec_full).astype(bf16)
    ).astype(f32)
    pair_shard = chip_scatter(pair_grads.astype(bf16), "yxz")
    normed_in_grad = lax.dot_general(
        gate_pre_low, full_gate_in, transposed, preferred_element_type=f32
    ) + lax.dot_general(signal_low, full_signal, transposed, preferred_element_type=f32)
    in_back, gain_in_grad = norm_back(normed_in_grad, inputs, scale_in, gain_in)
    tokens_grad = (middle_grad + in_back).reshape(tokens.shape)

    decay_grad = sums[0] * rate_scale * jax.nn.sigmoid(-decay_full)
    tap_grads = sums[1:].reshape(tap_count, device_count, lru_piece).transpose(1, 0, 2)
    small_grads = jnp.concatenate(
        [
            gain_in_grad.reshape(device_count, model_piece),
            gain_mid_grad.reshape(device_count, model_piece),
            decay_grad.reshape(device_count, lru_piece),
            tap_grads.reshape(device_count, tap_count * lru_piece),
        ],
        axis=1,
    )
    sizes = [grid_axes()[a][3] for a in "zxyc"]
    small_shard = scatter_rings(small_grads.reshape(*sizes, 1, small_size), "cxyz", "zxyc")[0]
    start = 2 * model_piece + lru_piece
    return (
        block_out.reshape(tokens.shape),
        tokens_grad,
        small_shard[:model_piece],
        gate_in_shard,
        signal_shard,
        small_shard[start:].reshape(tap_count, lru_piece),
        pair_shard[:, :block_width],
        pair_shard[:, block_width:],
        small_shard[2 * model_piece : start],
        branch_shard,
        small_shard[model_piece : 2 * model_piece],
        mlp_gate_shard,
        mlp_up_shard,
        down_shard,
    )


def solution(mesh):
    rows = P(("dp", "seq"))
    matrix = P(("dp", "seq"), None)
    columns = P(None, ("dp", "seq"))
    tokens = P("dp", "seq", None)
    return jax.shard_map(
        body,
        mesh=mesh,
        in_specs=(
            tokens,
            P("dp", "seq"),
            rows,
            matrix,
            matrix,
            columns,
            matrix,
            matrix,
            rows,
            matrix,
            rows,
            matrix,
            matrix,
            matrix,
            tokens,
        ),
        out_specs=(
            tokens,
            tokens,
            rows,
            matrix,
            matrix,
            columns,
            matrix,
            matrix,
            rows,
            matrix,
            rows,
            matrix,
            matrix,
            matrix,
        ),
        check_vma=False,
    )
```

time: 2200 us -> 697 us (0.32)
  waiting for transfers between devices: 1020 us -> 353 us
  local copies, waits for them, and re-layouts: 572 us -> 56.9 us
  blocking collectives: 222 us -> 10.7 us
  other arithmetic: 200 us -> 63.4 us
  starting transfers between devices: 6.82 us -> 61.6 us
  matrix products: 149 us -> 95.1 us
  Pallas kernels: 0 us -> 45.9 us
    reduce_scatter x8 -> x0, waiting for transfers between devices: 1010 us -> none  [the longest x1 162 us: body(): lax.psum_scatter(mlp_gate_full, ('dp', 'seq'), scatter_dimension=0, tiled...]
    ppermute x0 -> x101, waiting for transfers between devices: none -> 352 us  [ring_step(): return lax.ppermute(block, name, route)]
    slice x116 -> x16, local copies, waits for them, and re-layouts: 333 us -> 8.14 us  [the longest x1 2.08 us: body(): gate_pairs = full_pack[:, :lru_piece].reshape(lru_width, pair_width)]
    all_gather x7 -> x2, blocking collectives: 143 us -> 10.7 us  [carry_before(): both = lax.all_gather(jnp.stack([factor, value]), 'seq')]
    pad x56 -> x0, local copies, waits for them, and re-layouts: 129 us -> none  [the longest x28 64.4 us: body(): lax.associative_scan(combine_pairs, (keep_factor, inject), axis=1)]
    add x51 -> x14, other arithmetic: 92.7 us -> 2.58 us  [the longest x1 2.29 us: body(): tokens_grad = (middle_grad + in_back).reshape(tokens.shape)]
    unnamed x2 -> x0, blocking collectives: 79.5 us -> none
    ppermute x0 -> x101, starting transfers between devices: none -> 56.5 us  [ring_step(): return lax.ppermute(block, name, route)]
  transfers between devices with their start and end apart: 18 -> 104, of which waited for: 10 -> 53; matrix products, arithmetic and copies ran while one was open for 23% -> 31% of each run, Pallas kernels for 0% -> 7%
where the time goes in v1:
time: 697 us; the launch traced here: 690 us
  waiting for transfers between devices  353 us (51%)
  matrix products  95.1 us (14%)
  other arithmetic  63.4 us (9%)
  starting transfers between devices  61.6 us (9%)
  local copies, waits for them, and re-layouts  56.9 us (8%)
  Pallas kernels  45.9 us (7%)
  blocking collectives  10.7 us (2%)
    ppermute x101, waiting for transfers between devices, ring_step(): return lax.ppermute(block, name, route)  352 us
    ppermute x101, starting transfers between devices, ring_step(): return lax.ppermute(block, name, route)  56.5 us
    pallas_call x3, Pallas kernels, channel_call(): pl.pallas_call(functools.partial(kernel, row_count), grid=(width // block...  45.9 us
    another operation x42, other arithmetic, gather_rings(): jnp.stack([jnp.where(first, a, b), jnp.where(first, b, a)], axis=spot)  41.6 us
    dot_general x6, matrix products, chip_grad(): lax.dot_general(left_rows, right_half, (((0,), (0,)), ((), ())), preferre...  22.1 us
    dynamic_update_slice x26, local copies, waits for them, and re-layouts, gather_rings(): lax.dynamic_update_index_in_dim(stacked, part, lax.rem(me - t + count, co...  17.5 us
    dot_general x1, matrix products, body(): jnp.dot(normed_mid, full_mlp_gate, preferred_element_type=f32)  14.5 us
  transfers between devices with their start and end apart: 104, of which 53 were waited for; matrix products, arithmetic and copies ran while one was open for 31% of the time, Pallas kernels for 7%

profile of v1, /device:TPU:0, one launch (start us, length us, event | category | flops | bytes accessed | tf_op | source)
XLA Modules:
  0.0 689.7 jit_solution(13040668315377111039)
XLA Ops:
  25.0 5.7 collective-permute-done.1
  30.7 5.7 collective-permute-done.2
  45.1 4.2 collective-permute-start.13
  57.5 7.3 %collective-permute-done.8 = bf16[32,1536]{1,0:T(8,128)(2,1)S(1)} collective-permute-done((bf16[32,1536]{1,0:T(8,128)(2,1)S(1)}, bf16[32,1536]{1,0:T(8,128)(2,1)S(1)}, u32[]{:S(2)}, u32[]{:S(2)}) %collective-permute-start.8) | collective-permute-done | bytes 98336 | tf_op jit(solution)/shard_map/ppermute | solution.py:41
  78.6 7.4 %collective-permute-done.28 = bf16[32,3072]{1,0:T(8,128)(2,1)S(1)} collective-permute-done((bf16[32,3072]{1,0:T(8,128)(2,1)S(1)}, bf16[32,3072]{1,0:T(8,128)(2,1)S(1)}, u32[]{:S(2)}, u32[]{:S(2)}) %collective-permute-start.28) | collective-permute-done | bytes 196640 | tf_op jit(solution)/shard_map/ppermute | solution.py:41
  86.6 6.8 collective-permute-done.34
  126.1 12.6 %collective-permute-done.24 = bf16[4,2,48,1024]{3,2,1,0:T(8,128)(2,1)} collective-permute-done((bf16[4,2,48,1024]{3,2,1,0:T(8,128)(2,1)}, bf16[4,2,48,1024]{3,2,1,0:T(8,128)(2,1)}, u32[]{:S(2)}, u32[]{:S(2)}) %collective-permute-start.24) | collective-permute-done | bytes 786464 | tf_op jit(solution)/shard_map/ppermute | solution.py:41
  141.8 13.7 %collective-permute-done.16 = bf16[4,2,32,1536]{3,2,1,0:T(8,128)(2,1)S(1)} collective-permute-done((bf16[4,2,32,1536]{3,2,1,0:T(8,128)(2,1)S(1)}, bf16[4,2,32,1536]{3,2,1,0:T(8,128)(2,1)S(1)}, u32[]{:S(2)}, u32[]{:S(2)}) %collective-permute-start.16) | collective-permute-done | bytes 786464 | tf_op jit(solution)/shard_map/ppermute | solution.py:41
  160.3 17.8 %collective-permute-done.42 = bf16[2,2,96,1024]{3,2,1,0:T(8,128)(2,1)S(1)} collective-permute-done((bf16[2,2,96,1024]{3,2,1,0:T(8,128)(2,1)S(1)}, bf16[2,2,96,1024]{3,2,1,0:T(8,128)(2,1)S(1)}, u32[]{:S(2)}, u32[]{:S(2)}) %collective-permute-start.42) | collective-permute-done | bytes 786464 | tf_op jit(solution)/shard_map/ppermute | solution.py:41
  179.0 9.5 %collective-permute-done.30 = bf16[4,2,32,3072]{3,2,0,1:T(8,128)(2,1)S(1)} collective-permute-done((bf16[4,2,32,3072]{3,2,0,1:T(8,128)(2,1)S(1)}, bf16[4,2,32,3072]{3,2,0,1:T(8,128)(2,1)S(1)}, u32[]{:S(2)}, u32[]{:S(2)}) %collective-permute-start.30) | collective-permute-done | bytes 1572896 | tf_op jit(solution)/shard_map/ppermute | solution.py:41
  203.1 13.2 %shard_map.254 = (bf16[512,1536]{1,0:T(8,128)(2,1)S(1)}, f32[512,1536]{1,0:T(8,128)}, f32[512,1536]{1,0:T(8,128)}, f32[512,1536]{1,0:T(8,128)}) custom-call(bf16[512,1536]{1,0:T(8,128)(2,1)S(1)} %convolution_convert_fusion.2.sig_ref, f32[16,1536]{1,0:T(8,128)S(1)} %bitcast_convert_fusion.tail_ref.before_ref, f32[3,512,128]{2,1,0:T(8,128)S(1)} %broadcast_in_dim.134.mask_ref, ...), custom_call_target="tpu_custom_call" | custom-call | flops 402653184 | bytes 14284800 | tf_op jit(solution)/shard_map/pallas_call | solution.py:288
  218.3 5.4 all-gather
  223.7 8.9 %fusion.20 = (bf16[512,1536]{1,0:T(8,128)(2,1)}, f32[512,1536]{1,0:T(8,128)}, f32[512,1536]{1,0:T(8,128)}) fusion(f32[512,1536]{1,0:T(8,128)} %get-tuple-element.26, f32[512,1536]{1,0:T(8,128)} %get-tuple-element.27, f32[2,1536]{1,0:T(2,128)S(1)} %fusion.113.state_in_ref, bf16[512,1024]{1,0:T(8,128)(2,1)} %bitcast.607, bf16[1024,1536]{1,0:T(8,128)(2,1)S(1)} %bitcast.592), kind=kOutput, calls=%fused_computation.30 | convolution fusion | flops 1620049920 | bytes 18362368 | tf_op jit(solution)/shard_map/dot_general | solution.py:382
  238.7 4.9 select_bitcast_fusion.1
  243.6 5.2 pad_maximum_fusion.2
  248.8 8.3 %fusion.159 = f32[3072,512]{0,1:T(8,128)} fusion(bf16[3072,1024]{1,0:T(8,128)(2,1)} %bitcast.596, bf16[512,1024]{1,0:T(8,128)(2,1)S(1)} %bitcast.595), kind=kOutput, calls=%fused_computation.430 | convolution fusion | flops 3221225472 | bytes 13631488 | tf_op jit(solution)/shard_map/dot_general | solution.py:463
  272.3 8.1 %fusion.158 = f32[512,3072]{1,0:T(8,128)} fusion(bf16[512,1024]{1,0:T(8,128)(2,1)S(1)} %copy-done.30, bf16[1024,3072]{1,0:T(8,128)(2,1)} %bitcast.598), kind=kOutput, calls=%fused_computation.429 | convolution fusion | flops 3221225472 | bytes 13631488 | tf_op jit(solution)/shard_map/dot_general | solution.py:423
  280.4 14.5 %fusion.6 = (bf16[512,3072]{1,0:T(8,128)(2,1)S(1)}, bf16[512,3072]{1,0:T(8,128)(2,1)S(1)}, bf16[512,3072]{1,0:T(8,128)(2,1)}) fusion(f32[512,3072]{1,0:T(8,128)} %fusion.158, f32[3072,512]{0,1:T(8,128)} %fusion.159, bf16[512,1024]{1,0:T(8,128)(2,1)S(1)} %copy-done.30, bf16[1024,3072]{1,0:T(8,128)(2,1)} %bitcast.602), kind=kOutput, calls=%fused_computation.8 | convolution fusion | flops 3260547072 | bytes 29360128 | tf_op jit(solution)/shard_map/dot_general | solution.py:422
  298.5 6.1 multiply_reduce_fusion
  313.5 13.3 %shard_map.255 = (bf16[512,1536]{1,0:T(8,128)(2,1)S(1)}, f32[512,1536]{1,0:T(8,128)S(1)}, f32[512,1536]{1,0:T(8,128)}) custom-call(f32[512,1536]{1,0:T(8,128)} %fusion.161.mixed_grad_ref, f32[512,1536]{1,0:T(8,128)} %get-tuple-element.43.states_ref, f32[512,1536]{1,0:T(8,128)} %get-tuple-element.129.gate_ref, f32[512,1536]{1,0:T(8,128)} %get-tuple-element.28.keep_ref), custom_call_target="tpu_custom_call" | custom-call | bytes 20447232 | tf_op jit(solution)/shard_map/pallas_call | solution.py:288
  327.9 5.3 all-gather.1
  333.3 19.4 %shard_map.256 = (f32[512,1536]{1,0:T(8,128)}, f32[16,1536]{1,0:T(8,128)S(1)}, f32[1536,128]{1,0:T(8,128)S(1)}, f32[1536,128]{1,0:T(8,128)S(1)}, f32[5,1536]{1,0:T(8,128)S(1)}) custom-call(bf16[512,1536]{1,0:T(8,128)(2,1)S(1)} %convolution_convert_fusion.2.sig_ref, f32[16,1536]{1,0:T(8,128)S(1)} %bitcast_convert_fusion.tail_ref.before_ref, ...), custom_call_target="tpu_custom_call" | custom-call | flops 1207959552 | bytes 19156992 | tf_op jit(solution)/shard_map/pallas_call | solution.py:288
  355.4 9.0 %convolution_add_fusion.2 = f32[512,1024]{1,0:T(8,128)} fusion(f32[512,1024]{1,0:T(8,128)} %copy-done.2, bf16[512,3072]{1,0:T(8,128)(2,1)} %get-tuple-element.46, bf16[3072,1024]{1,0:T(8,128)(2,1)} %bitcast.597), kind=kOutput, calls=%fused_computation.128 | convolution fusion | flops 3221749760 | bytes 13631488 | tf_op jit(solution)/shard_map/dot_general | solution.py:426
  392.5 5.2 collective-permute-done.49
  398.9 4.2 collective-permute-done.50
  404.5 4.8 collective-permute-done.67
  414.7 5.0 collective-permute-done.69
  420.6 4.9 collective-permute-done.70
  440.1 13.8 %collective-permute-done.75 = bf16[4,2,96,512]{3,2,1,0:T(8,128)(2,1)S(1)} collective-permute-done((bf16[4,2,96,512]{3,2,1,0:T(8,128)(2,1)S(1)}, bf16[4,2,96,512]{3,2,1,0:T(8,128)(2,1)S(1)}, u32[]{:S(2)}, u32[]{:S(2)}) %collective-permute-start.75) | collective-permute-done | bytes 786464 | tf_op jit(solution)/shard_map/ppermute | solution.py:41
  456.1 5.3 convolution_convert_fusion
  466.1 16.7 %collective-permute-done.76 = bf16[4,96,512]{2,1,0:T(8,128)(2,1)S(1)} collective-permute-done((bf16[4,96,512]{2,1,0:T(8,128)(2,1)S(1)}, bf16[4,96,512]{2,1,0:T(8,128)(2,1)S(1)}, u32[]{:S(2)}, u32[]{:S(2)}) %collective-permute-start.76) | collective-permute-done | bytes 393248 | tf_op jit(solution)/shard_map/ppermute | solution.py:41
  483.1 6.3 collective-permute-done.77
  491.1 6.1 collective-permute-done.78
  498.3 6.2 collective-permute-done.79
  508.2 24.2 %collective-permute-done.61 = bf16[4,64,768]{2,1,0:T(8,128)(2,1)S(1)} collective-permute-done((bf16[4,64,768]{2,1,0:T(8,128)(2,1)S(1)}, bf16[4,64,768]{2,1,0:T(8,128)(2,1)S(1)}, u32[]{:S(2)}, u32[]{:S(2)}) %collective-permute-start.61) | collective-permute-done | bytes 393248 | tf_op jit(solution)/shard_map/ppermute | solution.py:41
  534.4 6.2 collective-permute-done.62
  540.9 7.2 %collective-permute-done.55 = bf16[64,768]{1,0:T(8,128)(2,1)S(1)} collective-permute-done((bf16[64,768]{1,0:T(8,128)(2,1)S(1)}, bf16[64,768]{1,0:T(8,128)(2,1)S(1)}, u32[]{:S(2)}, u32[]{:S(2)}) %collective-permute-start.55) | collective-permute-done | bytes 98336 | tf_op jit(solution)/shard_map/ppermute | solution.py:41
  548.2 6.6 collective-permute-done.63
  554.8 6.4 collective-permute-done.56
  561.2 6.4 collective-permute-done.64
  567.6 6.4 collective-permute-done.57
  584.1 18.5 %collective-permute-done.98 = bf16[2,2,192,512]{3,2,1,0:T(8,128)(2,1)S(1)} collective-permute-done((bf16[2,2,192,512]{3,2,1,0:T(8,128)(2,1)S(1)}, bf16[2,2,192,512]{3,2,1,0:T(8,128)(2,1)S(1)}, u32[]{:S(2)}, u32[]{:S(2)}) %collective-permute-start.98) | collective-permute-done | bytes 786464 | tf_op jit(solution)/shard_map/ppermute | solution.py:41
  604.2 25.2 %collective-permute-done.92 = bf16[64,1536]{1,0:T(8,128)(2,1)S(1)} collective-permute-done((bf16[64,1536]{1,0:T(8,128)(2,1)S(1)}, bf16[64,1536]{1,0:T(8,128)(2,1)S(1)}, u32[]{:S(2)}, u32[]{:S(2)}) %collective-permute-start.92) | collective-permute-done | bytes 196640 | tf_op jit(solution)/shard_map/ppermute | solution.py:41
  633.2 5.8 collective-permute-done.93
  643.3 4.4 collective-permute-done.94
  651.0 18.9 %collective-permute-done.100 = bf16[2,2,192,512]{3,2,1,0:T(8,128)(2,1)S(1)} collective-permute-done((bf16[2,2,192,512]{3,2,1,0:T(8,128)(2,1)S(1)}, bf16[2,2,192,512]{3,2,1,0:T(8,128)(2,1)S(1)}, u32[]{:S(2)}, u32[]{:S(2)}) %collective-permute-start.100) | collective-permute-done | bytes 786464 | tf_op jit(solution)/shard_map/ppermute | solution.py:41
  671.6 9.3 %collective-permute-done.101 = bf16[2,192,512]{2,1,0:T(8,128)(2,1)S(1)} collective-permute-done((bf16[2,192,512]{2,1,0:T(8,128)(2,1)S(1)}, bf16[2,192,512]{2,1,0:T(8,128)(2,1)S(1)}, u32[]{:S(2)}, u32[]{:S(2)}) %collective-permute-start.101) | collective-permute-done | bytes 393248 | tf_op jit(solution)/shard_map/ppermute | solution.py:41
  682.4 4.5 collective-permute-done.102
  (536 shorter events, 245.6 us)
Async XLA Ops:
  0.8 43.6 %collective-permute-start.26 = (bf16[32,3072]{1,0:T(8,128)(2,1)}, bf16[32,3072]{1,0:T(8,128)(2,1)S(1)}, u32[]{:S(2)}, u32[]{:S(2)}) collective-permute-start(bf16[32,3072]{1,0:T(8,128)(2,1)} %param.26), channel_id=1, source_target_pairs={{0,8},{4,12},{8,16},{12,20},{16,24},{20,28},{24,0},{28,4},{1,9},{5... | collective-permute-start | bytes 589832 | tf_op jit(solution)/shard_map/ppermute | solution.py:41
  3.8 45.6 %collective-permute-start.32 = (bf16[32,3072]{1,0:T(8,128)(2,1)}, bf16[32,3072]{1,0:T(8,128)(2,1)S(1)}, u32[]{:S(2)}, u32[]{:S(2)}) collective-permute-start(bf16[32,3072]{1,0:T(8,128)(2,1)} %param.27), channel_id=1, source_target_pairs={{0,8},{4,12},{8,16},{12,20},{16,24},{20,28},{24,0},{28,4},{1,9},{5... | collective-permute-start | bytes 589832 | tf_op jit(solution)/shard_map/ppermute | solution.py:41
  5.4 34.4 %collective-permute-start.20 = (bf16[48,1024]{1,0:T(8,128)(2,1)}, bf16[48,1024]{1,0:T(8,128)(2,1)}, u32[]{:S(2)}, u32[]{:S(2)}) collective-permute-start(bf16[48,1024]{1,0:T(8,128)(2,1)} %param.24), channel_id=1, source_target_pairs={{0,8},{4,12},{8,16},{12,20},{16,24},{20,28},{24,0},{28,4},{1,9},{5... | collective-permute-start | bytes 294920 | tf_op jit(solution)/shard_map/ppermute | solution.py:41
  7.0 29.4 %collective-permute-start.6 = (bf16[32,1536]{1,0:T(8,128)(2,1)}, bf16[32,1536]{1,0:T(8,128)(2,1)}, u32[]{:S(2)}, u32[]{:S(2)}) collective-permute-start(bf16[32,1536]{1,0:T(8,128)(2,1)} %param.18), channel_id=1, source_target_pairs={{0,8},{4,12},{8,16},{12,20},{16,24},{20,28},{24,0},{28,4},{1,9},{5... | collective-permute-start | bytes 294920 | tf_op jit(solution)/shard_map/ppermute | solution.py:41
  49.4 44.7 %collective-permute-start.39 = (bf16[2,96,1024]{2,1,0:T(8,128)(2,1)S(1)}, bf16[2,96,1024]{2,1,0:T(8,128)(2,1)S(1)}, u32[]{:S(2)}, u32[]{:S(2)}) collective-permute-start(bf16[2,96,1024]{2,1,0:T(8,128)(2,1)S(1)} %pad_maximum_fusion.25), channel_id=1, source_target_pairs={{0,2},{1,3},{2,0},{3,1},{4,6},{5,7},{6,4},{7,5},{8,10},{9,11},{10,... | collective-permute-start | bytes 1179656 | tf_op jit(solution)/shard_map/ppermute | solution.py:41
  51.1 24.4 %collective-permute-start.27 = (bf16[32,3072]{1,0:T(8,128)(2,1)S(1)}, bf16[32,3072]{1,0:T(8,128)(2,1)S(1)}, u32[]{:S(2)}, u32[]{:S(2)}) collective-permute-start(bf16[32,3072]{1,0:T(8,128)(2,1)S(1)} %collective-permute-done.26), channel_id=1, source_target_pairs={{0,8},{4,12},{8,16},{12,20},{16,24},{20,28},{24,0},{28,4},{1,9},{5... | collective-permute-start | bytes 589832 | tf_op jit(solution)/shard_map/ppermute | solution.py:41
  54.7 23.1 %collective-permute-start.33 = (bf16[32,3072]{1,0:T(8,128)(2,1)S(1)}, bf16[32,3072]{1,0:T(8,128)(2,1)S(1)}, u32[]{:S(2)}, u32[]{:S(2)}) collective-permute-start(bf16[32,3072]{1,0:T(8,128)(2,1)S(1)} %collective-permute-done.32), channel_id=1, source_target_pairs={{0,8},{4,12},{8,16},{12,20},{16,24},{20,28},{24,0},{28,4},{1,9},{5... | collective-permute-start | bytes 589832 | tf_op jit(solution)/shard_map/ppermute | solution.py:41
  71.2 29.0 %collective-permute-start.23 = (bf16[4,48,1024]{2,1,0:T(8,128)(2,1)S(1)}, bf16[4,48,1024]{2,1,0:T(8,128)(2,1)S(1)}, u32[]{:S(2)}, u32[]{:S(2)}) collective-permute-start(bf16[4,48,1024]{2,1,0:T(8,128)(2,1)S(1)} %bitcast_dynamic-update-slice_fusion.12), channel_id=1, source_target_pairs={{0,2},{1,3},{2,0},{3,1},{4,6},{5,7},{6,4},{7,5},{8,10},{9,11},{10,... | collective-permute-start | bytes 1179656 | tf_op jit(solution)/shard_map/ppermute | solution.py:41
  75.5 25.7 %collective-permute-start.9 = (bf16[4,32,1536]{2,1,0:T(8,128)(2,1)}, bf16[4,32,1536]{2,1,0:T(8,128)(2,1)S(1)}, u32[]{:S(2)}, u32[]{:S(2)}) collective-permute-start(bf16[4,32,1536]{2,1,0:T(8,128)(2,1)} %bitcast_dynamic-update-slice_fusion.20), channel_id=1, source_target_pairs={{0,4},{4,0},{8,12},{12,8},{16,20},{20,16},{24,28},{28,24},{1,5},{5... | collective-permute-start | bytes 1179656 | tf_op jit(solution)/shard_map/ppermute | solution.py:41
  77.8 24.9 %collective-permute-start.15 = (bf16[4,32,1536]{2,1,0:T(8,128)(2,1)}, bf16[4,32,1536]{2,1,0:T(8,128)(2,1)S(1)}, u32[]{:S(2)}, u32[]{:S(2)}) collective-permute-start(bf16[4,32,1536]{2,1,0:T(8,128)(2,1)} %bitcast_dynamic-update-slice_fusion.16), channel_id=1, source_target_pairs={{0,2},{1,3},{2,0},{3,1},{4,6},{5,7},{6,4},{7,5},{8,10},{9,11},{10,... | collective-permute-start | bytes 1179656 | tf_op jit(solution)/shard_map/ppermute | solution.py:41
  94.1 22.1 %collective-permute-start.29 = (bf16[4,32,3072]{2,1,0:T(8,128)(2,1)}, bf16[4,32,3072]{2,1,0:T(8,128)(2,1)}, u32[]{:S(2)}, u32[]{:S(2)}) collective-permute-start(bf16[4,32,3072]{2,1,0:T(8,128)(2,1)} %bitcast_dynamic-update-slice_fusion.8), channel_id=1, source_target_pairs={{0,2},{1,3},{2,0},{3,1},{4,6},{5,7},{6,4},{7,5},{8,10},{9,11},{10,... | collective-permute-start | bytes 2359304 | tf_op jit(solution)/shard_map/ppermute | solution.py:41
  100.2 23.8 %collective-permute-start.40 = (bf16[2,2,96,1024]{3,2,1,0:T(8,128)(2,1)}, bf16[2,2,96,1024]{3,2,1,0:T(8,128)(2,1)}, u32[]{:S(2)}, u32[]{:S(2)}) collective-permute-start(bf16[2,2,96,1024]{3,2,1,0:T(8,128)(2,1)} %pad_maximum_fusion.23), channel_id=1, source_target_pairs={{0,8},{4,12},{8,16},{12,20},{16,24},{20,28},{24,0},{28,4},{1,9},{5... | collective-permute-start | bytes 2359304 | tf_op jit(solution)/shard_map/ppermute | solution.py:41
  101.2 20.7 %collective-permute-start.35 = (bf16[4,32,3072]{2,1,0:T(8,128)(2,1)}, bf16[4,32,3072]{2,1,0:T(8,128)(2,1)}, u32[]{:S(2)}, u32[]{:S(2)}) collective-permute-start(bf16[4,32,3072]{2,1,0:T(8,128)(2,1)} %bitcast_dynamic-update-slice_fusion.4), channel_id=1, source_target_pairs={{0,4},{4,0},{8,12},{12,8},{16,20},{20,16},{24,28},{28,24},{1,5},{5... | collective-permute-start | bytes 2359304 | tf_op jit(solution)/shard_map/ppermute | solution.py:41
  102.7 36.1 %collective-permute-start.24 = (bf16[4,2,48,1024]{3,2,1,0:T(8,128)(2,1)}, bf16[4,2,48,1024]{3,2,1,0:T(8,128)(2,1)}, u32[]{:S(2)}, u32[]{:S(2)}) collective-permute-start(bf16[4,2,48,1024]{3,2,1,0:T(8,128)(2,1)} %pad_maximum_fusion.22), channel_id=1, source_target_pairs={{0,4},{4,0},{8,12},{12,8},{16,20},{20,16},{24,28},{28,24},{1,5},{5... | collective-permute-start | bytes 2359304 | tf_op jit(solution)/shard_map/ppermute | solution.py:41
  107.3 32.8 %collective-permute-start.10 = (bf16[4,2,32,1536]{3,2,0,1:T(8,128)(2,1)}, bf16[4,2,32,1536]{3,2,0,1:T(8,128)(2,1)}, u32[]{:S(2)}, u32[]{:S(2)}) collective-permute-start(bf16[4,2,32,1536]{3,2,0,1:T(8,128)(2,1)} %pad_maximum_fusion.20), channel_id=1, source_target_pairs={{0,2},{1,3},{2,0},{3,1},{4,6},{5,7},{6,4},{7,5},{8,10},{9,11},{10,... | collective-permute-start | bytes 2359304 | tf_op jit(solution)/shard_map/ppermute | solution.py:41
  116.4 39.1 %collective-permute-start.16 = (bf16[4,2,32,1536]{3,2,1,0:T(8,128)(2,1)S(1)}, bf16[4,2,32,1536]{3,2,1,0:T(8,128)(2,1)S(1)}, u32[]{:S(2)}, u32[]{:S(2)}) collective-permute-start(bf16[4,2,32,1536]{3,2,1,0:T(8,128)(2,1)S(1)} %copy-done.32), channel_id=1, source_target_pairs={{0,4},{4,0},{8,12},{12,8},{16,20},{20,16},{24,28},{28,24},{1,5},{5... | collective-permute-start | bytes 2359304 | tf_op jit(solution)/shard_map/ppermute | solution.py:41
  121.9 66.6 %collective-permute-start.30 = (bf16[4,2,32,3072]{3,2,0,1:T(8,128)(2,1)S(1)}, bf16[4,2,32,3072]{3,2,0,1:T(8,128)(2,1)S(1)}, u32[]{:S(2)}, u32[]{:S(2)}) collective-permute-start(bf16[4,2,32,3072]{3,2,0,1:T(8,128)(2,1)S(1)} %pad_maximum_fusion.13), channel_id=1, source_target_pairs={{0,4},{4,0},{8,12},{12,8},{16,20},{20,16},{24,28},{28,24},{1,5},{5... | collective-permute-start | bytes 4718600 | tf_op jit(solution)/shard_map/ppermute | solution.py:41
  124.0 67.0 %collective-permute-start.36 = (bf16[4,2,32,3072]{3,2,1,0:T(8,128)(2,1)S(1)}, bf16[4,2,32,3072]{3,2,1,0:T(8,128)(2,1)S(1)}, u32[]{:S(2)}, u32[]{:S(2)}) collective-permute-start(bf16[4,2,32,3072]{3,2,1,0:T(8,128)(2,1)S(1)} %pad_maximum_fusion.14), channel_id=1, source_target_pairs={{0,2},{1,3},{2,0},{3,1},{4,6},{5,7},{6,4},{7,5},{8,10},{9,11},{10,... | collective-permute-start | bytes 4718600 | tf_op jit(solution)/shard_map/ppermute | solution.py:41
  138.8 20.2 %collective-permute-start.41 = (bf16[2,2,96,1024]{3,2,1,0:T(8,128)(2,1)}, bf16[2,2,96,1024]{3,2,1,0:T(8,128)(2,1)S(1)}, u32[]{:S(2)}, u32[]{:S(2)}) collective-permute-start(bf16[2,2,96,1024]{3,2,1,0:T(8,128)(2,1)} %collective-permute-done.40), channel_id=1, source_target_pairs={{0,8},{4,12},{8,16},{12,20},{16,24},{20,28},{24,0},{28,4},{1,9},{5... | collective-permute-start | bytes 2359304 | tf_op jit(solution)/shard_map/ppermute | solution.py:41
  140.2 59.7 %collective-permute-start.25 = (bf16[4,2,2,48,1024]{4,3,2,1,0:T(8,128)(2,1)S(1)}, bf16[4,2,2,48,1024]{4,3,2,1,0:T(8,128)(2,1)S(1)}, u32[]{:S(2)}, u32[]{:S(2)}) collective-permute-start(bf16[4,2,2,48,1024]{4,3,2,1,0:T(8,128)(2,1)S(1)} %pad_maximum_fusion.12), channel_id=1, source_target_pairs={{0,1},{1,0},{2,3},{3,2},{4,5},{5,4},{6,7},{7,6},{8,9},{9,8},{10,11... | collective-permute-start | bytes 4718600 | tf_op jit(solution)/shard_map/ppermute | solution.py:41
  155.5 40.8 %collective-permute-start.11 = (bf16[4,2,2,32,1536]{4,3,2,1,0:T(8,128)(2,1)S(1)}, bf16[4,2,2,32,1536]{4,3,2,1,0:T(8,128)(2,1)S(1)}, u32[]{:S(2)}, u32[]{:S(2)}) collective-permute-start(bf16[4,2,2,32,1536]{4,3,2,1,0:T(8,128)(2,1)S(1)} %copy.131), channel_id=1, source_target_pairs={{0,1},{1,0},{2,3},{3,2},{4,5},{5,4},{6,7},{7,6},{8,9},{9,8},{10,11... | collective-permute-start | bytes 4718600 | tf_op jit(solution)/shard_map/ppermute | solution.py:41
  188.5 50.2 %collective-permute-start.43 = (bf16[4,2,2,96,1024]{4,3,2,1,0:T(8,128)(2,1)}, bf16[4,2,2,96,1024]{4,3,2,1,0:T(8,128)(2,1)}, u32[]{:S(2)}, u32[]{:S(2)}) collective-permute-start(bf16[4,2,2,96,1024]{4,3,2,1,0:T(8,128)(2,1)} %bitcast_dynamic-update-slice_fusion), channel_id=1, source_target_pairs={{0,1},{1,0},{2,3},{3,2},{4,5},{5,4},{6,7},{7,6},{8,9},{9,8},{10,11... | collective-permute-start | bytes 9437192 | tf_op jit(solution)/shard_map/ppermute | solution.py:41
  191.0 75.1 %collective-permute-start.31 = (bf16[4,2,2,32,3072]{4,3,2,1,0:T(8,128)(2,1)}, bf16[4,2,2,32,3072]{4,3,2,1,0:T(8,128)(2,1)}, u32[]{:S(2)}, u32[]{:S(2)}) collective-permute-start(bf16[4,2,2,32,3072]{4,3,2,1,0:T(8,128)(2,1)} %copy.132), channel_id=1, source_target_pairs={{0,1},{1,0},{2,3},{3,2},{4,5},{5,4},{6,7},{7,6},{8,9},{9,8},{10,11... | collective-permute-start | bytes 9437192 | tf_op jit(solution)/shard_map/ppermute | solution.py:41
  193.6 63.5 %collective-permute-start.37 = (bf16[4,2,2,32,3072]{4,3,2,1,0:T(8,128)(2,1)}, bf16[4,2,2,32,3072]{4,3,2,1,0:T(8,128)(2,1)}, u32[]{:S(2)}, u32[]{:S(2)}) collective-permute-start(bf16[4,2,2,32,3072]{4,3,2,1,0:T(8,128)(2,1)} %pad_maximum_fusion.7), channel_id=1, source_target_pairs={{0,1},{1,0},{2,3},{3,2},{4,5},{5,4},{6,7},{7,6},{8,9},{9,8},{10,11... | collective-permute-start | bytes 9437192 | tf_op jit(solution)/shard_map/ppermute | solution.py:41
  232.6 192.9 %collective-permute-start.73 = (bf16[512,1536]{1,0:T(8,128)(2,1)}, bf16[512,1536]{1,0:T(8,128)(2,1)}, u32[]{:S(2)}, u32[]{:S(2)}) collective-permute-start(bf16[512,1536]{1,0:T(8,128)(2,1)} %get-tuple-element.42), channel_id=1, source_target_pairs={{0,1},{1,0},{2,3},{3,2},{4,5},{5,4},{6,7},{7,6},{8,9},{9,8},{10,11... | collective-permute-start | bytes 4718600 | tf_op jit(solution)/shard_map/ppermute | solution.py:41
  313.0 141.7 %collective-permute-start.89 = (bf16[512,1536]{1,0:T(8,128)(2,1)}, bf16[512,1536]{1,0:T(8,128)(2,1)}, u32[]{:S(2)}, u32[]{:S(2)}) collective-permute-start(bf16[512,1536]{1,0:T(8,128)(2,1)} %get-tuple-element.54), channel_id=1, source_target_pairs={{0,1},{1,0},{2,3},{3,2},{4,5},{5,4},{6,7},{7,6},{8,9},{9,8},{10,11... | collective-permute-start | bytes 4718600 | tf_op jit(solution)/shard_map/ppermute | solution.py:41
  313.2 112.9 %collective-permute-start.74 = (bf16[512,512]{1,0:T(8,128)(2,1)}, bf16[512,512]{1,0:T(8,128)(2,1)}, u32[]{:S(2)}, u32[]{:S(2)}) collective-permute-start(bf16[512,512]{1,0:T(8,128)(2,1)} %get-tuple-element.85), channel_id=1, source_target_pairs={{0,1},{1,0},{2,3},{3,2},{4,5},{5,4},{6,7},{7,6},{8,9},{9,8},{10,11... | collective-permute-start | bytes 1572872 | tf_op jit(solution)/shard_map/ppermute | solution.py:41
  353.5 44.3 %collective-permute-start.66 = (bf16[1536,128]{1,0:T(8,128)(2,1)}, bf16[1536,128]{1,0:T(8,128)(2,1)}, u32[]{:S(2)}, u32[]{:S(2)}) collective-permute-start(bf16[1536,128]{1,0:T(8,128)(2,1)} %select_convert_fusion), channel_id=1, source_target_pairs={{0,1},{1,0},{2,3},{3,2},{4,5},{5,4},{6,7},{7,6},{8,9},{9,8},{10,11... | collective-permute-start | bytes 1179656 | tf_op jit(solution)/shard_map/ppermute | solution.py:41
  397.7 39.0 %collective-permute-start.52 = (bf16[512,768]{1,0:T(8,128)(2,1)}, bf16[512,768]{1,0:T(8,128)(2,1)}, u32[]{:S(2)}, u32[]{:S(2)}) collective-permute-start(bf16[512,768]{1,0:T(8,128)(2,1)} %get-tuple-element.70), channel_id=1, source_target_pairs={{0,1},{1,0},{2,3},{3,2},{4,5},{5,4},{6,7},{7,6},{8,9},{9,8},{10,11... | collective-permute-start | bytes 2359304 | tf_op jit(solution)/shard_map/ppermute | solution.py:41
  433.2 21.0 %collective-permute-start.81 = (bf16[512,1024]{1,0:T(8,128)(2,1)S(1)}, bf16[512,1024]{1,0:T(8,128)(2,1)S(1)}, u32[]{:S(2)}, u32[]{:S(2)}) collective-permute-start(bf16[512,1024]{1,0:T(8,128)(2,1)S(1)} %copy-done.31), channel_id=1, source_target_pairs={{0,1},{1,0},{2,3},{3,2},{4,5},{5,4},{6,7},{7,6},{8,9},{9,8},{10,11... | collective-permute-start | bytes 3145736 | tf_op jit(solution)/shard_map/ppermute | solution.py:41
  434.0 27.4 %collective-permute-start.82 = (bf16[512,1536]{1,0:T(8,128)(2,1)S(1)}, bf16[512,1536]{1,0:T(8,128)(2,1)S(1)}, u32[]{:S(2)}, u32[]{:S(2)}) collective-permute-start(bf16[512,1536]{1,0:T(8,128)(2,1)S(1)} %copy-done.29), channel_id=1, source_target_pairs={{0,1},{1,0},{2,3},{3,2},{4,5},{5,4},{6,7},{7,6},{8,9},{9,8},{10,11... | collective-permute-start | bytes 4718600 | tf_op jit(solution)/shard_map/ppermute | solution.py:41
  436.7 140.6 %collective-permute-start.97 = (bf16[512,512]{1,0:T(8,128)(2,1)S(1)}, bf16[512,512]{1,0:T(8,128)(2,1)S(1)}, u32[]{:S(2)}, u32[]{:S(2)}) collective-permute-start(bf16[512,512]{1,0:T(8,128)(2,1)S(1)} %copy-done.35), channel_id=1, source_target_pairs={{0,1},{1,0},{2,3},{3,2},{4,5},{5,4},{6,7},{7,6},{8,9},{9,8},{10,11... | collective-permute-start | bytes 1572872 | tf_op jit(solution)/shard_map/ppermute | solution.py:41
  453.9 123.4 %collective-permute-start.96 = (bf16[512,3072]{1,0:T(8,128)(2,1)S(1)}, bf16[512,3072]{1,0:T(8,128)(2,1)S(1)}, u32[]{:S(2)}, u32[]{:S(2)}) collective-permute-start(bf16[512,3072]{1,0:T(8,128)(2,1)S(1)} %copy-done.50), channel_id=1, source_target_pairs={{0,1},{1,0},{2,3},{3,2},{4,5},{5,4},{6,7},{7,6},{8,9},{9,8},{10,11... | collective-permute-start | bytes 9437192 | tf_op jit(solution)/shard_map/ppermute | solution.py:41
  454.2 36.6 %collective-permute-start.60 = (bf16[4,2,64,768]{3,2,1,0:T(8,128)(2,1)S(1)}, bf16[4,2,64,768]{3,2,1,0:T(8,128)(2,1)S(1)}, u32[]{:S(2)}, u32[]{:S(2)}) collective-permute-start(bf16[4,2,64,768]{3,2,1,0:T(8,128)(2,1)S(1)} %dynamic-slice_bitcast_fusion.6), channel_id=1, source_target_pairs={{0,4},{4,0},{8,12},{12,8},{16,20},{20,16},{24,28},{28,24},{1,5},{5... | collective-permute-start | bytes 2359304 | tf_op jit(solution)/shard_map/ppermute | solution.py:41
  454.7 43.3 %collective-permute-start.53 = (bf16[4,2,64,768]{3,2,1,0:T(8,128)(2,1)S(1)}, bf16[4,2,64,768]{3,2,1,0:T(8,128)(2,1)S(1)}, u32[]{:S(2)}, u32[]{:S(2)}) collective-permute-start(bf16[4,2,64,768]{3,2,1,0:T(8,128)(2,1)S(1)} %dynamic-slice_bitcast_fusion.7), channel_id=1, source_target_pairs={{0,2},{1,3},{2,0},{3,1},{4,6},{5,7},{6,4},{7,5},{8,10},{9,11},{10,... | collective-permute-start | bytes 2359304 | tf_op jit(solution)/shard_map/ppermute | solution.py:41
  461.4 21.4 %collective-permute-start.76 = (bf16[4,96,512]{2,1,0:T(8,128)(2,1)S(1)}, bf16[4,96,512]{2,1,0:T(8,128)(2,1)S(1)}, u32[]{:S(2)}, u32[]{:S(2)}) collective-permute-start(bf16[4,96,512]{2,1,0:T(8,128)(2,1)S(1)} %dynamic-slice_bitcast_fusion.9), channel_id=1, source_target_pairs={{0,2},{1,3},{2,0},{3,1},{4,6},{5,7},{6,4},{7,5},{8,10},{9,11},{10,... | collective-permute-start | bytes 1179656 | tf_op jit(solution)/shard_map/ppermute | solution.py:41
  489.4 91.8 %collective-permute-start.90 = (bf16[4,2,64,1536]{3,2,1,0:T(8,128)(2,1)S(1)}, bf16[4,2,64,1536]{3,2,1,0:T(8,128)(2,1)S(1)}, u32[]{:S(2)}, u32[]{:S(2)}) collective-permute-start(bf16[4,2,64,1536]{3,2,1,0:T(8,128)(2,1)S(1)} %dynamic-slice_bitcast_fusion), channel_id=1, source_target_pairs={{0,2},{1,3},{2,0},{3,1},{4,6},{5,7},{6,4},{7,5},{8,10},{9,11},{10,... | collective-permute-start | bytes 4718600 | tf_op jit(solution)/shard_map/ppermute | solution.py:41
  497.3 35.1 %collective-permute-start.61 = (bf16[4,64,768]{2,1,0:T(8,128)(2,1)S(1)}, bf16[4,64,768]{2,1,0:T(8,128)(2,1)S(1)}, u32[]{:S(2)}, u32[]{:S(2)}) collective-permute-start(bf16[4,64,768]{2,1,0:T(8,128)(2,1)S(1)} %dynamic-slice_bitcast_fusion.10), channel_id=1, source_target_pairs={{0,2},{1,3},{2,0},{3,1},{4,6},{5,7},{6,4},{7,5},{8,10},{9,11},{10,... | collective-permute-start | bytes 1179656 | tf_op jit(solution)/shard_map/ppermute | solution.py:41
  505.9 28.3 %collective-permute-start.54 = (bf16[4,64,768]{2,1,0:T(8,128)(2,1)S(1)}, bf16[4,64,768]{2,1,0:T(8,128)(2,1)S(1)}, u32[]{:S(2)}, u32[]{:S(2)}) collective-permute-start(bf16[4,64,768]{2,1,0:T(8,128)(2,1)S(1)} %dynamic-slice_bitcast_fusion.11), channel_id=1, source_target_pairs={{0,4},{4,0},{8,12},{12,8},{16,20},{20,16},{24,28},{28,24},{1,5},{5... | collective-permute-start | bytes 1179656 | tf_op jit(solution)/shard_map/ppermute | solution.py:41
  532.4 49.8 %collective-permute-start.83 = (bf16[4,2,64,1536]{3,2,1,0:T(8,128)(2,1)S(1)}, bf16[4,2,64,1536]{3,2,1,0:T(8,128)(2,1)S(1)}, u32[]{:S(2)}, u32[]{:S(2)}) collective-permute-start(bf16[4,2,64,1536]{3,2,1,0:T(8,128)(2,1)S(1)} %dynamic-slice_bitcast_fusion.1), channel_id=1, source_target_pairs={{0,4},{4,0},{8,12},{12,8},{16,20},{20,16},{24,28},{28,24},{1,5},{5... | collective-permute-start | bytes 4718600 | tf_op jit(solution)/shard_map/ppermute | solution.py:41
  581.2 21.4 %collective-permute-start.98 = (bf16[2,2,192,512]{3,2,1,0:T(8,128)(2,1)S(1)}, bf16[2,2,192,512]{3,2,1,0:T(8,128)(2,1)S(1)}, u32[]{:S(2)}, u32[]{:S(2)}) collective-permute-start(bf16[2,2,192,512]{3,2,1,0:T(8,128)(2,1)S(1)} %dynamic-slice_bitcast_fusion.2), channel_id=1, source_target_pairs={{0,8},{4,12},{8,16},{12,20},{16,24},{20,28},{24,0},{28,4},{1,9},{5... | collective-permute-start | bytes 2359304 | tf_op jit(solution)/shard_map/ppermute | solution.py:41
  581.7 21.2 %collective-permute-start.91 = (bf16[4,64,1536]{2,1,0:T(8,128)(2,1)S(1)}, bf16[4,64,1536]{2,1,0:T(8,128)(2,1)S(1)}, u32[]{:S(2)}, u32[]{:S(2)}) collective-permute-start(bf16[4,64,1536]{2,1,0:T(8,128)(2,1)S(1)} %dynamic-slice_bitcast_fusion.3), channel_id=1, source_target_pairs={{0,4},{4,0},{8,12},{12,8},{16,20},{20,16},{24,28},{28,24},{1,5},{5... | collective-permute-start | bytes 2359304 | tf_op jit(solution)/shard_map/ppermute | solution.py:41
  582.7 20.5 %collective-permute-start.84 = (bf16[4,64,1536]{2,1,0:T(8,128)(2,1)S(1)}, bf16[4,64,1536]{2,1,0:T(8,128)(2,1)S(1)}, u32[]{:S(2)}, u32[]{:S(2)}) collective-permute-start(bf16[4,64,1536]{2,1,0:T(8,128)(2,1)S(1)} %dynamic-slice_bitcast_fusion.4), channel_id=1, source_target_pairs={{0,2},{1,3},{2,0},{3,1},{4,6},{5,7},{6,4},{7,5},{8,10},{9,11},{10,... | collective-permute-start | bytes 2359304 | tf_op jit(solution)/shard_map/ppermute | solution.py:41
  602.8 45.0 %collective-permute-start.99 = (bf16[2,2,192,512]{3,2,1,0:T(8,128)(2,1)S(1)}, bf16[2,2,192,512]{3,2,1,0:T(8,128)(2,1)S(1)}, u32[]{:S(2)}, u32[]{:S(2)}) collective-permute-start(bf16[2,2,192,512]{3,2,1,0:T(8,128)(2,1)S(1)} %fusion.55), channel_id=1, source_target_pairs={{0,8},{4,12},{8,16},{12,20},{16,24},{20,28},{24,0},{28,4},{1,9},{5... | collective-permute-start | bytes 2359304 | tf_op jit(solution)/shard_map/ppermute | solution.py:41
  603.1 26.2 %collective-permute-start.92 = (bf16[64,1536]{1,0:T(8,128)(2,1)S(1)}, bf16[64,1536]{1,0:T(8,128)(2,1)S(1)}, u32[]{:S(2)}, u32[]{:S(2)}) collective-permute-start(bf16[64,1536]{1,0:T(8,128)(2,1)S(1)} %dynamic-slice_bitcast_fusion.15), channel_id=1, source_target_pairs={{0,8},{4,12},{8,16},{12,20},{16,24},{20,28},{24,0},{28,4},{1,9},{5... | collective-permute-start | bytes 589832 | tf_op jit(solution)/shard_map/ppermute | solution.py:41
  603.5 29.6 %collective-permute-start.85 = (bf16[64,1536]{1,0:T(8,128)(2,1)S(1)}, bf16[64,1536]{1,0:T(8,128)(2,1)S(1)}, u32[]{:S(2)}, u32[]{:S(2)}) collective-permute-start(bf16[64,1536]{1,0:T(8,128)(2,1)S(1)} %dynamic-slice_bitcast_fusion.17), channel_id=1, source_target_pairs={{0,8},{4,12},{8,16},{12,20},{16,24},{20,28},{24,0},{28,4},{1,9},{5... | collective-permute-start | bytes 589832 | tf_op jit(solution)/shard_map/ppermute | solution.py:41
  648.1 21.8 %collective-permute-start.100 = (bf16[2,2,192,512]{3,2,1,0:T(8,128)(2,1)S(1)}, bf16[2,2,192,512]{3,2,1,0:T(8,128)(2,1)S(1)}, u32[]{:S(2)}, u32[]{:S(2)}) collective-permute-start(bf16[2,2,192,512]{3,2,1,0:T(8,128)(2,1)S(1)} %fusion.54), channel_id=1, source_target_pairs={{0,8},{4,12},{8,16},{12,20},{16,24},{20,28},{24,0},{28,4},{1,9},{5... | collective-permute-start | bytes 2359304 | tf_op jit(solution)/shard_map/ppermute | solution.py:41
  650.8 20.8 %collective-permute-start.88 = (f32[32,1536]{1,0:T(8,128)S(1)}, f32[32,1536]{1,0:T(8,128)S(1)}, u32[]{:S(2)}, u32[]{:S(2)}) collective-permute-start(f32[32,1536]{1,0:T(8,128)S(1)} %dynamic-slice_bitcast_fusion.16), channel_id=1, source_target_pairs={{0,1},{1,0},{2,3},{3,2},{4,5},{5,4},{6,7},{7,6},{8,9},{9,8},{10,11... | collective-permute-start | bytes 589832 | tf_op jit(solution)/shard_map/ppermute | solution.py:41
  (111 other events, 1061.1 us)

commit v2 on v1

--- a/solution.py
+++ b/solution.py
@@ -51,15 +51,40 @@
     return lax.ppermute(block, axis, route)
 
 
-def gather_rings(piece, order):
-    have = []
-    for which in order:
+def after(value, *others):
+    return lax.optimization_barrier((value, *others))[0]
+
+
+def hop(block, which, distance):
+    name, total, stride, count = grid_axes()[which]
+    route = []
+    for i in range(total):
+        k = (i // stride) % count
+        route.append((i, i + ((k + distance) % count - k) * stride))
+    return lax.ppermute(block, name, route)
+
+
+class Flight:
+    def done(self):
+        return not self.order
+
+
+class Gather(Flight):
+    def __init__(self, piece, order):
+        self.piece = piece
+        self.order = list(order)
+        self.have = []
+
+    def sends(self, which):
+        return [self.piece] * (grid_axes()[which][3] - 1)
+
+    def finish(self):
+        which = self.order.pop(0)
         count = grid_axes()[which][3]
         me = place_on(which)
-        spot = sum(1 for other in have if "zxyc".index(other) < "zxyc".index(which))
-        parts = [piece]
-        for _ in range(count - 1):
-            parts.append(ring_step(parts[-1], which))
+        spot = sum(1 for other in self.have if "zxyc".index(other) < "zxyc".index(which))
+        piece = self.piece
+        parts = [piece] + self.moved
         if count == 2:
             first = me == 0
             a, b = parts
@@ -71,34 +96,67 @@
                     stacked, part, lax.rem(me - t + count, count), spot
                 )
             piece = stacked
-        have.append(which)
-    return piece
-
-
-def scatter_rings(whole, order, left):
-    left = list(left)
-    wide = whole.dtype
-    for which in order:
+        self.have.append(which)
+        self.piece = piece
+
+
+class Scatter(Flight):
+    def __init__(self, whole, order, left="zxy"):
+        self.whole = whole
+        self.wide = whole.dtype
+        self.order = list(order)
+        self.left = list(left)
+
+    def own(self, ahead):
+        which = self.order[0]
         count = grid_axes()[which][3]
-        me = place_on(which)
-        spot = left.index(which)
-
-        def own(back):
-            return lax.dynamic_index_in_dim(whole, lax.rem(me - back + count, count), spot, False)
-
-        total = own(1)
-        for step in range(count - 1):
-            moved = ring_step(total.astype(wide), which)
-            total = moved.astype(f32) + own(step + 2).astype(f32)
-        left.remove(which)
-        whole = total if which == order[-1] else total.astype(wide)
-    return whole
-
-
-def rms_scale(values, norm_gain):
-    return (
-        values * lax.rsqrt(jnp.mean(values * values, axis=-1, keepdims=True) + epsilon) * norm_gain
-    )
+        return lax.dynamic_index_in_dim(
+            self.whole,
+            lax.rem(place_on(which) + ahead, count),
+            self.left.index(which),
+            False,
+        )
+
+    def sends(self, which):
+        return [self.own(d) for d in range(1, grid_axes()[which][3])]
+
+    def finish(self):
+        total = self.own(0).astype(f32)
+        for moved in self.moved:
+            total = total + moved.astype(f32)
+        self.left.remove(self.order.pop(0))
+        self.whole = total.astype(self.wide) if self.order else total
+
+
+def launch(value, *flights):
+    blocks = [f.sends(f.order[0]) for f in flights]
+    value, blocks = lax.optimization_barrier((value, blocks))
+    for f, sent in zip(flights, blocks):
+        which = f.order[0]
+        f.moved = [hop(block, which, d + 1) for d, block in enumerate(sent)]
+    return value
+
+
+def land(value, *flights):
+    value, landed = lax.optimization_barrier((value, [f.moved for f in flights]))
+    for f, moved in zip(flights, landed):
+        f.moved = moved
+        f.finish()
+    return value
+
+
+def tick(value, *flights):
+    value = land(value, *flights)
+    return launch(value, *[f for f in flights if not f.done()])
+
+
+def run_out(flight):
+    if not flight.done():
+        flight.finish()
+    while not flight.done():
+        launch(None, flight)
+        flight.finish()
+    return flight.whole
 
 
 def gelu_parts(v):
@@ -282,9 +340,6 @@
             return pl.BlockSpec((block, block), lambda h: (h, 0))
         return pl.BlockSpec((shape[0], block), lambda h: (0, h))
 
-    moved = sum(a.size * a.dtype.itemsize for a in ins) + sum(
-        o.size * o.dtype.itemsize for o in outs
-    )
     return pl.pallas_call(
         functools.partial(kernel, row_count),
         grid=(width // block,),
@@ -292,8 +347,135 @@
         out_specs=[spec(o.shape) for o in outs],
         out_shape=outs,
         compiler_params=pltpu.CompilerParams(vmem_limit_bytes=vmem_bytes),
-        cost_estimate=pl.CostEstimate(flops=flops, bytes_accessed=moved, transcendentals=0),
+        cost_estimate=pl.CostEstimate(flops=flops, bytes_accessed=1, transcendentals=0),
     )(*ins)
+
+
+def feature_call(kernel, core, grid, ins, in_specs, outs, out_specs, scratch=()):
+    return pl.pallas_call(
+        kernel,
+        grid_spec=pltpu.PrefetchScalarGridSpec(
+            num_scalar_prefetch=1,
+            grid=(grid,),
+            in_specs=in_specs,
+            out_specs=out_specs,
+            scratch_shapes=list(scratch),
+        ),
+        out_shape=outs,
+        compiler_params=pltpu.CompilerParams(vmem_limit_bytes=vmem_bytes),
+        cost_estimate=pl.CostEstimate(flops=1, bytes_accessed=1, transcendentals=0),
+    )(core, *ins)
+
+
+def whole_spec(shape):
+    return pl.BlockSpec(shape, lambda j, core: (0,) * len(shape))
+
+
+def mlp_kernel(core_ref, normed_ref, gate_w_ref, up_w_ref, act_ref, rise_ref, hidden_ref):
+    normed = normed_ref[...]
+    gate = jnp.dot(normed, gate_w_ref[...], preferred_element_type=f32)
+    up = jnp.dot(normed, up_w_ref[...], preferred_element_type=f32)
+    value, slope = gelu_parts(gate)
+    act_ref[...] = value
+    rise_ref[...] = up * slope
+    hidden_ref[...] = (value * up).astype(bf16)
+
+
+def down_kernel(core_ref, hidden_ref, down_ref, middle_ref, out_ref):
+    @pl.when(pl.program_id(0) == 0)
+    def _():
+        out_ref[...] = middle_ref[...]
+
+    out_ref[...] += jnp.dot(hidden_ref[...], down_ref[...], preferred_element_type=f32)
+
+
+def hidden_grad_kernel(
+    core_ref, grad_ref, down_ref, act_ref, rise_ref, gate_my, gate_other, up_my, up_other
+):
+    grad = lax.dot_general(
+        grad_ref[...], down_ref[...], (((1,), (1,)), ((), ())), preferred_element_type=f32
+    )
+    gate_low = (grad * rise_ref[...]).astype(bf16)
+    up_low = (grad * act_ref[...]).astype(bf16)
+    mine = pl.program_id(0) < pl.num_programs(0) // 2
+
+    @pl.when(mine)
+    def _():
+        gate_my[...] = gate_low
+        up_my[...] = up_low
+
+    @pl.when(jnp.logical_not(mine))
+    def _():
+        gate_other[...] = gate_low
+        up_other[...] = up_low
+
+
+def middle_kernel(
+    core_ref,
+    gate_my,
+    gate_other,
+    up_my,
+    up_other,
+    gate_w_ref,
+    up_w_ref,
+    middle_ref,
+    grad_ref,
+    gain_ref,
+    middle_grad_ref,
+    low_ref,
+    low_my,
+    low_other,
+    gain_grad_ref,
+    total,
+):
+    j = pl.program_id(0)
+    transposed = (((1,), (1,)), ((), ()))
+
+    @pl.when(j == 0)
+    def _():
+        total[...] = jnp.zeros_like(total)
+
+    def add(gate_ref, up_ref):
+        total[...] += lax.dot_general(
+            gate_ref[...], gate_w_ref[...], transposed, preferred_element_type=f32
+        ) + lax.dot_general(up_ref[...], up_w_ref[...], transposed, preferred_element_type=f32)
+
+    mine = j < pl.num_programs(0) // 2
+
+    @pl.when(mine)
+    def _():
+        add(gate_my, up_my)
+
+    @pl.when(jnp.logical_not(mine))
+    def _():
+        add(gate_other, up_other)
+
+    @pl.when(j == pl.num_programs(0) - 1)
+    def _():
+        middle = middle_ref[...]
+        scale = lax.rsqrt(jnp.mean(middle * middle, axis=-1, keepdims=True) + epsilon)
+        grad = total[...]
+        weighted = grad * gain_ref[...]
+        inner = jnp.mean(weighted * middle, axis=-1, keepdims=True)
+        back = scale * weighted - middle * (scale * scale * scale * inner)
+        middle_grad = grad_ref[...].astype(f32) + back
+        middle_grad_ref[...] = middle_grad
+        low = middle_grad.astype(bf16)
+        low_ref[...] = low
+        half = low.shape[1] // 2
+        first = core_ref[0] == 0
+
+        @pl.when(first)
+        def _():
+            low_my[...] = low[:, :half]
+            low_other[...] = low[:, half:]
+
+        @pl.when(jnp.logical_not(first))
+        def _():
+            low_my[...] = low[:, half:]
+            low_other[...] = low[:, :half]
+
+        gain_grad_ref[...] = jnp.sum(grad * middle * scale, axis=0, keepdims=True)
 
 
 def carry_before(factor, value, reverse):
@@ -338,30 +520,42 @@
     lru_piece = decay_param.shape[0]
 
     small = jnp.concatenate(
-        [norm_in_gain, norm_mid_gain, decay_param, conv_weight.reshape(-1)], axis=0
-    )
-    small_size = small.shape[0]
-    pair_width = 2 * block_width
-    small_rows = -(-small_size // pair_width)
-    small = jnp.pad(small, (0, small_rows * pair_width - small_size)).reshape(
-        small_rows, pair_width
-    )
-    gate_pair = jnp.concatenate([rec_gate_weight, input_gate_weight], axis=1)
-    pack = jnp.concatenate([gate_pair, small], axis=0)
-    pack_rows = pack.shape[0]
-    pack = jnp.pad(pack, ((0, -pack_rows % 16), (0, 0)))
-
-    full_signal = gather_rings(signal_in_weight, "zyxc").reshape(model_width, lru_width)
-    full_gate_in = gather_rings(gate_in_weight, "zxyc").reshape(model_width, lru_width)
-    full_pack = gather_rings(pack, "zyxc").reshape(device_count, pack.shape[0], pair_width)
-    full_branch = gather_rings(branch_out_weight, "zyxc").reshape(lru_width, model_width)
-    full_mlp_gate = gather_rings(mlp_gate_weight, "zyxc").reshape(model_width, ff_width)
-    full_mlp_up = gather_rings(mlp_up_weight, "zxyc").reshape(model_width, ff_width)
-    full_mlp_down = gather_rings(mlp_down_weight, "xyzc").reshape(ff_width, model_width)
-
-    gate_pairs = full_pack[:, :lru_piece].reshape(lru_width, pair_width)
-    full_rec, full_input = gate_pairs[:, :block_width], gate_pairs[:, block_width:]
-    smalls = full_pack[:, lru_piece : lru_piece + small_rows].reshape(device_count, -1).astype(f32)
+        [
+            rec_gate_weight.reshape(-1),
+            input_gate_weight.reshape(-1),
+            norm_in_gain,
+            norm_mid_gain,
+            decay_param,
+            conv_weight.reshape(-1),
+        ]
+    )
+    pack_width = -(-small.shape[0] // (model_piece * 128)) * 128
+    pack = jnp.pad(small, (0, model_piece * pack_width - small.shape[0]))
+    pack = pack.reshape(model_piece, pack_width)
+    everywhere = ("dp", "seq")
+    lru_half = lru_width // 2
+    mlp_pair = jnp.concatenate([mlp_gate_weight, mlp_up_weight], axis=1)
+    full_mlp = lax.all_gather(mlp_pair, everywhere, axis=0, tiled=True)
+    full_mlp_down = lax.all_gather(mlp_down_weight, everywhere, axis=0, tiled=True)
+    s1 = Gather(signal_in_weight[:, :lru_half], "zyxc")
+    s2 = Gather(jnp.concatenate([signal_in_weight[:, lru_half:], pack], axis=1), "zxyc")
+    launch(None, s1, s2)
+    tick(None, s1, s2)
+    gi = Gather(after(gate_in_weight, s1.piece), "zxyc")
+    br = Gather(after(branch_out_weight, s1.piece), "zyxc")
+    launch(None, gi, br)
+    tick(None, s1, s2)
+    tick(None, s1, s2, gi, br)
+    land(None, s1, s2)
+    smalls = s2.piece.reshape(model_width, -1)
+    full_signal = jnp.concatenate(
+        [s1.piece.reshape(model_width, -1), smalls[:, :lru_half]], axis=1
+    )
+    smalls = smalls[:, lru_half:].reshape(device_count, model_piece * pack_width)
+    gate_size = lru_piece * block_width
+    full_rec = smalls[:, :gate_size].reshape(lru_width, block_width)
+    full_input = smalls[:, gate_size : 2 * gate_size].reshape(lru_width, block_width)
+    smalls = smalls[:, 2 * gate_size :].astype(f32)
     gain_in = smalls[:, :model_piece].reshape(model_width)
     gain_mid = smalls[:, model_piece : 2 * model_piece].reshape(model_width)
     start = 2 * model_piece
@@ -375,11 +569,37 @@
     )
     rate = (-rate_scale * jax.nn.softplus(-decay_full))[None, :]
 
+    def other_half(a):
+        width = a.shape[1] // 2
+        return lax.dynamic_slice_in_dim(a, (1 - core) * width, width, 1)
+
+    def my_half(a):
+        width = a.shape[1] // 2
+        return lax.dynamic_slice_in_dim(a, core * width, width, 1)
+
+    def both_rows(a):
+        return jnp.concatenate([a, swap_cores(a)], axis=0)
+
+    def both_halves(a):
+        return jnp.concatenate([my_half(a), swap_cores(other_half(a))], axis=0)
+
+    out_grad = cotangent.reshape(token_count, model_width)
+
     inputs = tokens.astype(f32).reshape(token_count, model_width)
-    scale_in = lax.rsqrt(jnp.mean(inputs * inputs, axis=-1, keepdims=True) + epsilon)
+    tail_tokens = passed_along(tokens[:, row_tokens - halo_rows :], "seq", 1)
+
+    def norm_scale(values):
+        return lax.rsqrt(jnp.mean(values * values, axis=-1, keepdims=True) + epsilon)
+
+    scale_in = norm_scale(inputs)
     normed_in = (inputs * scale_in * gain_in).astype(bf16)
+    tail_rows = jnp.pad(tail_tokens.astype(f32), ((0, 0), (halo - halo_rows, 0), (0, 0)))
+    tail_rows = tail_rows.reshape(row_count * halo, model_width)
+    tail_normed = (tail_rows * norm_scale(tail_rows) * gain_in).astype(bf16)
+    before = (
+        jnp.dot(tail_normed, full_signal, preferred_element_type=f32).astype(bf16).astype(f32)
+    )
     signal = jnp.dot(normed_in, full_signal, preferred_element_type=f32).astype(bf16)
-    gate_pre = jnp.dot(normed_in, full_gate_in, preferred_element_type=f32)
     tail_ids = passed_along(segments[:, row_tokens - halo_rows :], "seq", 1)
     tail_ids = jnp.where(lax.axis_index("seq") == 0, jnp.int32(-1), tail_ids)
     ids_ext = jnp.concatenate([tail_ids, segments], axis=1)
@@ -392,16 +612,10 @@
     masks = jnp.broadcast_to(
         masks.reshape(halo_rows, token_count, 1), (halo_rows, token_count, block_width)
     )
-    tail_signal = passed_along(
-        signal.reshape(row_count, row_tokens, lru_width)[:, row_tokens - halo_rows :], "seq", 1
-    )
-    before = jnp.pad(
-        tail_signal.astype(f32), ((0, 0), (halo - halo_rows, 0), (0, 0))
-    ).reshape(row_count * halo, lru_width)
 
     wide_f32 = jax.ShapeDtypeStruct((token_count, lru_width), f32)
     wide_bf16 = jax.ShapeDtypeStruct((token_count, lru_width), bf16)
-    block_flops = 4 * token_count * lru_width * block_width
+    kernel_flops = 1
     conv_low, keep, cum_keep, local_state = channel_call(
         forward_kernel,
         row_count,
@@ -409,69 +623,188 @@
         [wide_bf16, wide_f32, wide_f32, wide_f32],
         lru_width,
         block_width,
-        block_flops,
+        kernel_flops,
     )
     cum3 = cum_keep.reshape(row_count, row_tokens, lru_width)
     local3 = local_state.reshape(row_count, row_tokens, lru_width)
     state_in = carry_before(cum3[:, -1], local3[:, -1], False)
+    state_in = tick(state_in, gi, br)
+    state_in = land(tick(state_in, gi, br), gi, br)
+    full_gate_in = gi.piece.reshape(model_width, lru_width)
+    gate_pre = jnp.dot(normed_in, full_gate_in, preferred_element_type=f32)
     states = (local3 + cum3 * state_in[:, None, :]).reshape(token_count, lru_width)
     mixed = (gelu_parts(gate_pre)[0] * states).astype(bf16)
+    full_branch = br.piece.reshape(lru_width, model_width)
     middle = inputs + jnp.dot(mixed, full_branch, preferred_element_type=f32)
-    scale_mid = lax.rsqrt(jnp.mean(middle * middle, axis=-1, keepdims=True) + epsilon)
+    scale_mid = norm_scale(middle)
     normed_mid = (middle * scale_mid * gain_mid).astype(bf16)
-    mlp_gate_pre = jnp.dot(normed_mid, full_mlp_gate, preferred_element_type=f32)
-    mlp_up_pre = jnp.dot(normed_mid, full_mlp_up, preferred_element_type=f32)
-    mlp_act, mlp_slope = gelu_parts(mlp_gate_pre)
-    hidden = (mlp_act * mlp_up_pre).astype(bf16)
-    block_out = middle + jnp.dot(hidden, full_mlp_down, preferred_element_type=f32)
-
-    out_grad = cotangent.reshape(token_count, model_width)
-
-    def other_half(a):
-        width = a.shape[1] // 2
-        return lax.dynamic_slice_in_dim(a, (1 - core) * width, width, 1)
-
-    def my_half(a):
-        width = a.shape[1] // 2
-        return lax.dynamic_slice_in_dim(a, core * width, width, 1)
-
-    def both_rows(a):
-        return jnp.concatenate([a, swap_cores(a)], axis=0)
-
-    def both_halves(a):
-        return jnp.concatenate([my_half(a), swap_cores(other_half(a))], axis=0)
-
-    def chip_grad(left_rows, right_half, order):
-        whole = lax.dot_general(
+    tile = 512
+    tiles = ff_width // tile
+    tokens_model = (token_count, model_width)
+    tokens_tile = (token_count, tile)
+    core_number = core.astype(jnp.int32).reshape(1)
+
+    def turned(j, core):
+        return lax.rem(j + core[0] * (tiles // 2), tiles)
+
+    def array(shape, kind):
+        return jax.ShapeDtypeStruct(shape, kind)
+
+    plain = pl.BlockSpec(tokens_tile, lambda j, core: (0, j))
+    mlp_act, mlp_rise, hidden = feature_call(
+        mlp_kernel,
+        core_number,
+        tiles,
+        [normed_mid, full_mlp, full_mlp],
+        [
+            whole_spec(tokens_model),
+            pl.BlockSpec((model_width, tile), lambda j, core: (0, j)),
+            pl.BlockSpec((model_width, tile), lambda j, core: (0, j + tiles)),
+        ],
+        [
+            array((token_count, ff_width), f32),
+            array((token_count, ff_width), f32),
+            array((token_count, ff_width), bf16),
+        ],
+        [plain, plain, plain],
+    )
+
+
+    def chip_grad(left_rows, right_half):
+        return lax.dot_general(
             left_rows, right_half, (((0,), (0,)), ((), ())), preferred_element_type=f32
         ).astype(bf16)
-        return chip_scatter(whole, order)
 
     def chip_scatter(whole, order):
         sizes = [grid_axes()[a][3] for a in "zxy"]
         rows = whole.shape[0] // (sizes[0] * sizes[1] * sizes[2])
-        mine = scatter_rings(whole.reshape(*sizes, rows, whole.shape[1]), order, "zxy")
-        mine = mine.reshape(2, rows // 2, whole.shape[1])
-        sent = swap_cores(lax.dynamic_index_in_dim(mine, 1 - core, 0, False))
-        kept = lax.dynamic_index_in_dim(mine, core, 0, False)
+        whole = whole.reshape(*sizes, rows, whole.shape[1])
+        return Scatter(whole, order)
+
+    def join_rows(flights):
+        joined = Scatter(
+            jnp.concatenate([f.whole for f in flights], axis=-2), flights[0].order, "z"
+        )
+        joined.parts = [f.whole.shape[-2] for f in flights]
+        return joined
+
+    def split_rows(flight):
+        whole = run_out(flight)
+        pieces, start = [], 0
+        for rows in flight.parts:
+            pieces.append(whole[start : start + rows])
+            start += rows
+        return pieces
+
+    def shards_of(pieces):
+        halves = [p.reshape(2, p.shape[0] // 2, p.shape[1]) for p in pieces]
+        sent = jnp.concatenate(
+            [lax.dynamic_index_in_dim(h, 1 - core, 0, False) for h in halves], axis=0
+        )
+        sent = swap_cores(sent)
+        shards, start = [], 0
         first = core == 0
-        return jnp.concatenate(
-            [jnp.where(first, kept, sent), jnp.where(first, sent, kept)], axis=1
-        )
-
-    down_shard = chip_grad(both_rows(hidden), both_halves(out_grad), "zyx")
-    hidden_grad = lax.dot_general(
-        out_grad, full_mlp_down, (((1,), (1,)), ((), ())), preferred_element_type=f32
-    )
-    gate_grad_low = (hidden_grad * mlp_up_pre * mlp_slope).astype(bf16)
-    up_grad_low = (hidden_grad * mlp_act).astype(bf16)
+        for h in halves:
+            kept = lax.dynamic_index_in_dim(h, core, 0, False)
+            came = sent[start : start + h.shape[1]]
+            start += h.shape[1]
+            shards.append((jnp.where(first, kept, came), jnp.where(first, came, kept)))
+        return shards
+
+    down_grad = chip_grad(hidden, out_grad)
+    down_shard = lax.psum_scatter(down_grad, everywhere, scatter_dimension=0, tiled=True)
+    my_tile = pl.BlockSpec(tokens_tile, lambda j, core: (0, jnp.minimum(j, tiles // 2 - 1)))
+    other_tile = pl.BlockSpec(tokens_tile, lambda j, core: (0, jnp.maximum(j - tiles // 2, 0)))
+    tile_at = pl.BlockSpec(tokens_tile, lambda j, core: (0, turned(j, core)))
+    half_array = array((token_count, ff_width // 2), bf16)
+    gate_my, gate_other, up_my, up_other = feature_call(
+        hidden_grad_kernel,
+        core_number,
+        tiles,
+        [after(out_grad, down_grad), full_mlp_down, mlp_act, mlp_rise],
+        [
+            whole_spec(tokens_model),
+            pl.BlockSpec((tile, model_width), lambda j, core: (turned(j, core), 0)),
+            tile_at,
+            tile_at,
+        ],
+        [half_array] * 4,
+        [my_tile, other_tile, my_tile, other_tile],
+    )
+    gate_my, gate_other, up_my, up_other, hidden = lax.optimization_barrier(
+        (gate_my, gate_other, up_my, up_other, hidden)
+    )
     normed_mid_pair = both_rows(normed_mid)
-    mlp_gate_shard = chip_grad(normed_mid_pair, both_halves(gate_grad_low), "xyz")
-    mlp_up_shard = chip_grad(normed_mid_pair, both_halves(up_grad_low), "yxz")
+    gate_grad_half = jnp.concatenate([gate_my, swap_cores(gate_other)], axis=0)
+    up_grad_half = jnp.concatenate([up_my, swap_cores(up_other)], axis=0)
+    (block_out,) = feature_call(
+        down_kernel,
+        core_number,
+        tiles,
+        [hidden, full_mlp_down, middle],
+        [
+            plain,
+            pl.BlockSpec((tile, model_width), lambda j, core: (j, 0)),
+            whole_spec(tokens_model),
+        ],
+        [array(tokens_model, f32)],
+        [whole_spec(tokens_model)],
+    )
+    block_out, gate_grad_half, up_grad_half, normed_mid_pair = lax.optimization_barrier(
+        (block_out, gate_grad_half, up_grad_half, normed_mid_pair)
+    )
+    mlp_gate_grad = chip_grad(normed_mid_pair, gate_grad_half)
+    mlp_up_grad = chip_grad(normed_mid_pair, up_grad_half)
+    gate_my, mlp_gate_grad, mlp_up_grad = lax.optimization_barrier(
+        (gate_my, mlp_gate_grad, mlp_up_grad)
+    )
+    gate_flight = chip_scatter(mlp_gate_grad, "xzy")
+    up_flight = chip_scatter(mlp_up_grad, "yxz")
+    gate_my = launch(gate_my, gate_flight, up_flight)
     transposed = (((1,), (1,)), ((), ()))
-    normed_mid_grad = lax.dot_general(
-        gate_grad_low, full_mlp_gate, transposed, preferred_element_type=f32
-    ) + lax.dot_general(up_grad_low, full_mlp_up, transposed, preferred_element_type=f32)
+    tokens_half = (token_count, model_width // 2)
+    middle_grad, middle_low, middle_my, middle_other, gain_mid_grad = feature_call(
+        middle_kernel,
+        core_number,
+        tiles,
+        [
+            gate_my,
+            gate_other,
+            up_my,
+            up_other,
+            full_mlp,
+            full_mlp,
+            middle,
+            out_grad,
+            gain_mid[None],
+        ],
+        [
+            my_tile,
+            other_tile,
+            my_tile,
+            other_tile,
+            pl.BlockSpec((model_width, tile), lambda j, core: (0, turned(j, core))),
+            pl.BlockSpec((model_width, tile), lambda j, core: (0, turned(j, core) + tiles)),
+            whole_spec(tokens_model),
+            whole_spec(tokens_model),
+            whole_spec((1, model_width)),
+        ],
+        [
+            array(tokens_model, f32),
+            array(tokens_model, bf16),
+            array(tokens_half, bf16),
+            array(tokens_half, bf16),
+            array((1, model_width), f32),
+        ],
+        [
+            whole_spec(tokens_model),
+            whole_spec(tokens_model),
+            whole_spec(tokens_half),
+            whole_spec(tokens_half),
+            whole_spec((1, model_width)),
+        ],
+        [pltpu.VMEM(tokens_model, f32)],
+    )
 
     def norm_back(grad, values, scale, gain):
         weighted = grad * gain
@@ -479,10 +812,8 @@
         back = scale * weighted - values * (scale * scale * scale * inner)
         return back, jnp.sum(grad * values * scale, axis=0)
 
-    mid_back, gain_mid_grad = norm_back(normed_mid_grad, middle, scale_mid, gain_mid)
-    middle_grad = out_grad.astype(f32) + mid_back
-    middle_low = middle_grad.astype(bf16)
-    branch_shard = chip_grad(both_rows(mixed), both_halves(middle_low), "xyz")
+    middle_half = jnp.concatenate([middle_my, swap_cores(middle_other)], axis=0)
+    mixed_pair = both_rows(mixed)
     mixed_grad = lax.dot_general(middle_low, full_branch, transposed, preferred_element_type=f32)
     gate_pre_low, tail_keep, local_grad = channel_call(
         reverse_kernel,
@@ -491,14 +822,24 @@
         [wide_bf16, wide_f32, wide_f32],
         lru_width,
         block_width,
-        0,
+        kernel_flops,
     )
     normed_in_pair = both_rows(normed_in)
-    gate_in_shard = chip_grad(normed_in_pair, both_halves(gate_pre_low), "yxz")
     first_keep = keep.reshape(row_count, row_tokens, lru_width)[:, 0]
     head_factor = first_keep * tail_keep.reshape(row_count, row_tokens, lru_width)[:, 0]
     head_grad = first_keep * local_grad.reshape(row_count, row_tokens, lru_width)[:, 0]
     grad_in = carry_before(head_factor, head_grad, True)
+    grad_in, gate_pre_low, mixed_pair = tick(
+        (grad_in, gate_pre_low, mixed_pair), gate_flight, up_flight
+    )
+    branch_grad = chip_grad(mixed_pair, middle_half)
+    gate_in_grad = chip_grad(normed_in_pair, both_halves(gate_pre_low))
+    grad_in, branch_grad, gate_in_grad = lax.optimization_barrier(
+        (grad_in, branch_grad, gate_in_grad)
+    )
+    branch_flight = chip_scatter(branch_grad, "xyz")
+    gate_in_flight = chip_scatter(gate_in_grad, "yxz")
+    grad_in = launch(grad_in, branch_flight, gate_in_flight)
     square = jax.ShapeDtypeStruct((lru_width, block_width), f32)
     signal_part, head_part, rec_full, input_full, sums = channel_call(
         backward_kernel,
@@ -527,8 +868,9 @@
         ],
         lru_width,
         block_width,
-        3 * block_flops,
-    )
+        3 * kernel_flops // 2,
+    )
+    signal_part = land(signal_part, gate_flight, up_flight)
     from_right = passed_along(
         head_part.reshape(row_count, halo, lru_width)[:, halo - halo_rows :].astype(bf16),
         "seq",
@@ -542,46 +884,105 @@
         .astype(bf16)
         .reshape(token_count, lru_width)
     )
-    signal_shard = chip_grad(normed_in_pair, both_halves(signal_low), "xyz")
+    signal_low = launch(signal_low, gate_flight, up_flight)
+    signal_low, gate_pre_low, signal_half = lax.optimization_barrier(
+        (signal_low, gate_pre_low, my_half(signal_low))
+    )
+    gate_part = lax.dot_general(
+        gate_pre_low, full_gate_in, transposed, preferred_element_type=f32
+    )
+    gate_part, sent_half = lax.optimization_barrier(
+        (gate_part, swap_cores(other_half(signal_low)))
+    )
+    signal_grad = chip_grad(
+        normed_in_pair, jnp.concatenate([signal_half, sent_half], axis=0)
+    )
     pair_grads = jnp.where(core == 0, rec_full, input_full) + swap_cores(
         jnp.where(core == 0, input_full, rec_full).astype(bf16)
     ).astype(f32)
-    pair_shard = chip_scatter(pair_grads.astype(bf16), "yxz")
-    normed_in_grad = lax.dot_general(
-        gate_pre_low, full_gate_in, transposed, preferred_element_type=f32
-    ) + lax.dot_general(signal_low, full_signal, transposed, preferred_element_type=f32)
+    sizes = [grid_axes()[a][3] for a in "zxyc"]
+    chip_count = sizes[0] * sizes[1] * sizes[2]
+    quarter = lru_width // 4
+    signal_first = chip_scatter(signal_grad[:, :quarter], "xyz")
+    pair_rows = pair_grads.astype(bf16).reshape(chip_count, -1, quarter)
+    pair_count = pair_rows.shape[1]
+    signal_second = chip_scatter(
+        jnp.concatenate(
+            [signal_grad[:, quarter:].reshape(chip_count, -1, quarter), pair_rows], axis=1
+        ).reshape(-1, quarter),
+        "yxz",
+    )
+    signal_low = launch(signal_low, signal_first, signal_second)
+    normed_in_grad = gate_part + lax.dot_general(
+        signal_low, full_signal, transposed, preferred_element_type=f32
+    )
+    normed_in_grad = tick(
+        after(normed_in_grad, down_shard),
+        signal_first,
+        signal_second,
+        branch_flight,
+        gate_in_flight,
+    )
+    normed_in_grad = land(normed_in_grad, gate_flight, up_flight)
     in_back, gain_in_grad = norm_back(normed_in_grad, inputs, scale_in, gain_in)
+    in_back, gain_in_grad = land((in_back, gain_in_grad), signal_first, signal_second)
+    signal_last = join_rows([signal_first, signal_second])
+    in_back, gain_in_grad = launch((in_back, gain_in_grad), signal_last)
+    in_back = land(in_back, branch_flight, gate_in_flight)
+    branch_rows = branch_flight.whole.shape[-2]
+    branch_flight.whole = branch_flight.whole.reshape(sizes[0], -1, lru_half)
+    middle_two = join_rows([branch_flight, gate_in_flight])
+    in_back = launch(in_back, middle_two)
     tokens_grad = (middle_grad + in_back).reshape(tokens.shape)
 
     decay_grad = sums[0] * rate_scale * jax.nn.sigmoid(-decay_full)
-    tap_grads = sums[1:].reshape(tap_count, device_count, lru_piece).transpose(1, 0, 2)
-    small_grads = jnp.concatenate(
-        [
-            gain_in_grad.reshape(device_count, model_piece),
-            gain_mid_grad.reshape(device_count, model_piece),
-            decay_grad.reshape(device_count, lru_piece),
-            tap_grads.reshape(device_count, tap_count * lru_piece),
-        ],
-        axis=1,
-    )
-    sizes = [grid_axes()[a][3] for a in "zxyc"]
-    small_shard = scatter_rings(small_grads.reshape(*sizes, 1, small_size), "cxyz", "zxyc")[0]
-    start = 2 * model_piece + lru_piece
+    small_grads = [gain_in_grad, gain_mid_grad[0], decay_grad, *(sums[1 + k] for k in range(tap_count))]
+    every_small = jnp.concatenate(small_grads)
+    for which in "cxyz":
+        every_small = every_small + sum(
+            hop(every_small, which, d) for d in range(1, grid_axes()[which][3])
+        )
+    device = lax.axis_index("dp") * lax.axis_size("seq") + lax.axis_index("seq")
+    small_shards, start = [], 0
+    for grad in small_grads:
+        width = grad.shape[0] // device_count
+        small_shards.append(
+            lax.dynamic_slice_in_dim(every_small, start + device * width, width, 0)
+        )
+        start += grad.shape[0]
+    mlp_gate_shard, mlp_up_shard = [
+        jnp.concatenate(pair, axis=1)
+        for pair in shards_of([gate_flight.whole, up_flight.whole])
+    ]
+    branch_pair, gate_in_pair = shards_of(split_rows(middle_two))
+    branch_shard = jnp.concatenate(
+        [a.reshape(-1, model_width // 2) for a in branch_pair], axis=1
+    )
+    gate_in_shard = jnp.concatenate(gate_in_pair, axis=1)
+    signal_last.parts = [
+        signal_last.parts[0],
+        signal_last.parts[1] - pair_count,
+        pair_count,
+    ]
+    signal_one, signal_two, pair_halves = shards_of(split_rows(signal_last))
+    signal_shard = jnp.concatenate(
+        [signal_one[0], signal_two[0], signal_one[1], signal_two[1]], axis=1
+    )
     return (
         block_out.reshape(tokens.shape),
         tokens_grad,
-        small_shard[:model_piece],
+        small_shards[0],
         gate_in_shard,
         signal_shard,
-        small_shard[start:].reshape(tap_count, lru_piece),
-        pair_shard[:, :block_width],
-        pair_shard[:, block_width:],
-        small_shard[2 * model_piece : start],
+        jnp.stack(small_shards[3:]),
+        pair_halves[0].reshape(lru_piece, block_width),
+        pair_halves[1].reshape(lru_piece, block_width),
+        small_shards[2],
         branch_shard,
-        small_shard[model_piece : 2 * model_piece],
+        small_shards[1],
         mlp_gate_shard,
         mlp_up_shard,
-        down_shard,
+        down_shard.astype(f32),
     )
 
 

time: 697 us -> 474 us (0.68)
  waiting for transfers between devices: 353 us -> 70.8 us
  Pallas kernels: 45.9 us -> 96.4 us
  matrix products: 95.1 us -> 46.9 us
  starting transfers between devices: 61.6 us -> 101 us
  between operations: 3.24 us -> 15.7 us
  blocking collectives: 10.7 us -> 20.3 us
    ppermute x101 -> x12, waiting for transfers between devices: 352 us -> 3.99 us  [ring_step(): return lax.ppermute(block, name, route)]
    ppermute x0 -> x54, starting transfers between devices: none -> 92 us  [hop(): return lax.ppermute(block, name, route)]
    ppermute x0 -> x54, waiting for transfers between devices: none -> 55.1 us  [hop(): return lax.ppermute(block, name, route)]
    ppermute x101 -> x12, starting transfers between devices: 56.5 us -> 2.76 us  [ring_step(): return lax.ppermute(block, name, route)]
    pallas_call x0 -> x4, Pallas kernels: none -> 49.7 us  [feature_call(): pl.pallas_call(kernel, grid_spec=pltpu.PrefetchScalarGridSpec(num_scalar_...]
    dot_general x6 -> x1, matrix products: 49.6 us -> 0.56 us  [body(): jnp.dot(tail_normed, full_signal, preferred_element_type=f32).astype(bf16)]
    another operation x42 -> x25, other arithmetic: 41.6 us -> 14.6 us  [the longest x24 14 us: finish(): jnp.stack([jnp.where(first, a, b), jnp.where(first, b, a)], axis=spot)]
    unnamed x112 -> x180, local copies, waits for them, and re-layouts: 4.21 us -> 16.6 us
  transfers between devices with their start and end apart: 104 -> 72, of which waited for: 53 -> 18; matrix products, arithmetic and copies ran while one was open for 31% -> 30% of each run, Pallas kernels for 7% -> 21%
where the time goes in v2:
time: 474 us; the launch traced here: 465 us
  starting transfers between devices  101 us (21%)
  Pallas kernels  96.4 us (20%)
  waiting for transfers between devices  70.8 us (15%)
  other arithmetic  58 us (12%)
  local copies, waits for them, and re-layouts  55.7 us (12%)
  matrix products  46.9 us (10%)
  blocking collectives  20.3 us (4%)
  between operations  15.7 us (3%)
    ppermute x54, starting transfers between devices, hop(): return lax.ppermute(block, name, route)  92 us
    ppermute x54, waiting for transfers between devices, hop(): return lax.ppermute(block, name, route)  55.1 us
    pallas_call x4, Pallas kernels, feature_call(): pl.pallas_call(kernel, grid_spec=pltpu.PrefetchScalarGridSpec(num_scalar_...  49.7 us
    pallas_call x3, Pallas kernels, channel_call(): pl.pallas_call(functools.partial(kernel, row_count), grid=(width // block...  46.7 us
    dot_general x6, matrix products, chip_grad(): lax.dot_general(left_rows, right_half, (((0,), (0,)), ((), ())), preferre...  23.9 us
    all_gather x2, blocking collectives, carry_before(): both = lax.all_gather(jnp.stack([factor, value]), 'seq')  20.3 us
    unnamed x180, local copies, waits for them, and re-layouts  16.6 us
    another operation x24, other arithmetic, finish(): jnp.stack([jnp.where(first, a, b), jnp.where(first, b, a)], axis=spot)  14 us
  transfers between devices with their start and end apart: 72, of which 18 were waited for; matrix products, arithmetic and copies ran while one was open for 30% of the time, Pallas kernels for 21%

profile of v2, /device:TPU:0, one launch (start us, length us, event | category | flops | bytes accessed | tf_op | source)
XLA Modules:
  0.0 465.1 jit_solution(5106819135601860173)
XLA Ops:
  9.9 3.5 concatenate.82
  14.3 3.1 collective-permute-start
  17.4 2.6 collective-permute-start.1
  22.4 2.9 collective-permute-start.5
  25.4 4.3 collective-permute-done.3
  29.7 4.6 collective-permute-done.4
  37.5 4.2 collective-permute-start.10
  46.5 4.7 %collective-permute-start.13 = (bf16[48,1024]{1,0:T(8,128)(2,1)S(1)}, bf16[48,1024]{1,0:T(8,128)(2,1)S(1)}, u32[]{:S(2)}, u32[]{:S(2)}) collective-permute-start(bf16[48,1024]{1,0:T(8,128)(2,1)S(1)} %copy-done.78), channel_id=1, source_target_pairs={{0,8},{4,12},{8,16},{12,20},{16,24},{20,28},{24,0},{28,4},{1,9},{5... | collective-permute-start | bytes 294920 | tf_op jit(solution)/shard_map/ppermute | solution.py:64
  55.6 2.6 collective-permute-done.13
  58.2 5.8 %collective-permute-done.14 = bf16[48,1024]{1,0:T(8,128)(2,1)S(1)} collective-permute-done((bf16[48,1024]{1,0:T(8,128)(2,1)S(1)}, bf16[48,1024]{1,0:T(8,128)(2,1)S(1)}, u32[]{:S(2)}, u32[]{:S(2)}) %collective-permute-start.14) | collective-permute-done | bytes 98336 | tf_op jit(solution)/shard_map/ppermute | solution.py:64
  69.6 2.4 collective-permute-start.18
  72.1 2.5 collective-permute-start.19
  76.5 2.4 collective-permute-start.20
  95.6 13.2 %shard_map.254 = (bf16[512,1536]{1,0:T(8,128)(2,1)S(1)}, f32[512,1536]{1,0:T(8,128)}, f32[512,1536]{1,0:T(8,128)}, f32[512,1536]{1,0:T(8,128)}) custom-call(bf16[512,1536]{1,0:T(8,128)(2,1)S(1)} %convolution_convert_fusion.4.sig_ref, f32[16,1536]{1,0:T(8,128)S(1)} %fusion.9.tail_ref.before_ref, f32[3,512,128]{2,1,0:T(8,128)S(1)} %broadcast_in_dim.107.mask_ref, ...), custom_call_target="tpu_custom_call" | custom-call | flops 1 | bytes 1 | tf_op jit(solution)/shard_map/pallas_call | solution.py:343
  110.8 5.9 %all-gather = f32[8,2,1536]{2,1,0:T(2,128)S(1)} all-gather(f32[2,2,1536]{2,1,0:T(2,128)S(1)} %pad_maximum_fusion.33), channel_id=2, replica_groups=mesh['dp'=8,'seq'=4] {'seq'}, dimensions={0}, use_global_device_ids=true | all-gather | bytes 122880 | tf_op jit(solution)/shard_map/all_gather | solution.py:484
  119.8 19.3 %collective-permute-done.22 = bf16[4,2,32,1536]{3,2,1,0:T(8,128)(2,1)S(1)} collective-permute-done((bf16[4,2,32,1536]{3,2,1,0:T(8,128)(2,1)S(1)}, bf16[4,2,32,1536]{3,2,1,0:T(8,128)(2,1)S(1)}, u32[]{:S(2)}, u32[]{:S(2)}) %collective-permute-start.22) | collective-permute-done | bytes 786464 | tf_op jit(solution)/shard_map/ppermute | solution.py:64
  143.9 2.8 collective-permute-done.24
  151.0 2.7 copy-done.45
  154.7 5.8 %fusion.5 = (bf16[512,1536]{1,0:T(8,128)(2,1)}, f32[512,1536]{1,0:T(8,128)}, f32[512,1536]{1,0:T(8,128)}) fusion(f32[512,1536]{1,0:T(8,128)S(1)} %copy-done.46, f32[512,1536]{1,0:T(8,128)S(1)} %copy-done.45, f32[2,1536]{1,0:T(2,128)S(1)} %fusion.83.state_in_ref, bf16[512,1024]{1,0:T(8,128)(2,1)S(1)} %bitcast.438, bf16[1024,1536]{1,0:T(8,128)(2,1)S(1)} %bitcast.429), kind=kOutput, calls=%fused_computation.9 | convolution fusion | flops 1620049920 | bytes 18362368 | tf_op jit(solution)/shard_map/dot_general | solution.py:634
  162.5 4.4 multiply_reduce_fusion
  167.2 14.4 %shard_map.255 = (f32[512,3072]{1,0:T(8,128)}, f32[512,3072]{1,0:T(8,128)}, bf16[512,3072]{1,0:T(8,128)(2,1)S(1)}) custom-call(s32[1]{0:T(128)} %bitcast.core_ref, bf16[512,1024]{1,0:T(8,128)(2,1)S(1)} %multiply_convert_fusion.normed_ref, bf16[1024,6144]{1,0:T(8,128)(2,1)} %all-gather.5.cloned.1.call-done.gate_w_ref.up_w_ref, ...), custom_call_target="tpu_custom_call" | custom-call | flops 1 | bytes 1 | tf_op jit(solution)/shard_map/pallas_call | solution.py:355
  181.7 5.3 %convolution_convert_fusion = bf16[3072,1024]{1,0:T(8,128)(2,1)} fusion(bf16[512,3072]{1,0:T(8,128)(2,1)S(1)} %get-tuple-element.242.hidden_ref, bf16[512,1024]{1,0:T(8,128)(2,1)S(1)} %bitcast.424), kind=kOutput, calls=%fused_computation | convolution fusion | flops 3224371200 | bytes 10485760 | tf_op jit(solution)/shard_map/dot_general | solution.py:674
  188.7 11.6 %all-gather.7.cloned.1.call-done.down_ref = bf16[3072,1024]{1,0:T(8,128)(2,1)} async-done(((bf16[96,1024]{1,0:T(8,128)(2,1)}), bf16[3072,1024]{1,0:T(8,128)(2,1)}) %all-gather.7.cloned.1.call-update) | async-done | bytes 6291472 | tf_op jit(solution)/shard_map/all_gather | solution.py:539
  201.5 11.2 %shard_map.256 = (bf16[512,1536]{1,0:T(8,128)(2,1)S(1)}, bf16[512,1536]{1,0:T(8,128)(2,1)}, bf16[512,1536]{1,0:T(8,128)(2,1)S(1)}, bf16[512,1536]{1,0:T(8,128)(2,1)}) custom-call(s32[1]{0:T(128)} %bitcast.core_ref, bf16[512,1024]{1,0:T(8,128)(2,1)S(1)} %bitcast.425, bf16[3072,1024]{1,0:T(8,128)(2,1)} %all-gather.7.cloned.1.call-done.down_ref, ...), custom_call_target="tpu_custom_call" | custom-call | flops 1 | bytes 1 | tf_op jit(solution)/shard_map/pallas_call | solution.py:355
  218.4 3.2 collective-permute-done.28
  221.6 2.7 pad_maximum_fusion.7
  224.3 3.8 pad_maximum_fusion.5
  230.1 8.5 %shard_map.257 = f32[512,1024]{1,0:T(8,128)} custom-call(s32[1]{0:T(128)} %bitcast.core_ref, bf16[512,3072]{1,0:T(8,128)(2,1)S(1)} %copy-done.16, bf16[3072,1024]{1,0:T(8,128)(2,1)} %all-gather.7.cloned.1.call-done.down_ref, f32[512,1024]{1,0:T(8,128)S(1)} %get-tuple-element.439.middle_ref), custom_call_target="tpu_custom_call" | custom-call | flops 1 | bytes 1 | tf_op jit(solution)/shard_map/pallas_call | solution.py:355
  242.6 3.8 convolution_convert_fusion.2
  246.4 3.8 convolution_convert_fusion.1
  254.9 15.6 %shard_map.258 = (f32[512,1024]{1,0:T(8,128)}, bf16[512,1024]{1,0:T(8,128)(2,1)S(1)}, bf16[512,512]{1,0:T(8,128)(2,1)S(1)}, bf16[512,512]{1,0:T(8,128)(2,1)}, f32[1,1024]{1,0:T(1,128)S(1)}) custom-call(s32[1]{0:T(128)} %bitcast.core_ref, bf16[512,1536]{1,0:T(8,128)(2,1)S(1)} %copy-done.4, bf16[512,1536]{1,0:T(8,128)(2,1)} %get-tuple-element.244.gate_other, ...), custom_call_target="tpu_custom_call" | custom-call | flops 1 | bytes 1 | tf_op jit(solution)/shard_map/pallas_call | solution.py:355
  270.5 3.6 fusion.116.mixed_grad_ref
  274.1 13.8 %shard_map.259 = (bf16[512,1536]{1,0:T(8,128)(2,1)S(1)}, f32[512,1536]{1,0:T(8,128)S(1)}, f32[512,1536]{1,0:T(8,128)}) custom-call(f32[512,1536]{1,0:T(8,128)} %fusion.116.mixed_grad_ref, f32[512,1536]{1,0:T(8,128)} %get-tuple-element.348.states_ref, f32[512,1536]{1,0:T(8,128)} %get-tuple-element.437.gate_ref, f32[512,1536]{1,0:T(8,128)} %get-tuple-element.258.keep_ref), custom_call_target="tpu_custom_call" | custom-call | flops 1 | bytes 1 | tf_op jit(solution)/shard_map/pallas_call | solution.py:343
  289.0 14.5 %all-gather.1 = f32[8,2,1536]{2,1,0:T(2,128)S(1)} all-gather(f32[2,2,1536]{2,1,0:T(2,128)S(1)} %pad_maximum_fusion.34), channel_id=3, replica_groups=mesh['dp'=8,'seq'=4] {'seq'}, dimensions={0}, use_global_device_ids=true | all-gather | bytes 122880 | tf_op jit(solution)/shard_map/all_gather | solution.py:484
  314.5 4.0 convolution_convert_fusion.3
  318.5 2.4 collective-permute-start.37
  321.0 3.3 convolution_convert_fusion.7
  327.2 19.7 %shard_map.260 = (f32[512,1536]{1,0:T(8,128)}, f32[16,1536]{1,0:T(8,128)S(1)}, f32[1536,128]{1,0:T(8,128)S(1)}, f32[1536,128]{1,0:T(8,128)S(1)}, f32[5,1536]{1,0:T(8,128)S(1)}) custom-call(bf16[512,1536]{1,0:T(8,128)(2,1)S(1)} %copy-done.8, f32[16,1536]{1,0:T(8,128)S(1)} %copy-done.21, f32[3,512,128]{2,1,0:T(8,128)S(1)} %copy-done.2, ...), custom_call_target="tpu_custom_call" | custom-call | flops 1 | bytes 1 | tf_op jit(solution)/shard_map/pallas_call | solution.py:343
  346.9 3.3 collective-permute-done.36
  360.6 3.2 fusion.117
  364.1 3.7 convolution_convert_fusion.6
  373.7 3.7 fusion.32
  377.9 9.0 %collective-permute-start.47 = (bf16[64,1536]{1,0:T(8,128)(2,1)}, bf16[64,1536]{1,0:T(8,128)(2,1)S(1)}, u32[]{:S(2)}, u32[]{:S(2)}) collective-permute-start(bf16[64,1536]{1,0:T(8,128)(2,1)} %get-tuple-element.310), channel_id=1, source_target_pairs={{0,8},{4,12},{8,16},{12,20},{16,24},{20,28},{24,0},{28,4},{1,9},{5... | collective-permute-start | bytes 589832 | tf_op jit(solution)/shard_map/ppermute | solution.py:64
  387.4 5.9 %collective-permute-start.49 = (bf16[64,1536]{1,0:T(8,128)(2,1)S(1)}, bf16[64,1536]{1,0:T(8,128)(2,1)S(1)}, u32[]{:S(2)}, u32[]{:S(2)}) collective-permute-start(bf16[64,1536]{1,0:T(8,128)(2,1)S(1)} %get-tuple-element.312), channel_id=1, source_target_pairs={{0,24},{4,28},{8,0},{12,4},{16,8},{20,12},{24,16},{28,20},{1,25},{... | collective-permute-start | bytes 589832 | tf_op jit(solution)/shard_map/ppermute | solution.py:64
  410.3 4.0 collective-permute-done.51
  417.7 3.7 collective-permute-start.66
  437.5 8.1 %collective-permute-start.58 = (f32[9728]{0:T(1024)S(1)}, f32[9728]{0:T(1024)S(1)}, u32[]{:S(2)}, u32[]{:S(2)}) collective-permute-start(f32[9728]{0:T(1024)S(1)} %add.466), channel_id=1, source_target_pairs={{0,16},{4,20},{8,24},{12,28},{16,0},{20,4},{24,8},{28,12},{1,17},{... | collective-permute-start | bytes 116744 | tf_op jit(solution)/shard_map/ppermute | solution.py:64
  446.8 3.5 collective-permute-start.60
  (490 shorter events, 156.3 us)
Async XLA Ops:
  7.2 160.0 %all-gather.5.cloned.1.call-start = ((), (), s32[]{:S(2)}) async-start(), calls=%async_computation.1 | async-start | bytes 12976128 | tf_op jit(solution)/shard_map/all_gather | solution.py:538
  9.1 191.2 %all-gather.7.cloned.1.call-start = ((), (), s32[]{:S(2)}) async-start(), calls=%async_computation.2 | async-start | bytes 6488064 | tf_op jit(solution)/shard_map/all_gather | solution.py:539
  22.0 12.2 %collective-permute-start.4 = (bf16[32,1280]{1,0:T(8,128)(2,1)S(1)}, bf16[32,1280]{1,0:T(8,128)(2,1)S(1)}, u32[]{:S(2)}, u32[]{:S(2)}) collective-permute-start(bf16[32,1280]{1,0:T(8,128)(2,1)S(1)} %pad_maximum_fusion.32), channel_id=1, source_target_pairs={{0,16},{4,20},{8,24},{12,28},{16,0},{20,4},{24,8},{28,12},{1,17},{... | collective-permute-start | bytes 245768 | tf_op jit(solution)/shard_map/ppermute | solution.py:64
  22.4 11.9 %collective-permute-start.5 = (bf16[32,1280]{1,0:T(8,128)(2,1)S(1)}, bf16[32,1280]{1,0:T(8,128)(2,1)S(1)}, u32[]{:S(2)}, u32[]{:S(2)}) collective-permute-start(bf16[32,1280]{1,0:T(8,128)(2,1)S(1)} %pad_maximum_fusion.32), channel_id=1, source_target_pairs={{0,24},{4,28},{8,0},{12,4},{16,8},{20,12},{24,16},{28,20},{1,25},{... | collective-permute-start | bytes 245768 | tf_op jit(solution)/shard_map/ppermute | solution.py:64
  34.4 9.8 %collective-permute-start.7 = (bf16[4,32,1280]{2,1,0:T(8,128)(2,1)S(1)}, bf16[4,32,1280]{2,1,0:T(8,128)(2,1)S(1)}, u32[]{:S(2)}, u32[]{:S(2)}) collective-permute-start(bf16[4,32,1280]{2,1,0:T(8,128)(2,1)S(1)} %bitcast_dynamic-update-slice_fusion.8), channel_id=1, source_target_pairs={{0,4},{4,0},{8,12},{12,8},{16,20},{20,16},{24,28},{28,24},{1,5},{5... | collective-permute-start | bytes 983048 | tf_op jit(solution)/shard_map/ppermute | solution.py:64
  44.4 19.7 %collective-permute-start.8 = (bf16[4,2,32,768]{3,2,1,0:T(8,128)(2,1)S(1)}, bf16[4,2,32,768]{3,2,1,0:T(8,128)(2,1)S(1)}, u32[]{:S(2)}, u32[]{:S(2)}) collective-permute-start(bf16[4,2,32,768]{3,2,1,0:T(8,128)(2,1)S(1)} %pad_maximum_fusion.22), channel_id=1, source_target_pairs={{0,4},{4,0},{8,12},{12,8},{16,20},{20,16},{24,28},{28,24},{1,5},{5... | collective-permute-start | bytes 1179656 | tf_op jit(solution)/shard_map/ppermute | solution.py:64
  45.0 19.1 %collective-permute-start.9 = (bf16[4,2,32,1280]{3,2,1,0:T(8,128)(2,1)S(1)}, bf16[4,2,32,1280]{3,2,1,0:T(8,128)(2,1)S(1)}, u32[]{:S(2)}, u32[]{:S(2)}) collective-permute-start(bf16[4,2,32,1280]{3,2,1,0:T(8,128)(2,1)S(1)} %pad_maximum_fusion.21), channel_id=1, source_target_pairs={{0,2},{1,3},{2,0},{3,1},{4,6},{5,7},{6,4},{7,5},{8,10},{9,11},{10,... | collective-permute-start | bytes 1966088 | tf_op jit(solution)/shard_map/ppermute | solution.py:64
  46.5 11.7 %collective-permute-start.13 = (bf16[48,1024]{1,0:T(8,128)(2,1)S(1)}, bf16[48,1024]{1,0:T(8,128)(2,1)S(1)}, u32[]{:S(2)}, u32[]{:S(2)}) collective-permute-start(bf16[48,1024]{1,0:T(8,128)(2,1)S(1)} %copy-done.78), channel_id=1, source_target_pairs={{0,8},{4,12},{8,16},{12,20},{16,24},{20,28},{24,0},{28,4},{1,9},{5... | collective-permute-start | bytes 294920 | tf_op jit(solution)/shard_map/ppermute | solution.py:64
  51.2 12.8 %collective-permute-start.14 = (bf16[48,1024]{1,0:T(8,128)(2,1)S(1)}, bf16[48,1024]{1,0:T(8,128)(2,1)S(1)}, u32[]{:S(2)}, u32[]{:S(2)}) collective-permute-start(bf16[48,1024]{1,0:T(8,128)(2,1)S(1)} %copy-done.78), channel_id=1, source_target_pairs={{0,16},{4,20},{8,24},{12,28},{16,0},{20,4},{24,8},{28,12},{1,17},{... | collective-permute-start | bytes 294920 | tf_op jit(solution)/shard_map/ppermute | solution.py:64
  53.1 11.0 %collective-permute-start.15 = (bf16[48,1024]{1,0:T(8,128)(2,1)S(1)}, bf16[48,1024]{1,0:T(8,128)(2,1)S(1)}, u32[]{:S(2)}, u32[]{:S(2)}) collective-permute-start(bf16[48,1024]{1,0:T(8,128)(2,1)S(1)} %copy-done.78), channel_id=1, source_target_pairs={{0,24},{4,28},{8,0},{12,4},{16,8},{20,12},{24,16},{28,20},{1,25},{... | collective-permute-start | bytes 294920 | tf_op jit(solution)/shard_map/ppermute | solution.py:64
  69.6 11.2 %collective-permute-start.17 = (bf16[4,2,2,32,1280]{4,3,2,1,0:T(8,128)(2,1)}, bf16[4,2,2,32,1280]{4,3,2,1,0:T(8,128)(2,1)}, u32[]{:S(2)}, u32[]{:S(2)}) collective-permute-start(bf16[4,2,2,32,1280]{4,3,2,1,0:T(8,128)(2,1)} %pad_maximum_fusion.14), channel_id=1, source_target_pairs={{0,1},{1,0},{2,3},{3,2},{4,5},{5,4},{6,7},{7,6},{8,9},{9,8},{10,11... | collective-permute-start | bytes 3932168 | tf_op jit(solution)/shard_map/ppermute | solution.py:64
  74.7 303.2 %reduce-scatter.2.cloned.1.call-start = ((), (), s32[]{:S(2)}) async-start(), calls=%async_computation.3 | async-start | bytes 6488064 | tf_op jit(solution)/shard_map/reduce_scatter | solution.py:715
  76.5 40.2 %collective-permute-start.20 = (bf16[4,32,1536]{2,1,0:T(8,128)(2,1)}, bf16[4,32,1536]{2,1,0:T(8,128)(2,1)}, u32[]{:S(2)}, u32[]{:S(2)}) collective-permute-start(bf16[4,32,1536]{2,1,0:T(8,128)(2,1)} %bitcast_dynamic-update-slice_fusion.4), channel_id=1, source_target_pairs={{0,4},{4,0},{8,12},{12,8},{16,20},{20,16},{24,28},{28,24},{1,5},{5... | collective-permute-start | bytes 1179656 | tf_op jit(solution)/shard_map/ppermute | solution.py:64
  78.9 37.8 %collective-permute-start.21 = (bf16[4,48,1024]{2,1,0:T(8,128)(2,1)}, bf16[4,48,1024]{2,1,0:T(8,128)(2,1)}, u32[]{:S(2)}, u32[]{:S(2)}) collective-permute-start(bf16[4,48,1024]{2,1,0:T(8,128)(2,1)} %bitcast_dynamic-update-slice_fusion), channel_id=1, source_target_pairs={{0,2},{1,3},{2,0},{3,1},{4,6},{5,7},{6,4},{7,5},{8,10},{9,11},{10,... | collective-permute-start | bytes 1179656 | tf_op jit(solution)/shard_map/ppermute | solution.py:64
  119.2 19.9 %collective-permute-start.22 = (bf16[4,2,32,1536]{3,2,1,0:T(8,128)(2,1)S(1)}, bf16[4,2,32,1536]{3,2,1,0:T(8,128)(2,1)S(1)}, u32[]{:S(2)}, u32[]{:S(2)}) collective-permute-start(bf16[4,2,32,1536]{3,2,1,0:T(8,128)(2,1)S(1)} %pad_maximum_fusion.19), channel_id=1, source_target_pairs={{0,2},{1,3},{2,0},{3,1},{4,6},{5,7},{6,4},{7,5},{8,10},{9,11},{10,... | collective-permute-start | bytes 2359304 | tf_op jit(solution)/shard_map/ppermute | solution.py:64
  119.8 19.5 %collective-permute-start.23 = (bf16[4,2,48,1024]{3,2,1,0:T(8,128)(2,1)S(1)}, bf16[4,2,48,1024]{3,2,1,0:T(8,128)(2,1)S(1)}, u32[]{:S(2)}, u32[]{:S(2)}) collective-permute-start(bf16[4,2,48,1024]{3,2,1,0:T(8,128)(2,1)S(1)} %pad_maximum_fusion.20), channel_id=1, source_target_pairs={{0,4},{4,0},{8,12},{12,8},{16,20},{20,16},{24,28},{28,24},{1,5},{5... | collective-permute-start | bytes 2359304 | tf_op jit(solution)/shard_map/ppermute | solution.py:64
  160.4 63.9 %collective-permute-start.29 = (bf16[512,1536]{1,0:T(8,128)(2,1)}, bf16[512,1536]{1,0:T(8,128)(2,1)}, u32[]{:S(2)}, u32[]{:S(2)}) collective-permute-start(bf16[512,1536]{1,0:T(8,128)(2,1)} %get-tuple-element.347), channel_id=1, source_target_pairs={{0,1},{1,0},{2,3},{3,2},{4,5},{5,4},{6,7},{7,6},{8,9},{9,8},{10,11... | collective-permute-start | bytes 4718600 | tf_op jit(solution)/shard_map/ppermute | solution.py:41
  215.0 23.5 %collective-permute-start.26 = (bf16[512,1536]{1,0:T(8,128)(2,1)}, bf16[512,1536]{1,0:T(8,128)(2,1)}, u32[]{:S(2)}, u32[]{:S(2)}) collective-permute-start(bf16[512,1536]{1,0:T(8,128)(2,1)} %get-tuple-element.244.gate_other), channel_id=1, source_target_pairs={{0,1},{1,0},{2,3},{3,2},{4,5},{5,4},{6,7},{7,6},{8,9},{9,8},{10,11... | collective-permute-start | bytes 4718600 | tf_op jit(solution)/shard_map/ppermute | solution.py:41
  215.5 24.8 %collective-permute-start.27 = (bf16[512,1536]{1,0:T(8,128)(2,1)}, bf16[512,1536]{1,0:T(8,128)(2,1)}, u32[]{:S(2)}, u32[]{:S(2)}) collective-permute-start(bf16[512,1536]{1,0:T(8,128)(2,1)} %get-tuple-element.246.up_other), channel_id=1, source_target_pairs={{0,1},{1,0},{2,3},{3,2},{4,5},{5,4},{6,7},{7,6},{8,9},{9,8},{10,11... | collective-permute-start | bytes 4718600 | tf_op jit(solution)/shard_map/ppermute | solution.py:41
  216.6 101.9 %collective-permute-start.33 = (bf16[512,1024]{1,0:T(8,128)(2,1)}, bf16[512,1024]{1,0:T(8,128)(2,1)}, u32[]{:S(2)}, u32[]{:S(2)}) collective-permute-start(bf16[512,1024]{1,0:T(8,128)(2,1)} %copy-done.67), channel_id=1, source_target_pairs={{0,1},{1,0},{2,3},{3,2},{4,5},{5,4},{6,7},{7,6},{8,9},{9,8},{10,11... | collective-permute-start | bytes 3145736 | tf_op jit(solution)/shard_map/ppermute | solution.py:41
  252.9 51.2 %collective-permute-start.30 = (bf16[4,2,64,1536]{3,2,1,0:T(8,128)(2,1)}, bf16[4,2,64,1536]{3,2,1,0:T(8,128)(2,1)}, u32[]{:S(2)}, u32[]{:S(2)}) collective-permute-start(bf16[4,2,64,1536]{3,2,1,0:T(8,128)(2,1)} %dynamic-slice_bitcast_fusion.1), channel_id=1, source_target_pairs={{0,4},{4,0},{8,12},{12,8},{16,20},{20,16},{24,28},{28,24},{1,5},{5... | collective-permute-start | bytes 4718600 | tf_op jit(solution)/shard_map/ppermute | solution.py:64
  254.3 49.7 %collective-permute-start.31 = (bf16[4,2,64,1536]{3,2,1,0:T(8,128)(2,1)}, bf16[4,2,64,1536]{3,2,1,0:T(8,128)(2,1)}, u32[]{:S(2)}, u32[]{:S(2)}) collective-permute-start(bf16[4,2,64,1536]{3,2,1,0:T(8,128)(2,1)} %dynamic-slice_bitcast_fusion), channel_id=1, source_target_pairs={{0,2},{1,3},{2,0},{3,1},{4,6},{5,7},{6,4},{7,5},{8,10},{9,11},{10,... | collective-permute-start | bytes 4718600 | tf_op jit(solution)/shard_map/ppermute | solution.py:64
  288.9 25.1 %collective-permute-start.32 = (bf16[512,512]{1,0:T(8,128)(2,1)}, bf16[512,512]{1,0:T(8,128)(2,1)}, u32[]{:S(2)}, u32[]{:S(2)}) collective-permute-start(bf16[512,512]{1,0:T(8,128)(2,1)} %get-tuple-element.272), channel_id=1, source_target_pairs={{0,1},{1,0},{2,3},{3,2},{4,5},{5,4},{6,7},{7,6},{8,9},{9,8},{10,11... | collective-permute-start | bytes 1572872 | tf_op jit(solution)/shard_map/ppermute | solution.py:41
  311.5 35.4 %collective-permute-start.35 = (bf16[2,64,1536]{2,1,0:T(8,128)(2,1)}, bf16[2,64,1536]{2,1,0:T(8,128)(2,1)S(1)}, u32[]{:S(2)}, u32[]{:S(2)}) collective-permute-start(bf16[2,64,1536]{2,1,0:T(8,128)(2,1)} %get-tuple-element.279), channel_id=1, source_target_pairs={{0,8},{4,12},{8,16},{12,20},{16,24},{20,28},{24,0},{28,4},{1,9},{5... | collective-permute-start | bytes 1179656 | tf_op jit(solution)/shard_map/ppermute | solution.py:64
  313.0 37.1 %collective-permute-start.36 = (bf16[2,64,1536]{2,1,0:T(8,128)(2,1)}, bf16[2,64,1536]{2,1,0:T(8,128)(2,1)S(1)}, u32[]{:S(2)}, u32[]{:S(2)}) collective-permute-start(bf16[2,64,1536]{2,1,0:T(8,128)(2,1)} %get-tuple-element.280), channel_id=1, source_target_pairs={{0,16},{4,20},{8,24},{12,28},{16,0},{20,4},{24,8},{28,12},{1,17},{... | collective-permute-start | bytes 1179656 | tf_op jit(solution)/shard_map/ppermute | solution.py:64
  314.0 36.2 %collective-permute-start.38 = (bf16[4,64,1536]{2,1,0:T(8,128)(2,1)}, bf16[4,64,1536]{2,1,0:T(8,128)(2,1)S(1)}, u32[]{:S(2)}, u32[]{:S(2)}) collective-permute-start(bf16[4,64,1536]{2,1,0:T(8,128)(2,1)} %dynamic-slice_bitcast_fusion.4), channel_id=1, source_target_pairs={{0,4},{4,0},{8,12},{12,8},{16,20},{20,16},{24,28},{28,24},{1,5},{5... | collective-permute-start | bytes 2359304 | tf_op jit(solution)/shard_map/ppermute | solution.py:64
  318.5 31.6 %collective-permute-start.37 = (bf16[2,64,1536]{2,1,0:T(8,128)(2,1)S(1)}, bf16[2,64,1536]{2,1,0:T(8,128)(2,1)S(1)}, u32[]{:S(2)}, u32[]{:S(2)}) collective-permute-start(bf16[2,64,1536]{2,1,0:T(8,128)(2,1)S(1)} %copy-done.70), channel_id=1, source_target_pairs={{0,24},{4,28},{8,0},{12,4},{16,8},{20,12},{24,16},{28,20},{1,25},{... | collective-permute-start | bytes 1179656 | tf_op jit(solution)/shard_map/ppermute | solution.py:64
  355.9 22.0 %collective-permute-start.44 = (bf16[4,2,96,512]{3,2,1,0:T(8,128)(2,1)}, bf16[4,2,96,512]{3,2,1,0:T(8,128)(2,1)}, u32[]{:S(2)}, u32[]{:S(2)}) collective-permute-start(bf16[4,2,96,512]{3,2,1,0:T(8,128)(2,1)} %dynamic-slice_bitcast_fusion.3), channel_id=1, source_target_pairs={{0,4},{4,0},{8,12},{12,8},{16,20},{20,16},{24,28},{28,24},{1,5},{5... | collective-permute-start | bytes 2359304 | tf_op jit(solution)/shard_map/ppermute | solution.py:64
  356.5 30.5 %collective-permute-start.45 = (bf16[4,2,64,768]{3,2,1,0:T(8,128)(2,1)}, bf16[4,2,64,768]{3,2,1,0:T(8,128)(2,1)}, u32[]{:S(2)}, u32[]{:S(2)}) collective-permute-start(bf16[4,2,64,768]{3,2,1,0:T(8,128)(2,1)} %dynamic-slice_bitcast_fusion.2), channel_id=1, source_target_pairs={{0,2},{1,3},{2,0},{3,1},{4,6},{5,7},{6,4},{7,5},{8,10},{9,11},{10,... | collective-permute-start | bytes 2359304 | tf_op jit(solution)/shard_map/ppermute | solution.py:64
  370.5 22.9 %collective-permute-start.43 = (bf16[4,2,96,384]{3,2,1,0:T(8,128)(2,1)}, bf16[4,2,96,384]{3,2,1,0:T(8,128)(2,1)}, u32[]{:S(2)}, u32[]{:S(2)}) collective-permute-start(bf16[4,2,96,384]{3,2,1,0:T(8,128)(2,1)} %fusion.42), channel_id=1, source_target_pairs={{0,2},{1,3},{2,0},{3,1},{4,6},{5,7},{6,4},{7,5},{8,10},{9,11},{10,... | collective-permute-start | bytes 1769480 | tf_op jit(solution)/shard_map/ppermute | solution.py:64
  371.2 27.7 %collective-permute-start.46 = (bf16[64,1536]{1,0:T(8,128)(2,1)}, bf16[64,1536]{1,0:T(8,128)(2,1)}, u32[]{:S(2)}, u32[]{:S(2)}) collective-permute-start(bf16[64,1536]{1,0:T(8,128)(2,1)} %dynamic-slice_bitcast_fusion.17), channel_id=1, source_target_pairs={{0,2},{1,3},{2,0},{3,1},{4,6},{5,7},{6,4},{7,5},{8,10},{9,11},{10,... | collective-permute-start | bytes 589832 | tf_op jit(solution)/shard_map/ppermute | solution.py:64
  372.7 14.7 %collective-permute-start.42 = (bf16[4,2,64,384]{3,2,0,1:T(8,128)(2,1)}, bf16[4,2,64,384]{3,2,0,1:T(8,128)(2,1)}, u32[]{:S(2)}, u32[]{:S(2)}) collective-permute-start(bf16[4,2,64,384]{3,2,0,1:T(8,128)(2,1)} %bitcast.468), channel_id=1, source_target_pairs={{0,4},{4,0},{8,12},{12,8},{16,20},{20,16},{24,28},{28,24},{1,5},{5... | collective-permute-start | bytes 1179656 | tf_op jit(solution)/shard_map/ppermute | solution.py:64
  377.9 21.0 %collective-permute-start.47 = (bf16[64,1536]{1,0:T(8,128)(2,1)}, bf16[64,1536]{1,0:T(8,128)(2,1)S(1)}, u32[]{:S(2)}, u32[]{:S(2)}) collective-permute-start(bf16[64,1536]{1,0:T(8,128)(2,1)} %get-tuple-element.310), channel_id=1, source_target_pairs={{0,8},{4,12},{8,16},{12,20},{16,24},{20,28},{24,0},{28,4},{1,9},{5... | collective-permute-start | bytes 589832 | tf_op jit(solution)/shard_map/ppermute | solution.py:64
  387.0 12.7 %collective-permute-start.48 = (bf16[64,1536]{1,0:T(8,128)(2,1)}, bf16[64,1536]{1,0:T(8,128)(2,1)S(1)}, u32[]{:S(2)}, u32[]{:S(2)}) collective-permute-start(bf16[64,1536]{1,0:T(8,128)(2,1)} %get-tuple-element.311), channel_id=1, source_target_pairs={{0,16},{4,20},{8,24},{12,28},{16,0},{20,4},{24,8},{28,12},{1,17},{... | collective-permute-start | bytes 589832 | tf_op jit(solution)/shard_map/ppermute | solution.py:64
  387.4 13.9 %collective-permute-start.49 = (bf16[64,1536]{1,0:T(8,128)(2,1)S(1)}, bf16[64,1536]{1,0:T(8,128)(2,1)S(1)}, u32[]{:S(2)}, u32[]{:S(2)}) collective-permute-start(bf16[64,1536]{1,0:T(8,128)(2,1)S(1)} %get-tuple-element.312), channel_id=1, source_target_pairs={{0,24},{4,28},{8,0},{12,4},{16,8},{20,12},{24,16},{28,20},{1,25},{... | collective-permute-start | bytes 589832 | tf_op jit(solution)/shard_map/ppermute | solution.py:64
  404.4 9.9 %collective-permute-start.51 = (bf16[4,96,384]{2,1,0:T(8,128)(2,1)S(1)}, bf16[4,96,384]{2,1,0:T(8,128)(2,1)S(1)}, u32[]{:S(2)}, u32[]{:S(2)}) collective-permute-start(bf16[4,96,384]{2,1,0:T(8,128)(2,1)S(1)} %dynamic-slice_bitcast_fusion.10), channel_id=1, source_target_pairs={{0,4},{4,0},{8,12},{12,8},{16,20},{20,16},{24,28},{28,24},{1,5},{5... | collective-permute-start | bytes 884744 | tf_op jit(solution)/shard_map/ppermute | solution.py:64
  404.6 18.5 %collective-permute-start.52 = (bf16[4,96,512]{2,1,0:T(8,128)(2,1)S(1)}, bf16[4,96,512]{2,1,0:T(8,128)(2,1)S(1)}, u32[]{:S(2)}, u32[]{:S(2)}) collective-permute-start(bf16[4,96,512]{2,1,0:T(8,128)(2,1)S(1)} %dynamic-slice_bitcast_fusion.6), channel_id=1, source_target_pairs={{0,2},{1,3},{2,0},{3,1},{4,6},{5,7},{6,4},{7,5},{8,10},{9,11},{10,... | collective-permute-start | bytes 1179656 | tf_op jit(solution)/shard_map/ppermute | solution.py:64
  404.9 19.8 %collective-permute-start.53 = (bf16[4,64,768]{2,1,0:T(8,128)(2,1)S(1)}, bf16[4,64,768]{2,1,0:T(8,128)(2,1)S(1)}, u32[]{:S(2)}, u32[]{:S(2)}) collective-permute-start(bf16[4,64,768]{2,1,0:T(8,128)(2,1)S(1)} %dynamic-slice_bitcast_fusion.5), channel_id=1, source_target_pairs={{0,4},{4,0},{8,12},{12,8},{16,20},{20,16},{24,28},{28,24},{1,5},{5... | collective-permute-start | bytes 1179656 | tf_op jit(solution)/shard_map/ppermute | solution.py:64
  416.9 11.8 %collective-permute-start.68 = (f32[64,1536]{1,0:T(8,128)S(1)}, f32[64,1536]{1,0:T(8,128)}, u32[]{:S(2)}, u32[]{:S(2)}) collective-permute-start(f32[64,1536]{1,0:T(8,128)S(1)} %pad_maximum_fusion.24), channel_id=1, source_target_pairs={{0,1},{1,0},{2,3},{3,2},{4,5},{5,4},{6,7},{7,6},{8,9},{9,8},{10,11... | collective-permute-start | bytes 1179656 | tf_op jit(solution)/shard_map/ppermute | solution.py:41
  417.7 17.7 %collective-permute-start.66 = (bf16[160,384]{1,0:T(8,128)(2,1)}, bf16[160,384]{1,0:T(8,128)(2,1)}, u32[]{:S(2)}, u32[]{:S(2)}) collective-permute-start(bf16[160,384]{1,0:T(8,128)(2,1)} %get-tuple-element.335), channel_id=1, source_target_pairs={{0,24},{4,28},{8,0},{12,4},{16,8},{20,12},{24,16},{28,20},{1,25},{... | collective-permute-start | bytes 368648 | tf_op jit(solution)/shard_map/ppermute | solution.py:64
  421.8 15.7 %collective-permute-start.65 = (bf16[160,384]{1,0:T(8,128)(2,1)}, bf16[160,384]{1,0:T(8,128)(2,1)}, u32[]{:S(2)}, u32[]{:S(2)}) collective-permute-start(bf16[160,384]{1,0:T(8,128)(2,1)} %get-tuple-element.334), channel_id=1, source_target_pairs={{0,16},{4,20},{8,24},{12,28},{16,0},{20,4},{24,8},{28,12},{1,17},{... | collective-permute-start | bytes 368648 | tf_op jit(solution)/shard_map/ppermute | solution.py:64
  423.1 14.4 %collective-permute-start.64 = (bf16[160,384]{1,0:T(8,128)(2,1)}, bf16[160,384]{1,0:T(8,128)(2,1)}, u32[]{:S(2)}, u32[]{:S(2)}) collective-permute-start(bf16[160,384]{1,0:T(8,128)(2,1)} %get-tuple-element.333), channel_id=1, source_target_pairs={{0,8},{4,12},{8,16},{12,20},{16,24},{20,28},{24,0},{28,4},{1,9},{5... | collective-permute-start | bytes 368648 | tf_op jit(solution)/shard_map/ppermute | solution.py:64
  424.7 10.1 %collective-permute-start.56 = (f32[9728]{0:T(1024)S(1)}, f32[9728]{0:T(1024)S(1)}, u32[]{:S(2)}, u32[]{:S(2)}) collective-permute-start(f32[9728]{0:T(1024)S(1)} %add.465), channel_id=1, source_target_pairs={{0,2},{1,3},{2,0},{3,1},{4,6},{5,7},{6,4},{7,5},{8,10},{9,11},{10,... | collective-permute-start | bytes 116744 | tf_op jit(solution)/shard_map/ppermute | solution.py:64
  428.6 24.7 %collective-permute-start.62 = (bf16[128,768]{1,0:T(8,128)(2,1)}, bf16[128,768]{1,0:T(8,128)(2,1)S(1)}, u32[]{:S(2)}, u32[]{:S(2)}) collective-permute-start(bf16[128,768]{1,0:T(8,128)(2,1)} %get-tuple-element.332), channel_id=1, source_target_pairs={{0,24},{4,28},{8,0},{12,4},{16,8},{20,12},{24,16},{28,20},{1,25},{... | collective-permute-start | bytes 589832 | tf_op jit(solution)/shard_map/ppermute | solution.py:64
  434.8 18.5 %collective-permute-start.61 = (bf16[128,768]{1,0:T(8,128)(2,1)S(1)}, bf16[128,768]{1,0:T(8,128)(2,1)S(1)}, u32[]{:S(2)}, u32[]{:S(2)}) collective-permute-start(bf16[128,768]{1,0:T(8,128)(2,1)S(1)} %get-tuple-element.331), channel_id=1, source_target_pairs={{0,16},{4,20},{8,24},{12,28},{16,0},{20,4},{24,8},{28,12},{1,17},{... | collective-permute-start | bytes 589832 | tf_op jit(solution)/shard_map/ppermute | solution.py:64
  435.4 11.4 %collective-permute-start.59 = (f32[9728]{0:T(1024)S(1)}, f32[9728]{0:T(1024)S(1)}, u32[]{:S(2)}, u32[]{:S(2)}) collective-permute-start(f32[9728]{0:T(1024)S(1)} %add.466), channel_id=1, source_target_pairs={{0,24},{4,28},{8,0},{12,4},{16,8},{20,12},{24,16},{28,20},{1,25},{... | collective-permute-start | bytes 116744 | tf_op jit(solution)/shard_map/ppermute | solution.py:64
  437.5 12.8 %collective-permute-start.57 = (f32[9728]{0:T(1024)S(1)}, f32[9728]{0:T(1024)S(1)}, u32[]{:S(2)}, u32[]{:S(2)}) collective-permute-start(f32[9728]{0:T(1024)S(1)} %add.466), channel_id=1, source_target_pairs={{0,8},{4,12},{8,16},{12,20},{16,24},{20,28},{24,0},{28,4},{1,9},{5... | collective-permute-start | bytes 116744 | tf_op jit(solution)/shard_map/ppermute | solution.py:64
  437.5 12.8 %collective-permute-start.58 = (f32[9728]{0:T(1024)S(1)}, f32[9728]{0:T(1024)S(1)}, u32[]{:S(2)}, u32[]{:S(2)}) collective-permute-start(f32[9728]{0:T(1024)S(1)} %add.466), channel_id=1, source_target_pairs={{0,16},{4,20},{8,24},{12,28},{16,0},{20,4},{24,8},{28,12},{1,17},{... | collective-permute-start | bytes 116744 | tf_op jit(solution)/shard_map/ppermute | solution.py:64
  (111 other events, 864.4 us)
Sparse Core Ops, SparseCore 0:
  10.9 118.7 all-gather.4
  132.6 67.6 all-gather.6
  228.3 141.9 reduce-scatter.1

commit v3 on v2

--- a/solution.py
+++ b/solution.py
@@ -14,7 +14,7 @@
 gelu_rate = 0.7978845608028654
 gelu_cube = 0.044715
 halo = 8
-vmem_bytes = 48 * 1024 * 1024
+mib = 1024 * 1024
 
 
 def grid_axes():
@@ -169,37 +169,56 @@
 
 
 def scan_rows(a, b, reverse):
-    count = a.shape[0]
-    row = lax.broadcasted_iota(jnp.int32, a.shape, 0)
+    count, width = a.shape
+    a, b = a.reshape(-1, 8, width), b.reshape(-1, 8, width)
+    row = lax.broadcasted_iota(jnp.int32, a.shape, 1)
+    for s in (1, 2, 4):
+        shift = 8 - s if reverse else s
+        valid = row < 8 - s if reverse else row >= s
+        a_far = pltpu.roll(a, shift, 1)
+        b_far = pltpu.roll(b, shift, 1)
+        b = jnp.where(valid, a * b_far + b, b)
+        a = jnp.where(valid, a * a_far, a)
+    edge = 0 if reverse else 7
+    a_all, b_all = a[:, edge], b[:, edge]
+    groups = count // 8
+    one, zero = jnp.ones_like(a_all[:1]), jnp.zeros_like(a_all[:1])
     s = 1
-    while s < count:
-        if s < 8:
-            shift = count - s if reverse else s
-            valid = row < count - s if reverse else row >= s
-            a_far = pltpu.roll(a, shift, 0)
-            b_far = pltpu.roll(b, shift, 0)
-            b = jnp.where(valid, a * b_far + b, b)
-            a = jnp.where(valid, a * a_far, a)
-        elif reverse:
-            b = jnp.concatenate([a[:-s] * b[s:] + b[:-s], b[-s:]], axis=0)
-            a = jnp.concatenate([a[:-s] * a[s:], a[-s:]], axis=0)
+    while s < groups:
+        if reverse:
+            a_far = jnp.concatenate([a_all[s:], jnp.broadcast_to(one, (s, width))], axis=0)
+            b_far = jnp.concatenate([b_all[s:], jnp.broadcast_to(zero, (s, width))], axis=0)
         else:
-            b = jnp.concatenate([b[:s], a[s:] * b[:-s] + b[s:]], axis=0)
-            a = jnp.concatenate([a[:s], a[s:] * a[:-s]], axis=0)
+            a_far = jnp.concatenate([jnp.broadcast_to(one, (s, width)), a_all[:-s]], axis=0)
+            b_far = jnp.concatenate([jnp.broadcast_to(zero, (s, width)), b_all[:-s]], axis=0)
+        b_all = a_all * b_far + b_all
+        a_all = a_all * a_far
         s *= 2
-    return a, b
+    if reverse:
+        a_in = jnp.concatenate([a_all[1:], one], axis=0)
+        b_in = jnp.concatenate([b_all[1:], zero], axis=0)
+    else:
+        a_in = jnp.concatenate([one, a_all[:-1]], axis=0)
+        b_in = jnp.concatenate([zero, b_all[:-1]], axis=0)
+    b = a * b_in[:, None] + b
+    a = a * a_in[:, None]
+    return a.reshape(count, width), b.reshape(count, width)
+
+
+def sigmoid(x):
+    return 0.5 + 0.5 * jnp.tanh(0.5 * x)
 
 
 def minus_expm1(x):
-    t = 1.0 + x * (1.0 / 8.0)
-    for k in (7.0, 6.0, 5.0, 4.0, 3.0, 2.0):
-        t = 1.0 + x * (1.0 / k) * t
-    return jnp.where(x > -0.4, -x * t, 1.0 - jnp.exp(x))
+    t = 1.0 / 5040.0
+    for k in (720.0, 120.0, 24.0, 6.0, 2.0):
+        t = t * x + 1.0 / k
+    return -x * (t * x + 1.0)
 
 
 def gate_values(conv_low, rec_w, inp_w, rate, reset):
-    r = jax.nn.sigmoid(jnp.dot(conv_low, rec_w, preferred_element_type=f32))
-    g = jax.nn.sigmoid(jnp.dot(conv_low, inp_w, preferred_element_type=f32))
+    r = sigmoid(jnp.dot(conv_low, rec_w, preferred_element_type=f32))
+    g = sigmoid(jnp.dot(conv_low, inp_w, preferred_element_type=f32))
     log_keep = rate * (0.1 + 0.9 * r)
     keep = jnp.where(reset, 0.0, jnp.exp(log_keep))
     lost = minus_expm1(2.0 * log_keep)
@@ -346,12 +365,12 @@
         in_specs=[spec(a.shape) for a in ins],
         out_specs=[spec(o.shape) for o in outs],
         out_shape=outs,
-        compiler_params=pltpu.CompilerParams(vmem_limit_bytes=vmem_bytes),
+        compiler_params=pltpu.CompilerParams(vmem_limit_bytes=14 * mib),
         cost_estimate=pl.CostEstimate(flops=flops, bytes_accessed=1, transcendentals=0),
     )(*ins)
 
 
-def feature_call(kernel, core, grid, ins, in_specs, outs, out_specs, scratch=()):
+def feature_call(kernel, room, core, grid, ins, in_specs, outs, out_specs, scratch=()):
     return pl.pallas_call(
         kernel,
         grid_spec=pltpu.PrefetchScalarGridSpec(
@@ -362,7 +381,7 @@
             scratch_shapes=list(scratch),
         ),
         out_shape=outs,
-        compiler_params=pltpu.CompilerParams(vmem_limit_bytes=vmem_bytes),
+        compiler_params=pltpu.CompilerParams(vmem_limit_bytes=48 * mib),
         cost_estimate=pl.CostEstimate(flops=1, bytes_accessed=1, transcendentals=0),
     )(core, *ins)
 
@@ -376,8 +395,8 @@
     gate = jnp.dot(normed, gate_w_ref[...], preferred_element_type=f32)
     up = jnp.dot(normed, up_w_ref[...], preferred_element_type=f32)
     value, slope = gelu_parts(gate)
-    act_ref[...] = value
-    rise_ref[...] = up * slope
+    act_ref[...] = value.astype(bf16)
+    rise_ref[...] = (up * slope).astype(bf16)
     hidden_ref[...] = (value * up).astype(bf16)
 
 
@@ -638,7 +657,7 @@
     middle = inputs + jnp.dot(mixed, full_branch, preferred_element_type=f32)
     scale_mid = norm_scale(middle)
     normed_mid = (middle * scale_mid * gain_mid).astype(bf16)
-    tile = 512
+    tile = 768
     tiles = ff_width // tile
     tokens_model = (token_count, model_width)
     tokens_tile = (token_count, tile)
@@ -653,6 +672,7 @@
     plain = pl.BlockSpec(tokens_tile, lambda j, core: (0, j))
     mlp_act, mlp_rise, hidden = feature_call(
         mlp_kernel,
+        22,
         core_number,
         tiles,
         [normed_mid, full_mlp, full_mlp],
@@ -662,8 +682,8 @@
             pl.BlockSpec((model_width, tile), lambda j, core: (0, j + tiles)),
         ],
         [
-            array((token_count, ff_width), f32),
-            array((token_count, ff_width), f32),
+            array((token_count, ff_width), bf16),
+            array((token_count, ff_width), bf16),
             array((token_count, ff_width), bf16),
         ],
         [plain, plain, plain],
@@ -719,6 +739,7 @@
     half_array = array((token_count, ff_width // 2), bf16)
     gate_my, gate_other, up_my, up_other = feature_call(
         hidden_grad_kernel,
+        18,
         core_number,
         tiles,
         [after(out_grad, down_grad), full_mlp_down, mlp_act, mlp_rise],
@@ -739,6 +760,7 @@
     up_grad_half = jnp.concatenate([up_my, swap_cores(up_other)], axis=0)
     (block_out,) = feature_call(
         down_kernel,
+        16,
         core_number,
         tiles,
         [hidden, full_mlp_down, middle],
@@ -765,6 +787,7 @@
     tokens_half = (token_count, model_width // 2)
     middle_grad, middle_low, middle_my, middle_other, gain_mid_grad = feature_call(
         middle_kernel,
+        32,
         core_number,
         tiles,
         [

time: 474 us -> 471 us (level)
  Pallas kernels: 96.4 us -> 84.5 us
  local copies, waits for them, and re-layouts: 55.7 us -> 62.4 us
    unnamed x180 -> x194, local copies, waits for them, and re-layouts: 16.6 us -> 25.3 us
    pallas_call x3, Pallas kernels: 46.7 us -> 39.8 us  [channel_call(): pl.pallas_call(functools.partial(kernel, row_count), grid=(width // block...]
    pallas_call x4, Pallas kernels: 49.7 us -> 44.7 us  [feature_call(): pl.pallas_call(kernel, grid_spec=pltpu.PrefetchScalarGridSpec(num_scalar_...]
  transfers between devices with their start and end apart: 72 -> 72, of which waited for: 18 -> 18; matrix products, arithmetic and copies ran while one was open for 30% -> 30% of each run, Pallas kernels for 21% -> 18%
where the time goes in v3:
time: 471 us; the launch traced here: 463 us
  starting transfers between devices  102 us (22%)
  Pallas kernels  84.5 us (18%)
  waiting for transfers between devices  69.2 us (15%)
  local copies, waits for them, and re-layouts  62.4 us (13%)
  other arithmetic  58.5 us (12%)
  matrix products  45.5 us (10%)
  blocking collectives  24.6 us (5%)
  between operations  16.1 us (3%)
    ppermute x54, starting transfers between devices, hop(): return lax.ppermute(block, name, route)  92.7 us
    ppermute x54, waiting for transfers between devices, hop(): return lax.ppermute(block, name, route)  56.4 us
    pallas_call x4, Pallas kernels, feature_call(): pl.pallas_call(kernel, grid_spec=pltpu.PrefetchScalarGridSpec(num_scalar_...  44.7 us
    pallas_call x3, Pallas kernels, channel_call(): pl.pallas_call(functools.partial(kernel, row_count), grid=(width // block...  39.8 us
    dot_general x6, matrix products, chip_grad(): lax.dot_general(left_rows, right_half, (((0,), (0,)), ((), ())), preferre...  26.3 us
    unnamed x194, local copies, waits for them, and re-layouts  25.3 us
    all_gather x2, blocking collectives, carry_before(): both = lax.all_gather(jnp.stack([factor, value]), 'seq')  24.6 us
    another operation x24, other arithmetic, finish(): jnp.stack([jnp.where(first, a, b), jnp.where(first, b, a)], axis=spot)  15.3 us
  transfers between devices with their start and end apart: 72, of which 18 were waited for; matrix products, arithmetic and copies ran while one was open for 30% of the time, Pallas kernels for 18%

profile of v3, /device:TPU:0, one launch (start us, length us, event | category | flops | bytes accessed | tf_op | source)
XLA Modules:
  0.0 462.6 jit_solution(15827241252123254246)
XLA Ops:
  9.9 3.5 concatenate.82
  14.3 3.1 collective-permute-start
  17.4 2.6 collective-permute-start.1
  22.4 2.9 collective-permute-start.5
  25.4 4.3 collective-permute-done.3
  29.7 4.6 collective-permute-done.4
  37.5 4.2 collective-permute-start.10
  46.5 4.7 %collective-permute-start.13 = (bf16[48,1024]{1,0:T(8,128)(2,1)S(1)}, bf16[48,1024]{1,0:T(8,128)(2,1)S(1)}, u32[]{:S(2)}, u32[]{:S(2)}) collective-permute-start(bf16[48,1024]{1,0:T(8,128)(2,1)S(1)} %copy-done.88), channel_id=1, source_target_pairs={{0,8},{4,12},{8,16},{12,20},{16,24},{20,28},{24,0},{28,4},{1,9},{5... | collective-permute-start | bytes 294920 | tf_op jit(solution)/shard_map/ppermute | solution.py:64
  55.6 2.6 collective-permute-done.13
  58.2 5.8 %collective-permute-done.14 = bf16[48,1024]{1,0:T(8,128)(2,1)S(1)} collective-permute-done((bf16[48,1024]{1,0:T(8,128)(2,1)S(1)}, bf16[48,1024]{1,0:T(8,128)(2,1)S(1)}, u32[]{:S(2)}, u32[]{:S(2)}) %collective-permute-start.14) | collective-permute-done | bytes 98336 | tf_op jit(solution)/shard_map/ppermute | solution.py:64
  70.3 2.4 collective-permute-start.18
  72.8 2.5 collective-permute-start.19
  76.7 2.4 collective-permute-start.20
  79.1 2.4 collective-permute-start.21
  97.1 12.5 %shard_map.254 = (bf16[512,1536]{1,0:T(8,128)(2,1)S(1)}, f32[512,1536]{1,0:T(8,128)S(1)}, f32[512,1536]{1,0:T(8,128)S(1)}, f32[512,1536]{1,0:T(8,128)S(1)}) custom-call(bf16[512,1536]{1,0:T(8,128)(2,1)S(1)} %convolution_convert_fusion.4.sig_ref, f32[16,1536]{1,0:T(8,128)S(1)} %fusion.9.tail_ref.before_ref, f32[3,512,128]{2,1,0:T(8,128)S(1)} %broadcast_in_dim.107.mask_ref, ...), custom_call_target="tpu_custom_call" | custom-call | flops 1 | bytes 1 | tf_op jit(solution)/shard_map/pallas_call | solution.py:362
  112.5 5.5 %all-gather = f32[8,2,1536]{2,1,0:T(2,128)S(1)} all-gather(f32[2,2,1536]{2,1,0:T(2,128)S(1)} %pad_maximum_fusion.33), channel_id=2, replica_groups=mesh['dp'=8,'seq'=4] {'seq'}, dimensions={0}, use_global_device_ids=true | all-gather | bytes 122880 | tf_op jit(solution)/shard_map/all_gather | solution.py:503
  121.3 19.2 %collective-permute-done.22 = bf16[4,2,32,1536]{3,2,1,0:T(8,128)(2,1)S(1)} collective-permute-done((bf16[4,2,32,1536]{3,2,1,0:T(8,128)(2,1)S(1)}, bf16[4,2,32,1536]{3,2,1,0:T(8,128)(2,1)S(1)}, u32[]{:S(2)}, u32[]{:S(2)}) %collective-permute-start.22) | collective-permute-done | bytes 786464 | tf_op jit(solution)/shard_map/ppermute | solution.py:64
  144.6 2.9 collective-permute-done.24
  151.7 2.7 copy-done.21
  155.3 4.7 %fusion.5 = (bf16[512,1536]{1,0:T(8,128)(2,1)}, f32[512,1536]{1,0:T(8,128)S(1)}, f32[512,1536]{1,0:T(8,128)}) fusion(f32[512,1536]{1,0:T(8,128)S(1)} %copy-done.23, f32[512,1536]{1,0:T(8,128)S(1)} %copy-done.21, f32[2,1536]{1,0:T(2,128)S(1)} %fusion.83.state_in_ref, bf16[512,1024]{1,0:T(8,128)(2,1)S(1)} %bitcast.443, bf16[1024,1536]{1,0:T(8,128)(2,1)S(1)} %bitcast.434), kind=kOutput, calls=%fused_computation.9 | convolution fusion | flops 1620049920 | bytes 18362368 | tf_op jit(solution)/shard_map/dot_general | solution.py:653
  163.2 3.5 multiply_reduce_fusion
  169.2 13.0 %shard_map.255 = (bf16[512,3072]{1,0:T(8,128)(2,1)S(1)}, bf16[512,3072]{1,0:T(8,128)(2,1)}, bf16[512,3072]{1,0:T(8,128)(2,1)}) custom-call(s32[1]{0:T(128)} %bitcast.core_ref, bf16[512,1024]{1,0:T(8,128)(2,1)} %multiply_convert_fusion.normed_ref, bf16[1024,6144]{1,0:T(8,128)(2,1)} %all-gather.5.cloned.1.call-done.gate_w_ref.up_w_ref, ...), custom_call_target="tpu_custom_call" | custom-call | flops 1 | bytes 1 | tf_op jit(solution)/shard_map/pallas_call | solution.py:374
  183.9 7.3 %convolution_convert_fusion = bf16[3072,1024]{1,0:T(8,128)(2,1)} fusion(bf16[512,3072]{1,0:T(8,128)(2,1)} %get-tuple-element.242.hidden_ref, bf16[512,1024]{1,0:T(8,128)(2,1)S(1)} %bitcast.424), kind=kOutput, calls=%fused_computation | convolution fusion | flops 3224371200 | bytes 10485760 | tf_op jit(solution)/shard_map/dot_general | solution.py:694
  191.2 10.0 %all-gather.7.cloned.1.call-done.down_ref = bf16[3072,1024]{1,0:T(8,128)(2,1)} async-done(((bf16[96,1024]{1,0:T(8,128)(2,1)}), bf16[3072,1024]{1,0:T(8,128)(2,1)}) %all-gather.7.cloned.1.call-update) | async-done | bytes 6291472 | tf_op jit(solution)/shard_map/all_gather | solution.py:558
  202.4 9.1 %shard_map.256 = (bf16[512,1536]{1,0:T(8,128)(2,1)S(1)}, bf16[512,1536]{1,0:T(8,128)(2,1)}, bf16[512,1536]{1,0:T(8,128)(2,1)S(1)}, bf16[512,1536]{1,0:T(8,128)(2,1)}) custom-call(s32[1]{0:T(128)} %bitcast.core_ref, bf16[512,1024]{1,0:T(8,128)(2,1)S(1)} %bitcast.425, bf16[3072,1024]{1,0:T(8,128)(2,1)} %all-gather.7.cloned.1.call-done.down_ref, ...), custom_call_target="tpu_custom_call" | custom-call | flops 1 | bytes 1 | tf_op jit(solution)/shard_map/pallas_call | solution.py:374
  219.1 3.1 pad_maximum_fusion.7
  222.1 3.8 pad_maximum_fusion.5
  229.5 7.7 %shard_map.257 = f32[512,1024]{1,0:T(8,128)} custom-call(s32[1]{0:T(128)} %bitcast.core_ref, bf16[512,3072]{1,0:T(8,128)(2,1)S(1)} %copy-done.26, bf16[3072,1024]{1,0:T(8,128)(2,1)} %all-gather.7.cloned.1.call-done.down_ref, f32[512,1024]{1,0:T(8,128)S(1)} %copy-done.1), custom_call_target="tpu_custom_call" | custom-call | flops 1 | bytes 1 | tf_op jit(solution)/shard_map/pallas_call | solution.py:374
  241.2 3.9 convolution_convert_fusion.2
  245.1 3.9 convolution_convert_fusion.1
  253.5 15.0 %shard_map.258 = (f32[512,1024]{1,0:T(8,128)}, bf16[512,1024]{1,0:T(8,128)(2,1)S(1)}, bf16[512,512]{1,0:T(8,128)(2,1)S(1)}, bf16[512,512]{1,0:T(8,128)(2,1)}, f32[1,1024]{1,0:T(1,128)S(1)}) custom-call(s32[1]{0:T(128)} %bitcast.core_ref, bf16[512,1536]{1,0:T(8,128)(2,1)S(1)} %copy-done.6, bf16[512,1536]{1,0:T(8,128)(2,1)} %get-tuple-element.244.gate_other, ...), custom_call_target="tpu_custom_call" | custom-call | flops 1 | bytes 1 | tf_op jit(solution)/shard_map/pallas_call | solution.py:374
  271.6 9.6 %shard_map.259 = (bf16[512,1536]{1,0:T(8,128)(2,1)S(1)}, f32[512,1536]{1,0:T(8,128)S(1)}, f32[512,1536]{1,0:T(8,128)S(1)}) custom-call(f32[512,1536]{1,0:T(8,128)S(1)} %fusion.116.mixed_grad_ref, f32[512,1536]{1,0:T(8,128)S(1)} %get-tuple-element.348.states_ref, f32[512,1536]{1,0:T(8,128)S(1)} %copy-done.2, f32[512,1536]{1,0:T(8,128)S(1)} %copy-done.25), custom_call_target="tpu_custom_call" | custom-call | flops 1 | bytes 1 | tf_op jit(solution)/shard_map/pallas_call | solution.py:362
  283.0 19.0 %all-gather.1 = f32[8,2,1536]{2,1,0:T(2,128)S(1)} all-gather(f32[2,2,1536]{2,1,0:T(2,128)S(1)} %pad_maximum_fusion.34), channel_id=3, replica_groups=mesh['dp'=8,'seq'=4] {'seq'}, dimensions={0}, use_global_device_ids=true | all-gather | bytes 122880 | tf_op jit(solution)/shard_map/all_gather | solution.py:503
  311.9 4.1 convolution_convert_fusion.3
  316.1 2.6 collective-permute-start.37
  318.8 3.5 convolution_convert_fusion.7
  325.2 17.7 %shard_map.260 = (f32[512,1536]{1,0:T(8,128)S(1)}, f32[16,1536]{1,0:T(8,128)S(1)}, f32[1536,128]{1,0:T(8,128)S(1)}, f32[1536,128]{1,0:T(8,128)S(1)}, f32[5,1536]{1,0:T(8,128)S(1)}) custom-call(bf16[512,1536]{1,0:T(8,128)(2,1)S(1)} %copy-done.10, f32[16,1536]{1,0:T(8,128)S(1)} %copy-done.33, f32[3,512,128]{2,1,0:T(8,128)S(1)} %copy-done.4, ...), custom_call_target="tpu_custom_call" | custom-call | flops 1 | bytes 1 | tf_op jit(solution)/shard_map/pallas_call | solution.py:362
  342.9 4.6 collective-permute-done.36
  357.9 3.1 fusion.117
  361.4 3.7 convolution_convert_fusion.6
  371.0 3.7 fusion.32
  375.2 9.1 %collective-permute-start.47 = (bf16[64,1536]{1,0:T(8,128)(2,1)}, bf16[64,1536]{1,0:T(8,128)(2,1)S(1)}, u32[]{:S(2)}, u32[]{:S(2)}) collective-permute-start(bf16[64,1536]{1,0:T(8,128)(2,1)} %get-tuple-element.310), channel_id=1, source_target_pairs={{0,8},{4,12},{8,16},{12,20},{16,24},{20,28},{24,0},{28,4},{1,9},{5... | collective-permute-start | bytes 589832 | tf_op jit(solution)/shard_map/ppermute | solution.py:64
  384.6 6.2 %collective-permute-start.49 = (bf16[64,1536]{1,0:T(8,128)(2,1)S(1)}, bf16[64,1536]{1,0:T(8,128)(2,1)S(1)}, u32[]{:S(2)}, u32[]{:S(2)}) collective-permute-start(bf16[64,1536]{1,0:T(8,128)(2,1)S(1)} %get-tuple-element.312), channel_id=1, source_target_pairs={{0,24},{4,28},{8,0},{12,4},{16,8},{20,12},{24,16},{28,20},{1,25},{... | collective-permute-start | bytes 589832 | tf_op jit(solution)/shard_map/ppermute | solution.py:64
  399.4 2.4 collective-permute-start.50
  407.8 4.0 collective-permute-done.51
  415.2 3.5 collective-permute-start.66
  434.6 8.4 %collective-permute-start.58 = (f32[9728]{0:T(1024)S(1)}, f32[9728]{0:T(1024)S(1)}, u32[]{:S(2)}, u32[]{:S(2)}) collective-permute-start(f32[9728]{0:T(1024)S(1)} %add.466), channel_id=1, source_target_pairs={{0,16},{4,20},{8,24},{12,28},{16,0},{20,4},{24,8},{28,12},{1,17},{... | collective-permute-start | bytes 116744 | tf_op jit(solution)/shard_map/ppermute | solution.py:64
  444.1 3.4 collective-permute-start.60
  (504 shorter events, 162.2 us)
Async XLA Ops:
  7.2 162.0 %all-gather.5.cloned.1.call-start = ((), (), s32[]{:S(2)}) async-start(), calls=%async_computation.1 | async-start | bytes 12976128 | tf_op jit(solution)/shard_map/all_gather | solution.py:557
  9.1 192.1 %all-gather.7.cloned.1.call-start = ((), (), s32[]{:S(2)}) async-start(), calls=%async_computation.2 | async-start | bytes 6488064 | tf_op jit(solution)/shard_map/all_gather | solution.py:558
  22.0 12.2 %collective-permute-start.4 = (bf16[32,1280]{1,0:T(8,128)(2,1)S(1)}, bf16[32,1280]{1,0:T(8,128)(2,1)S(1)}, u32[]{:S(2)}, u32[]{:S(2)}) collective-permute-start(bf16[32,1280]{1,0:T(8,128)(2,1)S(1)} %pad_maximum_fusion.32), channel_id=1, source_target_pairs={{0,16},{4,20},{8,24},{12,28},{16,0},{20,4},{24,8},{28,12},{1,17},{... | collective-permute-start | bytes 245768 | tf_op jit(solution)/shard_map/ppermute | solution.py:64
  22.4 11.9 %collective-permute-start.5 = (bf16[32,1280]{1,0:T(8,128)(2,1)S(1)}, bf16[32,1280]{1,0:T(8,128)(2,1)S(1)}, u32[]{:S(2)}, u32[]{:S(2)}) collective-permute-start(bf16[32,1280]{1,0:T(8,128)(2,1)S(1)} %pad_maximum_fusion.32), channel_id=1, source_target_pairs={{0,24},{4,28},{8,0},{12,4},{16,8},{20,12},{24,16},{28,20},{1,25},{... | collective-permute-start | bytes 245768 | tf_op jit(solution)/shard_map/ppermute | solution.py:64
  44.4 19.7 %collective-permute-start.8 = (bf16[4,2,32,768]{3,2,1,0:T(8,128)(2,1)S(1)}, bf16[4,2,32,768]{3,2,1,0:T(8,128)(2,1)S(1)}, u32[]{:S(2)}, u32[]{:S(2)}) collective-permute-start(bf16[4,2,32,768]{3,2,1,0:T(8,128)(2,1)S(1)} %pad_maximum_fusion.22), channel_id=1, source_target_pairs={{0,4},{4,0},{8,12},{12,8},{16,20},{20,16},{24,28},{28,24},{1,5},{5... | collective-permute-start | bytes 1179656 | tf_op jit(solution)/shard_map/ppermute | solution.py:64
  45.0 19.1 %collective-permute-start.9 = (bf16[4,2,32,1280]{3,2,1,0:T(8,128)(2,1)S(1)}, bf16[4,2,32,1280]{3,2,1,0:T(8,128)(2,1)S(1)}, u32[]{:S(2)}, u32[]{:S(2)}) collective-permute-start(bf16[4,2,32,1280]{3,2,1,0:T(8,128)(2,1)S(1)} %pad_maximum_fusion.21), channel_id=1, source_target_pairs={{0,2},{1,3},{2,0},{3,1},{4,6},{5,7},{6,4},{7,5},{8,10},{9,11},{10,... | collective-permute-start | bytes 1966088 | tf_op jit(solution)/shard_map/ppermute | solution.py:64
  46.5 11.7 %collective-permute-start.13 = (bf16[48,1024]{1,0:T(8,128)(2,1)S(1)}, bf16[48,1024]{1,0:T(8,128)(2,1)S(1)}, u32[]{:S(2)}, u32[]{:S(2)}) collective-permute-start(bf16[48,1024]{1,0:T(8,128)(2,1)S(1)} %copy-done.88), channel_id=1, source_target_pairs={{0,8},{4,12},{8,16},{12,20},{16,24},{20,28},{24,0},{28,4},{1,9},{5... | collective-permute-start | bytes 294920 | tf_op jit(solution)/shard_map/ppermute | solution.py:64
  51.2 12.8 %collective-permute-start.14 = (bf16[48,1024]{1,0:T(8,128)(2,1)S(1)}, bf16[48,1024]{1,0:T(8,128)(2,1)S(1)}, u32[]{:S(2)}, u32[]{:S(2)}) collective-permute-start(bf16[48,1024]{1,0:T(8,128)(2,1)S(1)} %copy-done.88), channel_id=1, source_target_pairs={{0,16},{4,20},{8,24},{12,28},{16,0},{20,4},{24,8},{28,12},{1,17},{... | collective-permute-start | bytes 294920 | tf_op jit(solution)/shard_map/ppermute | solution.py:64
  53.1 11.0 %collective-permute-start.15 = (bf16[48,1024]{1,0:T(8,128)(2,1)S(1)}, bf16[48,1024]{1,0:T(8,128)(2,1)S(1)}, u32[]{:S(2)}, u32[]{:S(2)}) collective-permute-start(bf16[48,1024]{1,0:T(8,128)(2,1)S(1)} %copy-done.88), channel_id=1, source_target_pairs={{0,24},{4,28},{8,0},{12,4},{16,8},{20,12},{24,16},{28,20},{1,25},{... | collective-permute-start | bytes 294920 | tf_op jit(solution)/shard_map/ppermute | solution.py:64
  70.3 11.2 %collective-permute-start.17 = (bf16[4,2,2,32,1280]{4,3,2,1,0:T(8,128)(2,1)}, bf16[4,2,2,32,1280]{4,3,2,1,0:T(8,128)(2,1)}, u32[]{:S(2)}, u32[]{:S(2)}) collective-permute-start(bf16[4,2,2,32,1280]{4,3,2,1,0:T(8,128)(2,1)} %pad_maximum_fusion.14), channel_id=1, source_target_pairs={{0,1},{1,0},{2,3},{3,2},{4,5},{5,4},{6,7},{7,6},{8,9},{9,8},{10,11... | collective-permute-start | bytes 3932168 | tf_op jit(solution)/shard_map/ppermute | solution.py:64
  75.4 299.8 %reduce-scatter.2.cloned.1.call-start = ((), (), s32[]{:S(2)}) async-start(), calls=%async_computation.3 | async-start | bytes 6488064 | tf_op jit(solution)/shard_map/reduce_scatter | solution.py:735
  76.7 41.4 %collective-permute-start.20 = (bf16[4,32,1536]{2,1,0:T(8,128)(2,1)}, bf16[4,32,1536]{2,1,0:T(8,128)(2,1)}, u32[]{:S(2)}, u32[]{:S(2)}) collective-permute-start(bf16[4,32,1536]{2,1,0:T(8,128)(2,1)} %bitcast_dynamic-update-slice_fusion.4), channel_id=1, source_target_pairs={{0,4},{4,0},{8,12},{12,8},{16,20},{20,16},{24,28},{28,24},{1,5},{5... | collective-permute-start | bytes 1179656 | tf_op jit(solution)/shard_map/ppermute | solution.py:64
  79.1 39.0 %collective-permute-start.21 = (bf16[4,48,1024]{2,1,0:T(8,128)(2,1)}, bf16[4,48,1024]{2,1,0:T(8,128)(2,1)}, u32[]{:S(2)}, u32[]{:S(2)}) collective-permute-start(bf16[4,48,1024]{2,1,0:T(8,128)(2,1)} %bitcast_dynamic-update-slice_fusion), channel_id=1, source_target_pairs={{0,2},{1,3},{2,0},{3,1},{4,6},{5,7},{6,4},{7,5},{8,10},{9,11},{10,... | collective-permute-start | bytes 1179656 | tf_op jit(solution)/shard_map/ppermute | solution.py:64
  120.6 19.9 %collective-permute-start.22 = (bf16[4,2,32,1536]{3,2,1,0:T(8,128)(2,1)S(1)}, bf16[4,2,32,1536]{3,2,1,0:T(8,128)(2,1)S(1)}, u32[]{:S(2)}, u32[]{:S(2)}) collective-permute-start(bf16[4,2,32,1536]{3,2,1,0:T(8,128)(2,1)S(1)} %pad_maximum_fusion.19), channel_id=1, source_target_pairs={{0,2},{1,3},{2,0},{3,1},{4,6},{5,7},{6,4},{7,5},{8,10},{9,11},{10,... | collective-permute-start | bytes 2359304 | tf_op jit(solution)/shard_map/ppermute | solution.py:64
  121.1 19.5 %collective-permute-start.23 = (bf16[4,2,48,1024]{3,2,1,0:T(8,128)(2,1)S(1)}, bf16[4,2,48,1024]{3,2,1,0:T(8,128)(2,1)S(1)}, u32[]{:S(2)}, u32[]{:S(2)}) collective-permute-start(bf16[4,2,48,1024]{3,2,1,0:T(8,128)(2,1)S(1)} %pad_maximum_fusion.20), channel_id=1, source_target_pairs={{0,4},{4,0},{8,12},{12,8},{16,20},{20,16},{24,28},{28,24},{1,5},{5... | collective-permute-start | bytes 2359304 | tf_op jit(solution)/shard_map/ppermute | solution.py:64
  160.1 62.1 %collective-permute-start.29 = (bf16[512,1536]{1,0:T(8,128)(2,1)}, bf16[512,1536]{1,0:T(8,128)(2,1)}, u32[]{:S(2)}, u32[]{:S(2)}) collective-permute-start(bf16[512,1536]{1,0:T(8,128)(2,1)} %get-tuple-element.347), channel_id=1, source_target_pairs={{0,1},{1,0},{2,3},{3,2},{4,5},{5,4},{6,7},{7,6},{8,9},{9,8},{10,11... | collective-permute-start | bytes 4718600 | tf_op jit(solution)/shard_map/ppermute | solution.py:41
  213.8 23.3 %collective-permute-start.26 = (bf16[512,1536]{1,0:T(8,128)(2,1)}, bf16[512,1536]{1,0:T(8,128)(2,1)}, u32[]{:S(2)}, u32[]{:S(2)}) collective-permute-start(bf16[512,1536]{1,0:T(8,128)(2,1)} %get-tuple-element.244.gate_other), channel_id=1, source_target_pairs={{0,1},{1,0},{2,3},{3,2},{4,5},{5,4},{6,7},{7,6},{8,9},{9,8},{10,11... | collective-permute-start | bytes 4718600 | tf_op jit(solution)/shard_map/ppermute | solution.py:41
  214.3 24.6 %collective-permute-start.27 = (bf16[512,1536]{1,0:T(8,128)(2,1)}, bf16[512,1536]{1,0:T(8,128)(2,1)}, u32[]{:S(2)}, u32[]{:S(2)}) collective-permute-start(bf16[512,1536]{1,0:T(8,128)(2,1)} %get-tuple-element.246.up_other), channel_id=1, source_target_pairs={{0,1},{1,0},{2,3},{3,2},{4,5},{5,4},{6,7},{7,6},{8,9},{9,8},{10,11... | collective-permute-start | bytes 4718600 | tf_op jit(solution)/shard_map/ppermute | solution.py:41
  215.4 100.7 %collective-permute-start.33 = (bf16[512,1024]{1,0:T(8,128)(2,1)}, bf16[512,1024]{1,0:T(8,128)(2,1)}, u32[]{:S(2)}, u32[]{:S(2)}) collective-permute-start(bf16[512,1024]{1,0:T(8,128)(2,1)} %copy-done.77), channel_id=1, source_target_pairs={{0,1},{1,0},{2,3},{3,2},{4,5},{5,4},{6,7},{7,6},{8,9},{9,8},{10,11... | collective-permute-start | bytes 3145736 | tf_op jit(solution)/shard_map/ppermute | solution.py:41
  251.5 51.2 %collective-permute-start.30 = (bf16[4,2,64,1536]{3,2,1,0:T(8,128)(2,1)}, bf16[4,2,64,1536]{3,2,1,0:T(8,128)(2,1)}, u32[]{:S(2)}, u32[]{:S(2)}) collective-permute-start(bf16[4,2,64,1536]{3,2,1,0:T(8,128)(2,1)} %dynamic-slice_bitcast_fusion.1), channel_id=1, source_target_pairs={{0,4},{4,0},{8,12},{12,8},{16,20},{20,16},{24,28},{28,24},{1,5},{5... | collective-permute-start | bytes 4718600 | tf_op jit(solution)/shard_map/ppermute | solution.py:64
  253.0 49.7 %collective-permute-start.31 = (bf16[4,2,64,1536]{3,2,1,0:T(8,128)(2,1)}, bf16[4,2,64,1536]{3,2,1,0:T(8,128)(2,1)S(1)}, u32[]{:S(2)}, u32[]{:S(2)}) collective-permute-start(bf16[4,2,64,1536]{3,2,1,0:T(8,128)(2,1)} %dynamic-slice_bitcast_fusion), channel_id=1, source_target_pairs={{0,2},{1,3},{2,0},{3,1},{4,6},{5,7},{6,4},{7,5},{8,10},{9,11},{10,... | collective-permute-start | bytes 4718600 | tf_op jit(solution)/shard_map/ppermute | solution.py:64
  283.0 28.3 %collective-permute-start.32 = (bf16[512,512]{1,0:T(8,128)(2,1)}, bf16[512,512]{1,0:T(8,128)(2,1)}, u32[]{:S(2)}, u32[]{:S(2)}) collective-permute-start(bf16[512,512]{1,0:T(8,128)(2,1)} %get-tuple-element.272), channel_id=1, source_target_pairs={{0,1},{1,0},{2,3},{3,2},{4,5},{5,4},{6,7},{7,6},{8,9},{9,8},{10,11... | collective-permute-start | bytes 1572872 | tf_op jit(solution)/shard_map/ppermute | solution.py:41
  308.6 10.1 %collective-permute-start.34 = (bf16[512,768]{1,0:T(8,128)(2,1)}, bf16[512,768]{1,0:T(8,128)(2,1)}, u32[]{:S(2)}, u32[]{:S(2)}) collective-permute-start(bf16[512,768]{1,0:T(8,128)(2,1)} %get-tuple-element.358), channel_id=1, source_target_pairs={{0,1},{1,0},{2,3},{3,2},{4,5},{5,4},{6,7},{7,6},{8,9},{9,8},{10,11... | collective-permute-start | bytes 2359304 | tf_op jit(solution)/shard_map/ppermute | solution.py:41
  308.9 34.0 %collective-permute-start.35 = (bf16[2,64,1536]{2,1,0:T(8,128)(2,1)}, bf16[2,64,1536]{2,1,0:T(8,128)(2,1)S(1)}, u32[]{:S(2)}, u32[]{:S(2)}) collective-permute-start(bf16[2,64,1536]{2,1,0:T(8,128)(2,1)} %get-tuple-element.279), channel_id=1, source_target_pairs={{0,8},{4,12},{8,16},{12,20},{16,24},{20,28},{24,0},{28,4},{1,9},{5... | collective-permute-start | bytes 1179656 | tf_op jit(solution)/shard_map/ppermute | solution.py:64
  310.4 37.1 %collective-permute-start.36 = (bf16[2,64,1536]{2,1,0:T(8,128)(2,1)}, bf16[2,64,1536]{2,1,0:T(8,128)(2,1)S(1)}, u32[]{:S(2)}, u32[]{:S(2)}) collective-permute-start(bf16[2,64,1536]{2,1,0:T(8,128)(2,1)} %get-tuple-element.280), channel_id=1, source_target_pairs={{0,16},{4,20},{8,24},{12,28},{16,0},{20,4},{24,8},{28,12},{1,17},{... | collective-permute-start | bytes 1179656 | tf_op jit(solution)/shard_map/ppermute | solution.py:64
  311.3 36.2 %collective-permute-start.38 = (bf16[4,64,1536]{2,1,0:T(8,128)(2,1)}, bf16[4,64,1536]{2,1,0:T(8,128)(2,1)S(1)}, u32[]{:S(2)}, u32[]{:S(2)}) collective-permute-start(bf16[4,64,1536]{2,1,0:T(8,128)(2,1)} %dynamic-slice_bitcast_fusion.4), channel_id=1, source_target_pairs={{0,4},{4,0},{8,12},{12,8},{16,20},{20,16},{24,28},{28,24},{1,5},{5... | collective-permute-start | bytes 2359304 | tf_op jit(solution)/shard_map/ppermute | solution.py:64
  316.1 31.5 %collective-permute-start.37 = (bf16[2,64,1536]{2,1,0:T(8,128)(2,1)S(1)}, bf16[2,64,1536]{2,1,0:T(8,128)(2,1)S(1)}, u32[]{:S(2)}, u32[]{:S(2)}) collective-permute-start(bf16[2,64,1536]{2,1,0:T(8,128)(2,1)S(1)} %copy-done.80), channel_id=1, source_target_pairs={{0,24},{4,28},{8,0},{12,4},{16,8},{20,12},{24,16},{28,20},{1,25},{... | collective-permute-start | bytes 1179656 | tf_op jit(solution)/shard_map/ppermute | solution.py:64
  353.1 22.0 %collective-permute-start.44 = (bf16[4,2,96,512]{3,2,1,0:T(8,128)(2,1)}, bf16[4,2,96,512]{3,2,1,0:T(8,128)(2,1)}, u32[]{:S(2)}, u32[]{:S(2)}) collective-permute-start(bf16[4,2,96,512]{3,2,1,0:T(8,128)(2,1)} %dynamic-slice_bitcast_fusion.3), channel_id=1, source_target_pairs={{0,4},{4,0},{8,12},{12,8},{16,20},{20,16},{24,28},{28,24},{1,5},{5... | collective-permute-start | bytes 2359304 | tf_op jit(solution)/shard_map/ppermute | solution.py:64
  353.8 30.5 %collective-permute-start.45 = (bf16[4,2,64,768]{3,2,1,0:T(8,128)(2,1)}, bf16[4,2,64,768]{3,2,1,0:T(8,128)(2,1)}, u32[]{:S(2)}, u32[]{:S(2)}) collective-permute-start(bf16[4,2,64,768]{3,2,1,0:T(8,128)(2,1)} %dynamic-slice_bitcast_fusion.2), channel_id=1, source_target_pairs={{0,2},{1,3},{2,0},{3,1},{4,6},{5,7},{6,4},{7,5},{8,10},{9,11},{10,... | collective-permute-start | bytes 2359304 | tf_op jit(solution)/shard_map/ppermute | solution.py:64
  367.8 23.0 %collective-permute-start.43 = (bf16[4,2,96,384]{3,2,1,0:T(8,128)(2,1)}, bf16[4,2,96,384]{3,2,1,0:T(8,128)(2,1)}, u32[]{:S(2)}, u32[]{:S(2)}) collective-permute-start(bf16[4,2,96,384]{3,2,1,0:T(8,128)(2,1)} %fusion.42), channel_id=1, source_target_pairs={{0,2},{1,3},{2,0},{3,1},{4,6},{5,7},{6,4},{7,5},{8,10},{9,11},{10,... | collective-permute-start | bytes 1769480 | tf_op jit(solution)/shard_map/ppermute | solution.py:64
  368.5 27.7 %collective-permute-start.46 = (bf16[64,1536]{1,0:T(8,128)(2,1)}, bf16[64,1536]{1,0:T(8,128)(2,1)}, u32[]{:S(2)}, u32[]{:S(2)}) collective-permute-start(bf16[64,1536]{1,0:T(8,128)(2,1)} %dynamic-slice_bitcast_fusion.17), channel_id=1, source_target_pairs={{0,2},{1,3},{2,0},{3,1},{4,6},{5,7},{6,4},{7,5},{8,10},{9,11},{10,... | collective-permute-start | bytes 589832 | tf_op jit(solution)/shard_map/ppermute | solution.py:64
  370.1 14.5 %collective-permute-start.42 = (bf16[4,2,64,384]{3,2,0,1:T(8,128)(2,1)}, bf16[4,2,64,384]{3,2,0,1:T(8,128)(2,1)}, u32[]{:S(2)}, u32[]{:S(2)}) collective-permute-start(bf16[4,2,64,384]{3,2,0,1:T(8,128)(2,1)} %bitcast.468), channel_id=1, source_target_pairs={{0,4},{4,0},{8,12},{12,8},{16,20},{20,16},{24,28},{28,24},{1,5},{5... | collective-permute-start | bytes 1179656 | tf_op jit(solution)/shard_map/ppermute | solution.py:64
  375.2 21.1 %collective-permute-start.47 = (bf16[64,1536]{1,0:T(8,128)(2,1)}, bf16[64,1536]{1,0:T(8,128)(2,1)S(1)}, u32[]{:S(2)}, u32[]{:S(2)}) collective-permute-start(bf16[64,1536]{1,0:T(8,128)(2,1)} %get-tuple-element.310), channel_id=1, source_target_pairs={{0,8},{4,12},{8,16},{12,20},{16,24},{20,28},{24,0},{28,4},{1,9},{5... | collective-permute-start | bytes 589832 | tf_op jit(solution)/shard_map/ppermute | solution.py:64
  384.3 12.6 %collective-permute-start.48 = (bf16[64,1536]{1,0:T(8,128)(2,1)}, bf16[64,1536]{1,0:T(8,128)(2,1)S(1)}, u32[]{:S(2)}, u32[]{:S(2)}) collective-permute-start(bf16[64,1536]{1,0:T(8,128)(2,1)} %get-tuple-element.311), channel_id=1, source_target_pairs={{0,16},{4,20},{8,24},{12,28},{16,0},{20,4},{24,8},{28,12},{1,17},{... | collective-permute-start | bytes 589832 | tf_op jit(solution)/shard_map/ppermute | solution.py:64
  384.6 14.1 %collective-permute-start.49 = (bf16[64,1536]{1,0:T(8,128)(2,1)S(1)}, bf16[64,1536]{1,0:T(8,128)(2,1)S(1)}, u32[]{:S(2)}, u32[]{:S(2)}) collective-permute-start(bf16[64,1536]{1,0:T(8,128)(2,1)S(1)} %get-tuple-element.312), channel_id=1, source_target_pairs={{0,24},{4,28},{8,0},{12,4},{16,8},{20,12},{24,16},{28,20},{1,25},{... | collective-permute-start | bytes 589832 | tf_op jit(solution)/shard_map/ppermute | solution.py:64
  401.9 9.9 %collective-permute-start.51 = (bf16[4,96,384]{2,1,0:T(8,128)(2,1)S(1)}, bf16[4,96,384]{2,1,0:T(8,128)(2,1)S(1)}, u32[]{:S(2)}, u32[]{:S(2)}) collective-permute-start(bf16[4,96,384]{2,1,0:T(8,128)(2,1)S(1)} %dynamic-slice_bitcast_fusion.10), channel_id=1, source_target_pairs={{0,4},{4,0},{8,12},{12,8},{16,20},{20,16},{24,28},{28,24},{1,5},{5... | collective-permute-start | bytes 884744 | tf_op jit(solution)/shard_map/ppermute | solution.py:64
  402.1 18.3 %collective-permute-start.52 = (bf16[4,96,512]{2,1,0:T(8,128)(2,1)S(1)}, bf16[4,96,512]{2,1,0:T(8,128)(2,1)S(1)}, u32[]{:S(2)}, u32[]{:S(2)}) collective-permute-start(bf16[4,96,512]{2,1,0:T(8,128)(2,1)S(1)} %dynamic-slice_bitcast_fusion.6), channel_id=1, source_target_pairs={{0,2},{1,3},{2,0},{3,1},{4,6},{5,7},{6,4},{7,5},{8,10},{9,11},{10,... | collective-permute-start | bytes 1179656 | tf_op jit(solution)/shard_map/ppermute | solution.py:64
  402.3 19.6 %collective-permute-start.53 = (bf16[4,64,768]{2,1,0:T(8,128)(2,1)S(1)}, bf16[4,64,768]{2,1,0:T(8,128)(2,1)S(1)}, u32[]{:S(2)}, u32[]{:S(2)}) collective-permute-start(bf16[4,64,768]{2,1,0:T(8,128)(2,1)S(1)} %dynamic-slice_bitcast_fusion.5), channel_id=1, source_target_pairs={{0,4},{4,0},{8,12},{12,8},{16,20},{20,16},{24,28},{28,24},{1,5},{5... | collective-permute-start | bytes 1179656 | tf_op jit(solution)/shard_map/ppermute | solution.py:64
  414.3 11.4 %collective-permute-start.68 = (f32[64,1536]{1,0:T(8,128)S(1)}, f32[64,1536]{1,0:T(8,128)}, u32[]{:S(2)}, u32[]{:S(2)}) collective-permute-start(f32[64,1536]{1,0:T(8,128)S(1)} %pad_maximum_fusion.24), channel_id=1, source_target_pairs={{0,1},{1,0},{2,3},{3,2},{4,5},{5,4},{6,7},{7,6},{8,9},{9,8},{10,11... | collective-permute-start | bytes 1179656 | tf_op jit(solution)/shard_map/ppermute | solution.py:41
  415.2 17.3 %collective-permute-start.66 = (bf16[160,384]{1,0:T(8,128)(2,1)}, bf16[160,384]{1,0:T(8,128)(2,1)}, u32[]{:S(2)}, u32[]{:S(2)}) collective-permute-start(bf16[160,384]{1,0:T(8,128)(2,1)} %get-tuple-element.335), channel_id=1, source_target_pairs={{0,24},{4,28},{8,0},{12,4},{16,8},{20,12},{24,16},{28,20},{1,25},{... | collective-permute-start | bytes 368648 | tf_op jit(solution)/shard_map/ppermute | solution.py:64
  419.3 15.3 %collective-permute-start.65 = (bf16[160,384]{1,0:T(8,128)(2,1)}, bf16[160,384]{1,0:T(8,128)(2,1)}, u32[]{:S(2)}, u32[]{:S(2)}) collective-permute-start(bf16[160,384]{1,0:T(8,128)(2,1)} %get-tuple-element.334), channel_id=1, source_target_pairs={{0,16},{4,20},{8,24},{12,28},{16,0},{20,4},{24,8},{28,12},{1,17},{... | collective-permute-start | bytes 368648 | tf_op jit(solution)/shard_map/ppermute | solution.py:64
  420.4 14.2 %collective-permute-start.64 = (bf16[160,384]{1,0:T(8,128)(2,1)}, bf16[160,384]{1,0:T(8,128)(2,1)}, u32[]{:S(2)}, u32[]{:S(2)}) collective-permute-start(bf16[160,384]{1,0:T(8,128)(2,1)} %get-tuple-element.333), channel_id=1, source_target_pairs={{0,8},{4,12},{8,16},{12,20},{16,24},{20,28},{24,0},{28,4},{1,9},{5... | collective-permute-start | bytes 368648 | tf_op jit(solution)/shard_map/ppermute | solution.py:64
  421.9 10.0 %collective-permute-start.56 = (f32[9728]{0:T(1024)S(1)}, f32[9728]{0:T(1024)S(1)}, u32[]{:S(2)}, u32[]{:S(2)}) collective-permute-start(f32[9728]{0:T(1024)S(1)} %add.465), channel_id=1, source_target_pairs={{0,2},{1,3},{2,0},{3,1},{4,6},{5,7},{6,4},{7,5},{8,10},{9,11},{10,... | collective-permute-start | bytes 116744 | tf_op jit(solution)/shard_map/ppermute | solution.py:64
  425.7 24.9 %collective-permute-start.62 = (bf16[128,768]{1,0:T(8,128)(2,1)}, bf16[128,768]{1,0:T(8,128)(2,1)S(1)}, u32[]{:S(2)}, u32[]{:S(2)}) collective-permute-start(bf16[128,768]{1,0:T(8,128)(2,1)} %get-tuple-element.332), channel_id=1, source_target_pairs={{0,24},{4,28},{8,0},{12,4},{16,8},{20,12},{24,16},{28,20},{1,25},{... | collective-permute-start | bytes 589832 | tf_op jit(solution)/shard_map/ppermute | solution.py:64
  431.9 18.7 %collective-permute-start.61 = (bf16[128,768]{1,0:T(8,128)(2,1)S(1)}, bf16[128,768]{1,0:T(8,128)(2,1)S(1)}, u32[]{:S(2)}, u32[]{:S(2)}) collective-permute-start(bf16[128,768]{1,0:T(8,128)(2,1)S(1)} %get-tuple-element.331), channel_id=1, source_target_pairs={{0,16},{4,20},{8,24},{12,28},{16,0},{20,4},{24,8},{28,12},{1,17},{... | collective-permute-start | bytes 589832 | tf_op jit(solution)/shard_map/ppermute | solution.py:64
  432.5 11.7 %collective-permute-start.59 = (f32[9728]{0:T(1024)S(1)}, f32[9728]{0:T(1024)S(1)}, u32[]{:S(2)}, u32[]{:S(2)}) collective-permute-start(f32[9728]{0:T(1024)S(1)} %add.466), channel_id=1, source_target_pairs={{0,24},{4,28},{8,0},{12,4},{16,8},{20,12},{24,16},{28,20},{1,25},{... | collective-permute-start | bytes 116744 | tf_op jit(solution)/shard_map/ppermute | solution.py:64
  434.6 13.0 %collective-permute-start.57 = (f32[9728]{0:T(1024)S(1)}, f32[9728]{0:T(1024)S(1)}, u32[]{:S(2)}, u32[]{:S(2)}) collective-permute-start(f32[9728]{0:T(1024)S(1)} %add.466), channel_id=1, source_target_pairs={{0,8},{4,12},{8,16},{12,20},{16,24},{20,28},{24,0},{28,4},{1,9},{5... | collective-permute-start | bytes 116744 | tf_op jit(solution)/shard_map/ppermute | solution.py:64
  434.6 13.0 %collective-permute-start.58 = (f32[9728]{0:T(1024)S(1)}, f32[9728]{0:T(1024)S(1)}, u32[]{:S(2)}, u32[]{:S(2)}) collective-permute-start(f32[9728]{0:T(1024)S(1)} %add.466), channel_id=1, source_target_pairs={{0,16},{4,20},{8,24},{12,28},{16,0},{20,4},{24,8},{28,12},{1,17},{... | collective-permute-start | bytes 116744 | tf_op jit(solution)/shard_map/ppermute | solution.py:64
  (118 other events, 860.3 us)
Sparse Core Ops, SparseCore 0:
  10.9 118.3 all-gather.4
  132.2 68.9 all-gather.6
  226.1 141.4 reduce-scatter.1
